TPU v7x, 256 devices: a whole 4x4x8 slice. The times are simulated.
256 devices in a mesh: rep: 4 (over y), seq: 32 (over x, z), cfg: 2 (over core).
Axes of the slice: x: 4, y: 4, z: 8, core: 2. Of those that a mesh axis runs over, the one named last changes fastest.
Arguments:
- tokens: bfloat16 [128, 512, 1152], P(('rep', 'seq')), parts along dimension 0, may hold values from -36 to 36
- modulation: float32 [2, 6, 1152], P('cfg'), may hold values from -3 to 3
- w_qkv_s: bfloat16 [1152, 3456], P(None, ('seq', 'cfg')), may hold values from -0.1875 to 0.1875
- w_out_s: bfloat16 [1152, 1152], P(None, ('seq', 'cfg')), may hold values from -0.1875 to 0.1875
- w_qkv_t: bfloat16 [1152, 3456], P(None, ('seq', 'cfg')), may hold values from -0.1875 to 0.1875
- w_out_t: bfloat16 [1152, 1152], P(None, ('seq', 'cfg')), may hold values from -0.1875 to 0.1875
- w_final: bfloat16 [1152, 16], replicated, may hold values from -0.1875 to 0.1875
- norm_gains: float32 [4, 72], replicated, may hold values from 0.25 to 1.75
- clip_tokens: int32 [32], P('rep'), parts along dimension 0, may hold values from 64 to 512, as said below
- block_clip: int32 [128], P('rep'), parts along dimension 0, may hold values from 0 to 7, never falling along the last dimension, each value on 1 to 8 neighbouring positions
Outputs:
- guided: float32 [128, 512, 16], P('rep', 'seq', 'cfg'), parts along dimension 0
There are 4 independent parts, one for each index of `rep`. A program takes and returns all parts, laid end to end along the dimension named above; an argument that names none is the same for every part. Nothing has to cross between parts.
Inputs may be any that keep to these rules, and one draw needn't show every extreme that they name: `clip_tokens`: one clip has exactly 512 spatial tokens. `block_clip`: never falling along the blocks; every clip has 1 to 8 blocks, one exactly 8.
All inputs are finite; a program needn't handle non-finite values.
Results may differ from a plain program's by a relative error of at most 0.019.
Values may be sent and summed in bfloat16 or wider, within the bound.
No kernel may reach another device: no remote copies, remote signals or barrier semaphores. Data moves between devices by JAX's collectives and lax.ppermute only.
A program may use at most 128 MiB of HBM per device.

v0:
```python
import math

import jax
import jax.numpy as jnp
from jax import lax
from jax.sharding import PartitionSpec as P


def partner(array, axis, apart):
    return lax.ppermute(array, axis, [(i, i ^ 1 << apart) for i in range(lax.axis_size(axis))])


def layer_norm(values_in):
    average = jnp.mean(values_in, axis=-1, keepdims=True)
    centred = values_in - average
    variance = jnp.mean(centred * centred, axis=-1, keepdims=True)
    return centred * lax.rsqrt(variance + 1e-06)


def modulate(values_in, scale_row, offset_row):
    return (layer_norm(values_in.astype(jnp.float32)) * (1.0 + scale_row) + offset_row).astype(
        jnp.bfloat16
    )


def head_scale(values_in, gains_row):
    return (
        values_in
        * lax.rsqrt(jnp.mean(values_in * values_in, axis=-1, keepdims=True) + 1e-06)
        * gains_row
    ).astype(jnp.bfloat16)


def apply_weight(row_block, weight):
    return jnp.dot(
        row_block,
        lax.all_gather(weight, ("seq", "cfg"), axis=1, tiled=True),
        preferred_element_type=jnp.float32,
    )


def spatial_attend(projected, length, norm_gains):
    row_count = projected.shape[0]
    features = projected.shape[1] // 3
    head_size = norm_gains.shape[1]
    head_count = features // head_size
    queries = head_scale(
        projected[:, :features].reshape(row_count, head_count, head_size), norm_gains[0]
    )
    key_rows = head_scale(
        projected[:, features : 2 * features].reshape(row_count, head_count, head_size),
        norm_gains[1],
    )
    values = (
        projected[:, 2 * features :].reshape(row_count, head_count, head_size).astype(jnp.bfloat16)
    )
    scores = jnp.einsum(
        "qhd,khd->hqk", queries, key_rows, preferred_element_type=jnp.float32
    ) / math.sqrt(head_size)
    allowed = (jnp.arange(row_count, dtype=jnp.int32) < length)[None, None, :]
    unnormed = jnp.where(allowed, jnp.exp(scores), 0.0)
    shares = (unnormed / jnp.sum(unnormed, axis=-1, keepdims=True)).astype(jnp.bfloat16)
    attended = jnp.einsum("hqk,khd->qhd", shares, values, preferred_element_type=jnp.float32)
    return attended.astype(jnp.bfloat16).reshape(row_count, features)


def temporal_attend(projected, same_clip, norm_gains):
    frames, locations, triple = projected.shape
    features = triple // 3
    head_size = norm_gains.shape[1]
    head_count = features // head_size
    queries = head_scale(
        projected[..., :features].reshape(frames, locations, head_count, head_size), norm_gains[2]
    )
    key_rows = head_scale(
        projected[..., features : 2 * features].reshape(frames, locations, head_count, head_size),
        norm_gains[3],
    )
    values = (
        projected[..., 2 * features :]
        .reshape(frames, locations, head_count, head_size)
        .astype(jnp.bfloat16)
    )
    scores = jnp.einsum(
        "blhd,clhd->lhbc", queries, key_rows, preferred_element_type=jnp.float32
    ) / math.sqrt(head_size)
    unnormed = jnp.where(same_clip[None, None], jnp.exp(scores), 0.0)
    shares = (unnormed / jnp.sum(unnormed, axis=-1, keepdims=True)).astype(jnp.bfloat16)
    attended = jnp.einsum("lhbc,clhd->blhd", shares, values, preferred_element_type=jnp.float32)
    return attended.astype(jnp.bfloat16).reshape(frames, locations, features)


def body(
    tokens,
    modulation,
    w_qkv_s,
    w_out_s,
    w_qkv_t,
    w_out_t,
    w_final,
    norm_gains,
    clip_tokens,
    block_clip,
):
    features = tokens.shape[2]
    block_tokens = tokens.shape[1]
    frames = block_clip.shape[0]
    locations = block_tokens // lax.axis_size("seq")
    position = lax.axis_index("seq")
    levels = modulation[0]
    member = block_clip[:, None] == jnp.arange(clip_tokens.shape[0], dtype=jnp.int32)[None, :]
    lengths = jnp.sum(jnp.where(member, clip_tokens[None, :], 0), axis=1)
    own_length = lax.dynamic_slice_in_dim(lengths, position, 1)[0]
    normed = modulate(tokens[0], levels[1], levels[0])
    projected = apply_weight(normed, w_qkv_s)
    attended = spatial_attend(projected, own_length, norm_gains)
    residual = (tokens[0].astype(jnp.float32) + levels[2] * apply_weight(attended, w_out_s)).astype(
        jnp.bfloat16
    )
    regrouped = lax.all_to_all(residual[None], "seq", split_axis=1, concat_axis=0, tiled=True)
    temporal_in = modulate(regrouped, levels[4], levels[3])
    temporal_proj = apply_weight(temporal_in.reshape(-1, features), w_qkv_t).reshape(
        frames, locations, 3 * features
    )
    same_clip = block_clip[:, None] == block_clip[None, :]
    temporal_out = temporal_attend(temporal_proj, same_clip, norm_gains)
    projection = apply_weight(temporal_out.reshape(-1, features), w_out_t).reshape(
        frames, locations, features
    )
    updated = regrouped.astype(jnp.float32) + levels[5] * projection
    final_in = layer_norm(updated).astype(jnp.bfloat16)
    predicted = jnp.dot(final_in.reshape(-1, features), w_final, preferred_element_type=jnp.float32)
    predicted = predicted.reshape(frames, locations, -1)
    half_width = predicted.shape[2] // 2
    branch_index = lax.axis_index("cfg")
    outgoing = lax.dynamic_slice_in_dim(predicted, (1 - branch_index) * half_width, half_width, 2)
    received = partner(outgoing, "cfg", 0)
    own_part = lax.dynamic_slice_in_dim(predicted, branch_index * half_width, half_width, 2)
    conditional = jnp.where(branch_index == 0, own_part, received)
    unconditional = jnp.where(branch_index == 0, received, own_part)
    location_ids = position * locations + jnp.arange(locations, dtype=jnp.int32)
    inside = location_ids[None, :] < lengths[:, None]
    guided = unconditional + 7.0 * (conditional - unconditional)
    return jnp.where(inside[:, :, None], guided, 0.0)


def solution(mesh):
    in_specs = (
        P(("rep", "seq"), None, None),
        P("cfg", None, None),
        P(None, ("seq", "cfg")),
        P(None, ("seq", "cfg")),
        P(None, ("seq", "cfg")),
        P(None, ("seq", "cfg")),
        P(),
        P(),
        P("rep"),
        P("rep"),
    )
    out_specs = P("rep", "seq", "cfg")
    return jax.shard_map(body, mesh=mesh, in_specs=in_specs, out_specs=out_specs, check_vma=False)
```

profile of v0, /device:TPU:1, one launch (start us, length us, event | category | flops | bytes accessed | tf_op | source)
XLA Modules:
  0.0 428.1 jit_solution(15602338338302315237)
XLA Ops:
  6.5 0.7 all-gather.11.cloned.1.call-update
  7.3 0.7 all-gather.9.cloned.1.call-update
  8.1 0.7 all-gather.15.cloned.1.call-update
  8.8 0.5 all-gather.13.cloned.1.call-update
  9.3 0.8 select_reduce_fusion
  10.1 0.6 dynamic_slice.9
  10.7 0.6 iota_compare_fusion.1
  11.3 0.8 slice_reduce_fusion.1
  12.2 1.5 convert_reduce_fusion
  13.7 0.4 fusion.10
  14.2 78.7 %all-gather.11.cloned.1.call-done = bf16[64,18,1152]{2,1,0:T(8,128)(2,1)} async-done(((bf16[1,18,1152]{2,1,0:T(8,128)(2,1)}), bf16[64,18,1152]{2,1,0:T(8,128)(2,1)}) %all-gather.11.cloned.1.call-update) | async-done | bytes 2654224 | tf_op jit(solution)/shard_map/all_gather | solution.py:37
  92.9 5.4 %reshape.237 = bf16[1152,1152]{1,0:T(8,128)(2,1)} reshape(bf16[64,18,1152]{2,1,0:T(8,128)(2,1)} %all-gather.11.cloned.1.call-done) | data formatting | bytes 5308416
  98.3 77.5 %all-gather.9.cloned.1.call-done = bf16[64,54,1152]{2,1,0:T(8,128)(2,1)} async-done(((bf16[1,54,1152]{2,1,0:T(8,128)(2,1)}), bf16[64,54,1152]{2,1,0:T(8,128)(2,1)}) %all-gather.9.cloned.1.call-update) | async-done | bytes 7962640 | tf_op jit(solution)/shard_map/all_gather | solution.py:37
  175.8 9.5 %reshape.235 = bf16[3456,1152]{1,0:T(8,128)(2,1)} reshape(bf16[64,54,1152]{2,1,0:T(8,128)(2,1)} %all-gather.9.cloned.1.call-done) | data formatting | bytes 15925248
  185.2 7.8 %fusion.28 = f32[512,3456]{1,0:T(8,128)S(1)} fusion(bf16[3456,1152]{1,0:T(8,128)(2,1)} %reshape.235, bf16[1,512,1152]{2,1,0:T(8,128)(2,1)S(1)} %copy-done.4, f32[1152]{0:T(1024)S(1)} %get-tuple-element.6, f32[1152]{0:T(1024)S(1)} %get-tuple-element.7, f32[512]{0:T(512)S(1)} %add_rsqrt_fusion.6, f32[512]{0:T(512)S(1)} %broadcast_multiply_fusion.2), kind=kOutput, calls=%fused_computation.49 | convolution fusion | flops 4080402432 | bytes 16233472 | tf_op jit(solution)/shard_map/dot_general | solution.py:35
  193.0 2.9 copy-done.2
  196.0 0.1 slice.91
  196.1 1.5 copy.41
  197.5 4.8 %fusion.50 = (f32[512,1152]{1,0:T(8,128)}, f32[512,1152]{1,0:T(8,128)}) fusion(f32[512,3456]{1,0:T(8,128)} %copy-done.2), kind=kLoop, calls=%fused_computation.99 | loop fusion | bytes 9437184 | tf_op jit(solution)/shard_map/slice | solution.py:51
  202.4 2.0 copy.43
  204.4 3.3 copy.42
  207.7 0.3 multiply_reduce_fusion.4
  208.1 1.3 copy-done.1
  209.4 0.3 multiply_reduce_fusion.5
  209.8 4.6 %fusion = (f32[16,512]{1,0:T(8,128)S(1)}, f32[16,512,512]{1,2,0:T(8,128)S(1)}) fusion(pred[512]{0:T(512)(128)(4,1)S(1)} %iota_compare_fusion.1, f32[512,16,72]{0,2,1:T(8,128)S(1)} %bitcast.73, f32[72]{0:T(128)S(1)} %get-tuple-element.16, f32[512,16]{0,1:T(8,128)S(1)} %add_rsqrt_fusion.2, f32[512,16,72]{0,2,1:T(8,128)S(1)} %bitcast.75, ...), kind=kOutput, calls=%fused_computation.2 | convolution fusion | flops 620093440 | bytes 21595200 | tf_op jit(solution)/shard_map/qhd,khd->hqk/dot_general | solution.py:57
  214.4 3.7 fusion.24
  218.2 1.9 fusion.9
  220.1 2.2 copy.68
  222.3 0.5 broadcast.232
  222.8 9.2 %reduce.15 = bf16[512,1152]{1,0:T(8,128)(2,1)} reduce(bf16[512,1,1152]{2,1,0:T(2,128)(2,1)S(1)} %bitcast.76, bf16[]{:T(256)} %broadcast.232), dimensions={1}, to_apply=%bitcast.70.reduce_sub_computation | reduce | bytes 2359298
  232.0 3.8 reshape.253
  235.8 5.7 %all-to-all-start = ((bf16[32,2,9216]{2,1,0:T(2,128)(2,1)}), bf16[32,2,9216]{2,1,0:T(2,128)(2,1)}, u32[]{:S(2)}, u32[]{:S(2)}) async-start(bf16[32,2,9216]{2,1,0:T(2,128)(2,1)} %reshape.253), calls=%async_computation | async-start | bytes 2359296 | tf_op jit(solution)/shard_map/all_to_all | solution.py:120
  241.5 0.1 broadcast_compare_fusion
  241.6 15.5 %all-gather.15.cloned.1.call-done = bf16[64,18,1152]{2,1,0:T(8,128)(2,1)} async-done(((bf16[1,18,1152]{2,1,0:T(8,128)(2,1)}), bf16[64,18,1152]{2,1,0:T(8,128)(2,1)}) %all-gather.15.cloned.1.call-update) | async-done | bytes 2654224 | tf_op jit(solution)/shard_map/all_gather | solution.py:37
  257.1 5.4 %reshape.243 = bf16[1152,1152,1]{1,0,2:T(8,128)(2,1)} reshape(bf16[64,18,1152]{2,1,0:T(8,128)(2,1)} %all-gather.15.cloned.1.call-done) | data formatting | bytes 5308416
  262.5 78.7 %all-gather.13.cloned.1.call-done = bf16[64,54,1152]{2,1,0:T(8,128)(2,1)} async-done(((bf16[1,54,1152]{2,1,0:T(8,128)(2,1)}), bf16[64,54,1152]{2,1,0:T(8,128)(2,1)}) %all-gather.13.cloned.1.call-update) | async-done | bytes 7962640 | tf_op jit(solution)/shard_map/all_gather | solution.py:37
  341.2 9.5 %reshape.242 = bf16[3456,1152,1]{1,0,2:T(8,128)(2,1)} reshape(bf16[64,54,1152]{2,1,0:T(8,128)(2,1)} %all-gather.13.cloned.1.call-done) | data formatting | bytes 15925248
  350.7 4.3 reshape.254
  355.0 2.4 convert_reduce_fusion.1
  357.4 3.9 multiply_reduce_fusion.3
  361.3 0.1 div.69
  361.4 1.6 copy.54
  363.0 0.1 rsqrt.63
  363.1 8.5 %fusion.26 = f32[32,16,3456]{2,1,0:T(8,128)S(1)} fusion(bf16[3456,1152,1]{1,0,2:T(8,128)(2,1)} %reshape.242, f32[32,16,1152]{2,1,0:T(8,128)} %bitcast.77, f32[1152]{0:T(1024)S(1)} %get-tuple-element.9, f32[1152]{0:T(1024)S(1)} %get-tuple-element.10, f32[32,16]{1,0:T(8,128)S(1)} %rsqrt.63, f32[32,16]{1,0:T(8,128)S(1)} %div.69), kind=kOutput, calls=%fused_computation.47 | convolution fusion | flops 4079812608 | bytes 17413120 | tf_op jit(solution)/shard_map/dot_general | solution.py:35
  371.6 1.7 fusion.49
  373.3 1.2 slice.90
  374.5 6.1 %reshape.232 = f32[32,16,16,72]{3,2,1,0:T(8,128)} reshape(f32[32,16,1152]{2,1,0:T(8,128)} %get-tuple-element.12) | data formatting | bytes 4718592 | tf_op jit(solution)/shard_map/reshape | solution.py:76
  380.7 3.4 multiply_reduce_fusion
  384.1 0.7 add_rsqrt_fusion
  384.8 4.8 %reshape.231 = f32[32,16,16,72]{3,2,1,0:T(8,128)} reshape(f32[32,16,1152]{2,1,0:T(8,128)S(1)} %get-tuple-element.11) | data formatting | bytes 4718592 | tf_op jit(solution)/shard_map/reshape | solution.py:73
  389.6 3.4 multiply_reduce_fusion.1
  393.1 0.7 add_rsqrt_fusion.1
  393.8 3.7 convert_element_type.86
  397.5 5.4 %multiply_convert_fusion = (bf16[32,16,16,72]{3,2,1,0:T(8,128)(2,1)S(1)}, bf16[32,16,16,72]{3,2,1,0:T(8,128)(2,1)S(1)}) fusion(f32[32,16,16,72]{3,2,1,0:T(8,128)} %reshape.232, f32[72]{0:T(128)S(1)} %get-tuple-element.18, f32[32,16,16]{2,1,0:T(8,128)} %add_rsqrt_fusion, f32[72]{0:T(128)S(1)} %get-tuple-element.15, f32[32,16,16,72]{3,2,1,0:T(8,128)} %reshape.231, ...), kind=kLoop, calls=%fused_computation.6 | loop fusion | flops 3538944 | bytes 7144000 | tf_op jit(solution)/shard_map/convert_element_type | solution.py:31
  402.9 3.7 fusion.2
  406.6 2.3 convert_bitcast_fusion.1
  409.0 0.8 copy.50
  409.8 2.7 dot_general.36
  412.5 4.5 %fusion.51 = (f32[32,16]{1,0:T(8,128)S(1)}, f32[32,16,1152]{2,1,0:T(8,128)S(1)}) fusion(f32[32,16,1152]{2,1,0:T(8,128)} %bitcast.78, bf16[32,16,1152]{2,1,0:T(8,128)(2,1)S(1)} %dot_general.36, bf16[1152,1152,1]{1,0,2:T(8,128)(2,1)} %reshape.243, f32[1152]{0:T(1024)S(1)} %get-tuple-element.5), kind=kOutput, calls=%fused_computation.100 | convolution fusion | flops 1360723456 | bytes 8559104 | tf_op jit(solution)/shard_map/dot_general | solution.py:35
  417.0 0.4 multiply_reduce_fusion.2
  417.4 1.7 fusion.27
  419.2 0.3 collective-permute-start
  419.6 1.0 collective-permute-done
  420.6 0.7 copy.51
  (36 shorter events, 0.4 us)
Async XLA Ops:
  6.5 410.9 %copy-start = (bf16[1152,16]{0,1:T(8,128)(2,1)S(1)}, bf16[1152,16]{0,1:T(8,128)(2,1)}, u32[]{:S(2)}) copy-start(bf16[1152,16]{0,1:T(8,128)(2,1)} %param.16) | copy-start | bytes 110596
  6.5 7.2 %copy-start.4 = (bf16[1,512,1152]{2,1,0:T(8,128)(2,1)S(1)}, bf16[1,512,1152]{2,1,0:T(8,128)(2,1)}, u32[]{:S(2)}) copy-start(bf16[1,512,1152]{2,1,0:T(8,128)(2,1)} %param.10) | copy-start | bytes 3538948
  6.5 7.6 %copy-start.9 = (f32[4,72]{1,0:T(4,128)S(1)}, f32[4,72]{1,0:T(4,128)}, u32[]{:S(2)}) copy-start(f32[4,72]{1,0:T(4,128)} %param.17) | copy-start | bytes 3460
  6.5 86.4 %all-gather.11.cloned.1.call-start = ((), (), s32[]{:S(2)}) async-start(), calls=%async_computation.2 | async-start | bytes 3594240 | tf_op jit(solution)/shard_map/all_gather | solution.py:37
  7.3 168.5 %all-gather.9.cloned.1.call-start = ((), (), s32[]{:S(2)}) async-start(), calls=%async_computation.1 | async-start | bytes 8386560 | tf_op jit(solution)/shard_map/all_gather | solution.py:37
  8.0 249.1 %all-gather.15.cloned.1.call-start = ((), (), s32[]{:S(2)}) async-start(), calls=%async_computation.4 | async-start | bytes 3594240 | tf_op jit(solution)/shard_map/all_gather | solution.py:37
  8.7 332.5 %all-gather.13.cloned.1.call-start = ((), (), s32[]{:S(2)}) async-start(), calls=%async_computation.3 | async-start | bytes 8386560 | tf_op jit(solution)/shard_map/all_gather | solution.py:37
  193.0 2.9 copy-start.2
  207.7 1.7 copy-start.1
  209.8 4.6 %copy-start.7 = (bf16[512,1152]{0,1:T(8,128)(2,1)S(1)}, bf16[512,1152]{0,1:T(8,128)(2,1)}, u32[]{:S(2)}) copy-start(bf16[512,1152]{0,1:T(8,128)(2,1)} %copy.41) | copy-start | bytes 3538948
  214.4 3.8 copy-start.5
  214.4 3.8 copy-start.6
  232.0 9.5 %copy-start.8 = (s32[32]{0:T(128)S(1)}, s32[32]{0:T(128)}, u32[]{:S(2)}) copy-start(s32[32]{0:T(128)} %param.19) | copy-start | bytes 388
  235.8 114.9 %all-to-all-start = ((bf16[32,2,9216]{2,1,0:T(2,128)(2,1)}), bf16[32,2,9216]{2,1,0:T(2,128)(2,1)}, u32[]{:S(2)}, u32[]{:S(2)}) async-start(bf16[32,2,9216]{2,1,0:T(2,128)(2,1)} %reshape.253), calls=%async_computation | async-start | bytes 2359296 | tf_op jit(solution)/shard_map/all_to_all | solution.py:120
  389.6 4.2 copy-start.3
  419.2 1.4 collective-permute-start
Sparse Core Ops, SparseCore 0:
  10.1 82.7 all-gather.10
  95.6 80.1 all-gather.8
  178.5 78.5 all-gather.14
  259.6 81.5 all-gather.12
where the time goes:
time: 434 us; the launch traced here: 428 us
  waiting for transfers between devices  254 us (59%)
  local copies, waits for them, and re-layouts  80.7 us (19%)
  matrix products  38.8 us (9%)
  other arithmetic  34.7 us (8%)
  between operations  13.7 us (3%)
  starting transfers between devices  6.17 us (1%)
    all_gather x4, waiting for transfers between devices, apply_weight(): lax.all_gather(weight, ('seq', 'cfg'), axis=1, tiled=True)  250 us
    unnamed x28, local copies, waits for them, and re-layouts  44.1 us
    dot_general x4, matrix products, apply_weight(): jnp.dot(row_block, lax.all_gather(weight, ('seq', 'cfg'), axis=1, tiled=T...  22.7 us
    unnamed x1, other arithmetic  9.16 us
  transfers between devices with their start and end apart: 6, of which 5 were waited for; matrix products, arithmetic and copies ran while one was open for 19% of the time, Pallas kernels for 0%

commit v1 on v0

v1 whole, which is shorter than its diff:
```python
import functools
import math

import jax
import jax.numpy as jnp
from jax import lax
from jax.experimental import pallas as pl
from jax.experimental.pallas import tpu as pltpu
from jax.sharding import PartitionSpec as P

BF16 = jnp.bfloat16
F32 = jnp.float32
LANES = 128
TEMPORAL_ROWS = 128


def dot_nt(left, right):
    return lax.dot_general(left, right, (((1,), (1,)), ((), ())), preferred_element_type=F32)


def layer_norm(values_in):
    average = jnp.mean(values_in, axis=-1, keepdims=True)
    centred = values_in - average
    variance = jnp.mean(centred * centred, axis=-1, keepdims=True)
    return centred * lax.rsqrt(variance + 1e-06)


def modulate_rows(source, target, scale_row, offset_row, step):
    def chunk(i, carry):
        rows = pl.ds(pl.multiple_of(i * step, step), step)
        target[rows, :] = (layer_norm(source[rows, :].astype(F32)) * (1.0 + scale_row) + offset_row).astype(BF16)
        return carry

    lax.fori_loop(0, source.shape[0] // step, chunk, 0)


def lay_out_weights(landing, heads, out_rows, head_size):
    share = 3 * head_size // 4
    quarter = head_size // 4
    width = landing.shape[2]
    head_count = heads.shape[1]
    blank = jnp.zeros((LANES - head_size, width), BF16)

    def group(g, carry):
        for half in range(2):
            part = [landing[8 * g + 4 * half + i] for i in range(4)]
            pieces = (
                (part[0][:share], part[1][: head_size - share]),
                (part[1][head_size - share : share], part[2][: 2 * quarter]),
                (part[2][2 * quarter : share], part[3][:share]),
            )
            for i in range(3):
                block = 6 * g + 3 * half + i
                heads[block // head_count, block % head_count] = jnp.concatenate(pieces[i] + (blank,), axis=0)
        rows = [landing[8 * g + i][share:] for i in range(8)]
        size = 8 * quarter
        out_rows[pl.ds(pl.multiple_of(g * size, 16), size), :] = jnp.concatenate(rows, axis=0)
        return carry

    lax.fori_loop(0, landing.shape[0] // 8, group, 0)


def unit_heads(projected, gain_row, head_size, factor):
    total = jnp.sum(projected * projected, axis=-1, keepdims=True)
    return (projected * lax.rsqrt(total / head_size + 1e-06) * (gain_row * factor)).astype(BF16)


def project_pair(normed, heads, pair):
    found = []
    for kind in range(3):
        weight = heads[kind, pl.ds(2 * pair, 2)].reshape(2 * LANES, normed.shape[1])
        found.append(dot_nt(normed[...], weight))
    return found


def gather_heads(attended, packed, head_size, step):
    def chunk(i, carry):
        rows = pl.ds(pl.multiple_of(i * step, step), step)
        packed[rows, :] = jnp.concatenate(
            [attended[h, rows, :][:, :head_size] for h in range(attended.shape[0])], axis=1
        )
        return carry

    lax.fori_loop(0, packed.shape[0] // step, chunk, 0)


def spatial_kernel(head_size, length_ref, tokens, levels, gains, gathered, residual,
                   landing, heads, out_rows, normed, attended, packed, sem):
    arriving = pltpu.make_async_copy(gathered.at[:, 0], landing, sem)
    arriving.start()
    modulate_rows(tokens, normed, levels[1:2, :], levels[0:1, :], 64)
    arriving.wait()
    lay_out_weights(landing, heads, out_rows, head_size)
    row_count = tokens.shape[0]
    inside = lax.broadcasted_iota(jnp.int32, (row_count, LANES), 0) < length_ref[0]
    column = lax.broadcasted_iota(jnp.int32, (row_count, LANES), 1)
    factor = math.log2(math.e) / math.sqrt(head_size)

    def pair_step(pair, carry):
        queries, keys, values = project_pair(normed, heads, pair)
        for i in range(2):
            lanes = slice(i * LANES, (i + 1) * LANES)
            query = unit_heads(queries[:, lanes], gains[0:1, :], head_size, factor)
            key = unit_heads(keys[:, lanes], gains[1:2, :], head_size, 1.0)
            value = jnp.where(column == head_size, 1.0, values[:, lanes])
            value = jnp.where(inside, value, 0.0).astype(BF16)
            unnormed = jnp.exp2(dot_nt(query, key)).astype(BF16)
            summed = jnp.dot(unnormed, value, preferred_element_type=F32)
            attended[2 * pair + i] = (summed / summed[:, head_size : head_size + 1]).astype(BF16)
        return carry

    lax.fori_loop(0, heads.shape[1] // 2, pair_step, 0)
    gather_heads(attended, packed, head_size, 64)

    def finish(i, carry):
        rows = pl.ds(pl.multiple_of(i * 128, 128), 128)
        projection = dot_nt(packed[rows, :], out_rows[...])
        updated = (tokens[rows, :].astype(F32) + levels[2:3, :] * projection).astype(BF16)
        for d in range(8):
            for j in range(residual.shape[1] // 16):
                residual[8 * i + d, 16 * j : 16 * j + 16, :] = updated[
                    16 * d : 16 * d + 16, LANES * j : LANES * (j + 1)
                ]
        return carry

    lax.fori_loop(0, row_count // 128, finish, 0)


def temporal_kernel(head_size, received, levels, gains, allowed, w_final, gathered, predicted,
                    landing, heads, out_rows, normed, attended, packed, by_slot, sem):
    arriving = pltpu.make_async_copy(gathered.at[:, 1], landing, sem)
    arriving.start()
    frames = received.shape[0]
    locations = 16
    row_count, width = normed.shape

    def by_frame(b, carry):
        rows = pl.ds(pl.multiple_of(b * locations, 16), locations)
        for j in range(width // LANES):
            packed[rows, LANES * j : LANES * (j + 1)] = received[b, 16 * j : 16 * j + 16, :]
        return carry

    lax.fori_loop(0, frames, by_frame, 0)
    row = lax.broadcasted_iota(jnp.int32, (row_count, row_count), 0)
    column = lax.broadcasted_iota(jnp.int32, (row_count, row_count), 1)
    source = (row % frames) * locations + row // frames
    moved = (column == source).astype(F32).astype(BF16)
    by_slot[...] = jnp.dot(moved, packed[...], preferred_element_type=F32).astype(BF16)
    modulate_rows(by_slot, normed, levels[4:5, :], levels[3:4, :], 64)
    arriving.wait()
    lay_out_weights(landing, heads, out_rows, head_size)
    ones_column = lax.broadcasted_iota(jnp.int32, (row_count, LANES), 1) == head_size
    factor = math.log2(math.e) / math.sqrt(head_size)

    def pair_step(pair, carry):
        queries, keys, values = project_pair(normed, heads, pair)
        for i in range(2):
            lanes = slice(i * LANES, (i + 1) * LANES)
            query = unit_heads(queries[:, lanes], gains[2:3, :], head_size, factor)
            key = unit_heads(keys[:, lanes], gains[3:4, :], head_size, 1.0)
            value = jnp.where(ones_column, 1.0, values[:, lanes]).astype(BF16)
            for start in range(0, row_count, TEMPORAL_ROWS):
                rows = slice(start, start + TEMPORAL_ROWS)
                unnormed = (jnp.exp2(dot_nt(query[rows], key[rows])) * allowed[...]).astype(BF16)
                summed = jnp.dot(unnormed, value[rows], preferred_element_type=F32)
                attended[2 * pair + i, rows, :] = (summed / summed[:, head_size : head_size + 1]).astype(BF16)
        return carry

    lax.fori_loop(0, heads.shape[1] // 2, pair_step, 0)
    gather_heads(attended, packed, head_size, 64)

    def finish(i, carry):
        rows = pl.ds(pl.multiple_of(i * 128, 128), 128)
        projection = dot_nt(packed[rows, :], out_rows[...])
        updated = by_slot[rows, :].astype(F32) + levels[5:6, :] * projection
        normed[rows, :] = layer_norm(updated).astype(BF16)
        return carry

    lax.fori_loop(0, row_count // 128, finish, 0)
    predicted[...] = dot_nt(w_final[...], normed[...])


def weight_scratch(shards, shard_rows, rows, width, head_size):
    head_count = width // head_size
    return [
        pltpu.VMEM((shards, shard_rows, width), BF16),
        pltpu.VMEM((3, head_count, LANES, width), BF16),
        pltpu.VMEM((width, width), BF16),
        pltpu.VMEM((rows, width), BF16),
        pltpu.VMEM((head_count, rows, LANES), BF16),
        pltpu.VMEM((rows, width), BF16),
    ]


def body(
    tokens,
    modulation,
    w_qkv_s,
    w_out_s,
    w_qkv_t,
    w_out_t,
    w_final,
    norm_gains,
    clip_tokens,
    block_clip,
):
    rows, width = tokens.shape[1:]
    head_size = norm_gains.shape[1]
    frames = block_clip.shape[0]
    seq = lax.axis_size("seq")
    locations = rows // seq
    position = lax.axis_index("seq")
    branch_index = lax.axis_index("cfg")
    levels = modulation[0]
    member = block_clip[:, None] == jnp.arange(clip_tokens.shape[0], dtype=jnp.int32)[None, :]
    lengths = jnp.sum(jnp.where(member, clip_tokens[None, :], 0), axis=1)
    own_length = lax.dynamic_slice_in_dim(lengths, position, 1)
    gains = jnp.pad(norm_gains, ((0, 0), (0, LANES - head_size)))
    slot_of = jnp.arange(TEMPORAL_ROWS, dtype=jnp.int32) // frames
    clip_of = jnp.tile(block_clip, TEMPORAL_ROWS // frames)
    allowed = ((slot_of[:, None] == slot_of[None, :]) & (clip_of[:, None] == clip_of[None, :])).astype(F32)

    own_shard = jnp.stack(
        [
            jnp.concatenate([w_qkv_s.T, w_out_s.T], axis=0),
            jnp.concatenate([w_qkv_t.T, w_out_t.T], axis=0),
        ]
    )
    shard_rows = own_shard.shape[1]
    gathered = lax.all_gather(own_shard, ("seq", "cfg"), axis=0, tiled=False)
    shards = gathered.shape[0]
    params = pltpu.CompilerParams(vmem_limit_bytes=58 * 2**20)
    vmem = pl.BlockSpec(memory_space=pltpu.VMEM)
    smem = pl.BlockSpec(memory_space=pltpu.SMEM)
    anywhere = pl.BlockSpec(memory_space=pl.ANY)
    tile_rows = locations * width // LANES
    scratch = weight_scratch(shards, shard_rows, rows, width, head_size)
    residual = pl.pallas_call(
        functools.partial(spatial_kernel, head_size),
        out_shape=jax.ShapeDtypeStruct((seq, tile_rows, LANES), BF16),
        in_specs=[smem, vmem, vmem, vmem, anywhere],
        out_specs=vmem,
        scratch_shapes=scratch + [pltpu.SemaphoreType.DMA],
        compiler_params=params,
        name="spatial",
    )(own_length, tokens[0], levels, gains, gathered)
    received = lax.all_to_all(residual, "seq", split_axis=0, concat_axis=0, tiled=True)
    predicted = pl.pallas_call(
        functools.partial(temporal_kernel, head_size),
        out_shape=jax.ShapeDtypeStruct((w_final.shape[1], rows), F32),
        in_specs=[vmem, vmem, vmem, vmem, vmem, anywhere],
        out_specs=vmem,
        scratch_shapes=scratch + [pltpu.VMEM((rows, width), BF16), pltpu.SemaphoreType.DMA],
        compiler_params=params,
        name="temporal",
    )(received, levels, gains, allowed, w_final.T, gathered)

    half = predicted.shape[0] // 2
    outgoing = lax.dynamic_slice_in_dim(predicted, (1 - branch_index) * half, half, 0)
    other = lax.ppermute(outgoing, "cfg", [(0, 1), (1, 0)])
    own_part = lax.dynamic_slice_in_dim(predicted, branch_index * half, half, 0)
    conditional = jnp.where(branch_index == 0, own_part, other)
    unconditional = jnp.where(branch_index == 0, other, own_part)
    guided = (unconditional + 7.0 * (conditional - unconditional)).reshape(half, locations, frames)
    location_ids = position * locations + jnp.arange(locations, dtype=jnp.int32)
    inside = location_ids[:, None] < lengths[None, :]
    return jnp.where(inside[None], guided, 0.0).transpose(2, 1, 0)


def solution(mesh):
    in_specs = (
        P(("rep", "seq"), None, None),
        P("cfg", None, None),
        P(None, ("seq", "cfg")),
        P(None, ("seq", "cfg")),
        P(None, ("seq", "cfg")),
        P(None, ("seq", "cfg")),
        P(),
        P(),
        P("rep"),
        P("rep"),
    )
    out_specs = P("rep", "seq", "cfg")
    return jax.shard_map(body, mesh=mesh, in_specs=in_specs, out_specs=out_specs, check_vma=False)
```

time: 434 us -> 243 us (0.56); the launches traced: 428 us -> 243 us
  waiting for transfers between devices: 254 us -> 142 us
  local copies, waits for them, and re-layouts: 80.7 us -> 3.76 us
  Pallas kernels: 0 us -> 68.6 us
  matrix products: 38.8 us -> 0 us
  other arithmetic: 34.7 us -> 4.13 us
    all_gather x4 -> x1, waiting for transfers between devices: 250 us -> 115 us  [body(): gathered = lax.all_gather(own_shard, ('seq', 'cfg'), axis=0, tiled=False)]
    pallas_call x0 -> x2, Pallas kernels: none -> 68.6 us  [the longest x1 35.3 us: body(): pl.pallas_call(functools.partial(temporal_kernel, head_size), out_shape=j...]
    unnamed x28 -> x11, local copies, waits for them, and re-layouts: 44.1 us -> 1.69 us
    dot_general x9 -> x0, matrix products: 38.8 us -> none  [the longest x4 22.7 us: apply_weight(): jnp.dot(row_block, lax.all_gather(weight, ('seq', 'cfg'), axis=1, tiled=T...]
    all_to_all x1, waiting for transfers between devices: 0.01 us -> 26.4 us  [body(): lax.all_to_all(residual, 'seq', split_axis=0, concat_axis=0, tiled=True)]
    reduce_sum x9 -> x0, other arithmetic: 16.1 us -> none  [the longest x4 7.47 us: head_scale(): jnp.mean(values_in * values_in, axis=-1, keepdims=True) + 1e-06]
    slice x7 -> x0, local copies, waits for them, and re-layouts: 14.7 us -> none  [the longest x2 6.88 us: spatial_attend(): projected[:, features:2 * features]]
    reshape x2 -> x1, local copies, waits for them, and re-layouts: 11 us -> 0.08 us  [body(): (unconditional + 7.0 * (conditional - unconditional)).reshape(half, locat...]
  transfers between devices with their start and end apart: 6 -> 3, of which waited for: 5 -> 3; matrix products, arithmetic and copies ran while one was open for 19% -> 1% of each run, Pallas kernels for 0% -> 0%
where the time goes in v1:
time: 243 us
  waiting for transfers between devices  142 us (58%)
  Pallas kernels  68.6 us (28%)
  between operations  13.5 us (6%)
  starting transfers between devices  10.3 us (4%)
  other arithmetic  4.13 us (2%)
  local copies, waits for them, and re-layouts  3.76 us (2%)
    all_gather x1, waiting for transfers between devices, body(): gathered = lax.all_gather(own_shard, ('seq', 'cfg'), axis=0, tiled=False)  115 us
    pallas_call x1, Pallas kernels, body(): pl.pallas_call(functools.partial(temporal_kernel, head_size), out_shape=j...  35.3 us
    pallas_call x1, Pallas kernels, body(): pl.pallas_call(functools.partial(spatial_kernel, head_size), out_shape=ja...  33.4 us
    all_to_all x1, waiting for transfers between devices, body(): lax.all_to_all(residual, 'seq', split_axis=0, concat_axis=0, tiled=True)  26.4 us
    all_to_all x1, starting transfers between devices, body(): lax.all_to_all(residual, 'seq', split_axis=0, concat_axis=0, tiled=True)  5.26 us
    ppermute x1, starting transfers between devices, body(): other = lax.ppermute(outgoing, 'cfg', [(0, 1), (1, 0)])  4.98 us
  transfers between devices with their start and end apart: 3, of which 3 were waited for; matrix products, arithmetic and copies ran while one was open for 1% of the time, Pallas kernels for 0%

profile of v1, /device:TPU:1, one launch (start us, length us, event | category | flops | bytes accessed | tf_op | source)
XLA Modules:
  0.0 242.7 jit_solution(1631753290049558979)
XLA Ops:
  6.5 0.0 copy-start.1
  6.5 0.0 copy-start.4
  6.5 0.0 copy-start.3
  6.5 0.0 copy-start.2
  6.5 0.0 all-gather.3.cloned.1.call-start
  6.6 1.1 maximum_bitcast_fusion
  7.7 0.8 pad_maximum_fusion
  8.4 0.0 all-gather.3.cloned.1.call-update
  8.5 0.0 copy-done.1
  8.5 0.6 copy.19
  9.1 0.0 copy-done.4
  9.1 0.0 copy-done.3
  9.1 0.1 select_reduce_fusion
  9.2 0.6 dynamic_slice.9.length_ref
  9.8 0.0 copy-done.2
  9.8 0.6 pad.4.gains
  10.4 115.2 %all-gather.3.cloned.1.call-done = bf16[128,72,1152]{2,1,0:T(8,128)(2,1)} async-done(((bf16[2,72,1152]{2,1,0:T(8,128)(2,1)}), bf16[128,72,1152]{2,1,0:T(8,128)(2,1)}) %all-gather.3.cloned.1.call-update) | async-done | bytes 21233680 | tf_op jit(solution)/shard_map/all_gather | solution.py:230
  125.5 33.4 %spatial.1 = bf16[32,144,128]{2,1,0:T(8,128)(2,1)} custom-call(s32[1]{0:T(128)} %dynamic_slice.9.length_ref, bf16[512,1152]{1,0:T(8,128)(2,1)} %bitcast.18, f32[6,1152]{1,0:T(8,128)} %bitcast.19, f32[4,128]{1,0:T(4,128)} %pad.4.gains, bf16[64,2,72,1152]{3,2,1,0:T(8,128)(2,1)} %bitcast.16), custom_call_target="tpu_custom_call" | custom-call | tf_op jit(solution)/shard_map/spatial/pallas_call | solution.py:238
  158.9 5.3 %all-to-all-start = ((bf16[32,144,128]{2,1,0:T(8,128)(2,1)}), bf16[32,144,128]{2,1,0:T(8,128)(2,1)S(1)}, u32[]{:S(2)}, u32[]{:S(2)}) async-start(bf16[32,144,128]{2,1,0:T(8,128)(2,1)} %spatial.1), calls=%async_computation | async-start | bytes 2359296 | tf_op jit(solution)/shard_map/all_to_all | solution.py:247
  164.2 0.1 eq.52
  164.3 0.7 and_convert_fusion.allowed
  165.0 26.4 %all-to-all-done.received = bf16[32,144,128]{2,1,0:T(8,128)(2,1)S(1)} async-done(((bf16[32,144,128]{2,1,0:T(8,128)(2,1)}), bf16[32,144,128]{2,1,0:T(8,128)(2,1)S(1)}, u32[]{:S(2)}, u32[]{:S(2)}) %all-to-all-start) | async-done | bytes 1179680 | tf_op jit(solution)/shard_map/all_to_all | solution.py:247
  191.4 0.0 copy-start
  191.4 1.1 copy-done
  192.5 35.3 %temporal.1 = f32[16,512]{1,0:T(8,128)} custom-call(bf16[32,144,128]{2,1,0:T(8,128)(2,1)} %copy-done, f32[6,1152]{1,0:T(8,128)} %bitcast.20, f32[4,128]{1,0:T(4,128)} %pad.4.gains, f32[128,128]{1,0:T(8,128)} %and_convert_fusion.allowed, bf16[16,1152]{1,0:T(8,128)(2,1)} %bitcast.25, bf16[64,2,72,1152]{3,2,1,0:T(8,128)(2,1)} %bitcast.17), custom_call_target="tpu_custom_call" | custom-call | tf_op jit(solution)/shard_map/temporal/pallas_call | solution.py:248
  227.8 0.7 constant_dynamic-slice_fusion
  228.5 5.0 %collective-permute-start = (f32[8,512]{1,0:T(8,128)S(1)}, f32[8,512]{1,0:T(8,128)S(1)}, u32[]{:S(2)}, u32[]{:S(2)}) collective-permute-start(f32[8,512]{1,0:T(8,128)S(1)} %constant_dynamic-slice_fusion), channel_id=1, source_target_pairs={{0,1},{1,0},{2,3},{3,2},{4,5},{5,4},{6,7},{7,6},{8,9},{9,8},{10,11... | collective-permute-start | bytes 49160 | tf_op jit(solution)/shard_map/ppermute | solution.py:260
  233.5 0.1 broadcast_compare_fusion
  233.6 0.8 collective-permute-done
  234.3 0.7 multiply_add_fusion
  235.1 0.1 reshape.66
  235.2 0.7 fusion
  (3 shorter events, 0.0 us)
Async XLA Ops:
  6.5 1.9 copy-start.1
  6.5 2.6 %copy-start.4 = (s32[8]{0:T(128)S(1)}, s32[8]{0:T(128)}, u32[]{:S(2)}) copy-start(s32[8]{0:T(128)} %param.18) | copy-start | bytes 100
  6.5 2.6 %copy-start.3 = (s32[32]{0:T(128)S(1)}, s32[32]{0:T(128)}, u32[]{:S(2)}) copy-start(s32[32]{0:T(128)} %param.19) | copy-start | bytes 388
  6.5 3.2 %copy-start.2 = (f32[4,72]{1,0:T(4,128)S(1)}, f32[4,72]{1,0:T(4,128)}, u32[]{:S(2)}) copy-start(f32[4,72]{1,0:T(4,128)} %param.17) | copy-start | bytes 3460
  6.5 119.0 %all-gather.3.cloned.1.call-start = ((), (), s32[]{:S(2)}) async-start(), calls=%async_computation.1 | async-start | bytes 21565440 | tf_op jit(solution)/shard_map/all_gather | solution.py:230
  158.9 32.6 %all-to-all-start = ((bf16[32,144,128]{2,1,0:T(8,128)(2,1)}), bf16[32,144,128]{2,1,0:T(8,128)(2,1)S(1)}, u32[]{:S(2)}, u32[]{:S(2)}) async-start(bf16[32,144,128]{2,1,0:T(8,128)(2,1)} %spatial.1), calls=%async_computation | async-start | bytes 2359296 | tf_op jit(solution)/shard_map/all_to_all | solution.py:247
  191.4 1.1 copy-start
  228.5 5.8 %collective-permute-start = (f32[8,512]{1,0:T(8,128)S(1)}, f32[8,512]{1,0:T(8,128)S(1)}, u32[]{:S(2)}, u32[]{:S(2)}) collective-permute-start(f32[8,512]{1,0:T(8,128)S(1)} %constant_dynamic-slice_fusion), channel_id=1, source_target_pairs={{0,1},{1,0},{2,3},{3,2},{4,5},{5,4},{6,7},{7,6},{8,9},{9,8},{10,11... | collective-permute-start | bytes 49160 | tf_op jit(solution)/shard_map/ppermute | solution.py:260
Sparse Core Ops, SparseCore 0:
  10.1 115.4 all-gather.2

commit v2 on v1

v2 whole, which is shorter than its diff:
```python
import functools
import math

import jax
import jax.numpy as jnp
from jax import lax
from jax.experimental import pallas as pl
from jax.experimental.pallas import tpu as pltpu
from jax.sharding import PartitionSpec as P

BF16 = jnp.bfloat16
F32 = jnp.float32
LANES = 128
TEMPORAL_ROWS = 256
X_RING, Z_RING, SPLIT = 4, 8, 384
X_SLOTS = (0, -1, 1, 2)
Z_SLOTS = (0, -1, -2, -3, 1, 2, 3, 4)

def swap_cores(array):
    return lax.ppermute(array, "cfg", [(0, 1), (1, 0)])


def plane_step(array, along_x, far=1):
    pairs = []
    for x in range(X_RING):
        for z in range(Z_RING):
            for core in range(2):
                by = (1 - 2 * core) * far
                to = ((x + by) % X_RING, z) if along_x else (x, (z + by) % Z_RING)
                pairs.append((2 * (x * Z_RING + z) + core, 2 * (to[0] * Z_RING + to[1]) + core))
    return lax.ppermute(array, ("seq", "cfg"), pairs)


def replica_step(array):
    size = lax.axis_size("rep")
    pairs = []
    for y in range(size):
        for core in range(2):
            pairs.append((2 * y + core, 2 * ((y + 1 - 2 * core) % size) + core))
    return lax.ppermute(array, ("rep", "cfg"), pairs)


def in_core_order(core, first, second):
    return jnp.where(core == 0, first, second), jnp.where(core == 0, second, first)


def after(array, earlier):
    return array + earlier[(0,) * earlier.ndim] * jnp.zeros((), array.dtype)


def spread_in_plane(own, core):
    pair = jnp.stack(in_core_order(core, own, swap_cores(own)))
    first, second = pair[:, :, :SPLIT], pair[:, :, SPLIT:]

    def own_half(parts):
        return lax.dynamic_index_in_dim(parts, core, 0, keepdims=True)

    near = [plane_step(second, False, far) for far in (1, 2, 3)]
    near.append(plane_step(own_half(second), False, 4))
    mine = jnp.concatenate([plane_step(first, True), plane_step(own_half(first), True, 2)])
    started = mine
    mine = after(mine, near[3])
    theirs = swap_cores(mine)
    low, high = in_core_order(core, mine[:2], theirs[:2])
    opposite = jnp.concatenate(in_core_order(core, mine[2:], theirs[2:]))
    row = [first, low, high, opposite]
    mine = after(jnp.concatenate(near), started)
    theirs = swap_cores(mine)
    low, high = in_core_order(core, mine[:6], theirs[:6])
    opposite = jnp.concatenate(in_core_order(core, mine[6:], theirs[6:]))
    ring = jnp.concatenate([second, low, high, opposite]).reshape((Z_RING,) + second.shape)
    row = after(jnp.stack(row), theirs)
    across = plane_step(ring, True)
    beyond = plane_step(lax.dynamic_slice_in_dim(across, 4 * core, 4, 0), True)
    rows = [row]
    for hop in range(3):
        rows.append(plane_step(after(rows[-1], across) if hop == 2 else rows[-1], False))
    rows.append(plane_step(lax.dynamic_slice_in_dim(rows[3], 2 * core, 2, 0), False))
    rows += [swap_cores(part) for part in rows[1:]]
    return rows, [ring, across, beyond, swap_cores(across), swap_cores(beyond)]


def pick(table, index):
    found = table[-1]
    for i in range(len(table) - 1):
        found = jnp.where(index == i, table[i], found)
    return found


def plane_copies(place, rows, rings, landing, sem):
    x, z, core = place[0], place[1], place[2]
    sign = 1 - 2 * core
    rest = landing.shape[2] - SPLIT
    copies = []

    def to_landing(part, dx, dz, columns):
        shard = 2 * (lax.rem(x + dx + X_RING, X_RING) * Z_RING + lax.rem(z + dz + Z_RING, Z_RING))
        copies.append(pltpu.make_async_copy(part, landing.at[pl.ds(shard, 2), :, columns], sem))

    for k in range(9):
        hop = k if k < 5 else k - 4
        dz = -sign * hop if k < 5 else sign * hop
        for j in range(rows[k].shape[0]):
            dx = X_SLOTS[j] if hop < 4 else pick(X_SLOTS, (2 * core if k < 5 else 2 - 2 * core) + j)
            to_landing(rows[k].at[j], dx, dz, pl.ds(0, SPLIT))
    for part, dx, start in zip(rings, (0, -sign, 2, sign, 2), (0, 0, 4 * core, 0, 4 - 4 * core)):
        for j in range(part.shape[0]):
            dz = Z_SLOTS[j] if part.shape[0] == Z_RING else pick(Z_SLOTS, start + j)
            to_landing(part.at[j], dx, dz, pl.ds(SPLIT, rest))
    return copies


def replica_copies(place, parts, landing, sem):
    core, y = place[2], place[3]
    size = landing.shape[0]
    sign = 1 - 2 * core
    held, mine, theirs, mine_far, theirs_far = parts
    far = mine_far.shape[0]

    def to(part, dy, start=None):
        slot = landing.at[lax.rem(y + dy + size, size)]
        return pltpu.make_async_copy(part, slot if start is None else slot.at[pl.ds(start, far)], sem)

    return [
        to(held, 0),
        to(mine, -sign),
        to(theirs, sign),
        to(mine_far, 2, far * core),
        to(theirs_far, 2, far - far * core),
    ]


def dot_over(left, right, left_dim, right_dim):
    return lax.dot_general(
        left, right, (((left_dim,), (right_dim,)), ((), ())), preferred_element_type=F32
    )


def layer_norm(values_in, axis):
    average = jnp.mean(values_in, axis=axis, keepdims=True)
    centred = values_in - average
    variance = jnp.mean(centred * centred, axis=axis, keepdims=True)
    return centred * lax.rsqrt(variance + 1e-06)


def lay_out_weights(landing, columns, out_rows, head_size):
    share = 3 * head_size // 4

    def group(g, carry):
        parts = [landing[8 * g + i] for i in range(8)]
        for target, rows in (
            (columns, [part[:share] for part in parts]),
            (out_rows, [part[share:] for part in parts]),
        ):
            size = 8 * rows[0].shape[0]
            target[pl.ds(pl.multiple_of(g * size, 16), size), :] = jnp.concatenate(rows, axis=0)
        return carry

    lax.fori_loop(0, landing.shape[0] // 8, group, 0)


def lay_out_quarters(landing, columns, out_rows, head_size):
    quarter = head_size // 4

    def group(g, carry):
        for target, kinds in ((columns, (0, 1, 2)), (out_rows, (3,))):
            rows = [landing[kind, 8 * g + i][:quarter] for i in range(8) for kind in kinds]
            size = quarter * len(rows)
            target[pl.ds(pl.multiple_of(g * size, 16), size), :] = jnp.concatenate(rows, axis=0)
        return carry

    lax.fori_loop(0, landing.shape[1] // 8, group, 0)


def project(columns, normed, projected):
    width = normed.shape[0]

    def kind(i, carry):
        rows = pl.ds(pl.multiple_of(i * width, 16), width)
        projected[rows, :] = jnp.dot(columns[rows, :], normed[...], preferred_element_type=F32)
        return carry

    lax.fori_loop(0, 3, kind, 0)


def unit_heads(head, gain_column):
    total = jnp.sum(head * head, axis=0, keepdims=True)
    return (head * lax.rsqrt(total / head.shape[0] + 1e-06) * gain_column).astype(BF16)


def attend(projected, attended, gains, first_gain, inside, allowed, head_size):
    width = attended.shape[0]
    row_count = attended.shape[1]
    block = row_count if allowed is None else allowed.shape[0]
    factor = math.log2(math.e) / math.sqrt(head_size)
    query_gain = gains[:, first_gain : first_gain + 1] * factor
    key_gain = gains[:, first_gain + 1 : first_gain + 2]
    ones = jnp.ones((1, row_count), F32)
    blank = jnp.zeros((7, row_count), F32)

    def head(h):
        def part(kind):
            return projected[pl.ds(pl.multiple_of(kind * width + h * head_size, 8), head_size), :]

        query = unit_heads(part(0), query_gain)
        key = unit_heads(part(1), key_gain)
        value = jnp.concatenate([part(2), ones, blank], axis=0)
        if inside is not None:
            value = jnp.where(inside, value, 0.0)
        value = value.astype(BF16)
        found = []
        for start in range(0, row_count, block):
            tokens = slice(start, start + block)
            unnormed = jnp.exp2(dot_over(key[:, tokens], query[:, tokens], 0, 0))
            if allowed is not None:
                unnormed = unnormed * allowed[...]
            summed = jnp.dot(value[:, tokens], unnormed.astype(BF16), preferred_element_type=F32)
            found.append(summed[:head_size] / summed[head_size : head_size + 1])
        return jnp.concatenate(found, axis=1) if len(found) > 1 else found[0]

    def pair(p, carry):
        both = jnp.concatenate([head(2 * p), head(2 * p + 1)], axis=0)
        rows = pl.ds(pl.multiple_of(2 * head_size * p, 16), 2 * head_size)
        attended[rows, :] = both.astype(BF16)
        return carry

    lax.fori_loop(0, width // (2 * head_size), pair, 0)


def spatial_kernel(head_size, place, length_ref, tokens, levels, gains, *refs):
    rows, rings = refs[:9], refs[9:14]
    residual, landing, columns, out_rows, normed, projected, attended, sem = refs[14:]
    arriving = plane_copies(place, rows, rings, landing, sem)
    for copy in arriving:
        copy.start()
    row_count, width = tokens.shape
    for start in range(0, row_count, LANES):
        chunk = slice(start, start + LANES)
        values_in = layer_norm(tokens[chunk, :].astype(F32), 1) * (1.0 + levels[1:2, :]) + levels[0:1, :]
        normed[:, chunk] = values_in.astype(BF16).T
    for copy in arriving:
        copy.wait()
    lay_out_weights(landing, columns, out_rows, head_size)
    project(columns, normed, projected)
    inside = lax.broadcasted_iota(jnp.int32, (head_size + 8, row_count), 1) < length_ref[0]
    attend(projected, attended, gains, 0, inside, None, head_size)
    for start in range(0, row_count, 256):
        chunk = slice(start, start + 256)
        projection = dot_over(attended[:, chunk], out_rows[...], 0, 1)
        updated = (tokens[chunk, :].astype(F32) + levels[2:3, :] * projection).astype(BF16)
        for d in range(16):
            for j in range(residual.shape[1] // 16):
                residual[start // 16 + d, 16 * j : 16 * j + 16, :] = updated[
                    16 * d : 16 * d + 16, LANES * j : LANES * (j + 1)
                ]


def temporal_kernel(head_size, place, received, levels, gains, allowed, w_final, *refs):
    predicted, landing, columns, out_rows, normed, projected, attended, by_frame, by_slot, sem = refs[5:]
    arriving = replica_copies(place, refs[:5], landing, sem)
    for copy in arriving:
        copy.start()
    frames = received.shape[0]
    width, row_count = normed.shape
    locations = row_count // frames

    def unpack(b, carry):
        rows = pl.ds(pl.multiple_of(b * locations, 16), locations)
        for j in range(width // LANES):
            by_frame[rows, LANES * j : LANES * (j + 1)] = received[b, 16 * j : 16 * j + 16, :]
        return carry

    lax.fori_loop(0, frames, unpack, 0)
    row = lax.broadcasted_iota(jnp.int32, (row_count, row_count), 0)
    column = lax.broadcasted_iota(jnp.int32, (row_count, row_count), 1)
    moved = (row == (column % frames) * locations + column // frames).astype(F32).astype(BF16)
    by_slot[...] = dot_over(by_frame[...], moved, 0, 0).astype(BF16)
    for start in range(0, row_count, LANES):
        chunk = slice(start, start + LANES)
        values_in = layer_norm(by_slot[:, chunk].astype(F32), 0)
        normed[:, chunk] = (values_in * (1.0 + levels[:, 4:5]) + levels[:, 3:4]).astype(BF16)
    for copy in arriving:
        copy.wait()
    lay_out_quarters(landing, columns, out_rows, head_size)
    project(columns, normed, projected)
    attend(projected, attended, gains, 2, None, allowed, head_size)
    projected[0:width, :] = jnp.dot(out_rows[...], attended[...], preferred_element_type=F32)
    for start in range(0, row_count, LANES):
        chunk = slice(start, start + LANES)
        updated = by_slot[:, chunk].astype(F32) + levels[:, 5:6] * projected[0:width, chunk]
        normed[:, chunk] = layer_norm(updated, 0).astype(BF16)
    predicted[...] = jnp.dot(w_final[...], normed[...], preferred_element_type=F32)


def weight_scratch(landing_shape, rows, width):
    return [
        pltpu.VMEM(landing_shape, BF16),
        pltpu.VMEM((3 * width, width), BF16),
        pltpu.VMEM((width, width), BF16),
        pltpu.VMEM((width, rows), BF16),
        pltpu.VMEM((3 * width, rows), F32),
        pltpu.VMEM((width, rows), BF16),
    ]


def body(
    tokens,
    modulation,
    w_qkv_s,
    w_out_s,
    w_qkv_t,
    w_out_t,
    w_final,
    norm_gains,
    clip_tokens,
    block_clip,
):
    rows, width = tokens.shape[1:]
    head_size = norm_gains.shape[1]
    frames = block_clip.shape[0]
    seq = lax.axis_size("seq")
    locations = rows // seq
    position = lax.axis_index("seq")
    branch_index = lax.axis_index("cfg")
    levels = modulation[0]
    member = block_clip[:, None] == jnp.arange(clip_tokens.shape[0], dtype=jnp.int32)[None, :]
    lengths = jnp.sum(jnp.where(member, clip_tokens[None, :], 0), axis=1)
    own_length = lax.dynamic_slice_in_dim(lengths, position, 1)
    gains = norm_gains.T
    slot_of = jnp.arange(TEMPORAL_ROWS, dtype=jnp.int32) // frames
    clip_of = jnp.tile(block_clip, TEMPORAL_ROWS // frames)
    allowed = ((slot_of[:, None] == slot_of[None, :]) & (clip_of[:, None] == clip_of[None, :])).astype(F32)

    y = lax.axis_index("rep")
    place = jnp.stack([position // Z_RING, position % Z_RING, branch_index, y]).astype(jnp.int32)
    later = jnp.concatenate([w_qkv_t.T, w_out_t.T], axis=0)
    quarter_rows = later.shape[0] // lax.axis_size("rep")
    own_quarter = lax.dynamic_slice_in_dim(later, y * quarter_rows, quarter_rows, 0)
    own_quarter = jnp.pad(own_quarter, ((0, -quarter_rows % 8), (0, 0)))
    quarter = lax.all_gather(own_quarter, ("seq", "cfg"), axis=0, tiled=False)
    row_parts, ring_parts = spread_in_plane(jnp.concatenate([w_qkv_s.T, w_out_s.T], axis=0), branch_index)
    shards = quarter.shape[0]
    quarter = after(after(quarter, row_parts[4]), ring_parts[2])
    params = pltpu.CompilerParams(vmem_limit_bytes=58 * 2**20)
    vmem = pl.BlockSpec(memory_space=pltpu.VMEM)
    smem = pl.BlockSpec(memory_space=pltpu.SMEM)
    anywhere = pl.BlockSpec(memory_space=pl.ANY)
    tile_rows = locations * width // LANES
    cost = pl.CostEstimate(flops=30_000_000_000, bytes_accessed=20_000_000, transcendentals=0)
    residual = pl.pallas_call(
        functools.partial(spatial_kernel, head_size),
        out_shape=jax.ShapeDtypeStruct((seq, tile_rows, LANES), BF16),
        in_specs=[smem, smem, vmem, vmem, vmem] + [anywhere] * 14,
        out_specs=vmem,
        scratch_shapes=weight_scratch((shards, later.shape[0], width), rows, width)
        + [pltpu.SemaphoreType.DMA],
        compiler_params=params,
        cost_estimate=cost,
        name="spatial",
    )(place, own_length, tokens[0], levels, gains, *row_parts, *ring_parts)
    next_quarter = replica_step(quarter)
    next_quarter = after(next_quarter, residual)
    far_quarter = replica_step(
        lax.dynamic_slice_in_dim(next_quarter, branch_index * (shards // 2), shards // 2, 0)
    )
    quarters = (quarter, next_quarter, swap_cores(next_quarter), far_quarter, swap_cores(far_quarter))
    received = lax.all_to_all(residual, "seq", split_axis=0, concat_axis=0, tiled=True)
    predicted = pl.pallas_call(
        functools.partial(temporal_kernel, head_size),
        out_shape=jax.ShapeDtypeStruct((w_final.shape[1], rows), F32),
        in_specs=[smem, vmem, vmem, vmem, vmem, vmem] + [anywhere] * 5,
        out_specs=vmem,
        scratch_shapes=weight_scratch(
            (lax.axis_size("rep"), shards, quarter.shape[1], width), rows, width
        )
        + [pltpu.VMEM((rows, width), BF16), pltpu.VMEM((width, rows), BF16), pltpu.SemaphoreType.DMA],
        compiler_params=params,
        cost_estimate=cost,
        name="temporal",
    )(place, received, levels.T, gains, allowed, w_final.T, *quarters)

    half = predicted.shape[0] // 2
    outgoing = lax.dynamic_slice_in_dim(predicted, (1 - branch_index) * half, half, 0)
    other = lax.ppermute(outgoing, "cfg", [(0, 1), (1, 0)])
    own_part = lax.dynamic_slice_in_dim(predicted, branch_index * half, half, 0)
    conditional = jnp.where(branch_index == 0, own_part, other)
    unconditional = jnp.where(branch_index == 0, other, own_part)
    guided = (unconditional + 7.0 * (conditional - unconditional)).reshape(half, locations, frames)
    location_ids = position * locations + jnp.arange(locations, dtype=jnp.int32)
    inside = location_ids[:, None] < lengths[None, :]
    return jnp.where(inside[None], guided, 0.0).transpose(2, 1, 0)


def solution(mesh):
    in_specs = (
        P(("rep", "seq"), None, None),
        P("cfg", None, None),
        P(None, ("seq", "cfg")),
        P(None, ("seq", "cfg")),
        P(None, ("seq", "cfg")),
        P(None, ("seq", "cfg")),
        P(),
        P(),
        P("rep"),
        P("rep"),
    )
    out_specs = P("rep", "seq", "cfg")
    return jax.shard_map(body, mesh=mesh, in_specs=in_specs, out_specs=out_specs, check_vma=False)
```

time: 243 us -> 228 us (0.938)
  waiting for transfers between devices: 142 us -> 79.6 us
  starting transfers between devices: 10.3 us -> 50.6 us
  Pallas kernels: 68.6 us -> 48.1 us
  local copies, waits for them, and re-layouts: 3.76 us -> 17.1 us
  other arithmetic: 4.13 us -> 13.4 us
  between operations: 13.5 us -> 18.2 us
    all_gather x1, waiting for transfers between devices: 115 us -> 0.01 us  [body(): quarter = lax.all_gather(own_quarter, ('seq', 'cfg'), axis=0, tiled=False)]
    ppermute x0 -> x25, waiting for transfers between devices: none -> 66.7 us  [the longest x12 40.4 us: plane_step(): return lax.ppermute(array, ('seq', 'cfg'), pairs)]
    ppermute x0 -> x25, starting transfers between devices: none -> 44.5 us  [the longest x12 23.9 us: plane_step(): return lax.ppermute(array, ('seq', 'cfg'), pairs)]
    all_to_all x1, waiting for transfers between devices: 26.4 us -> 11.7 us  [body(): lax.all_to_all(residual, 'seq', split_axis=0, concat_axis=0, tiled=True)]
    pallas_call x1, Pallas kernels: 33.4 us -> 22.7 us  [body(): pl.pallas_call(functools.partial(spatial_kernel, head_size), out_shape=ja...]
    pallas_call x1, Pallas kernels: 35.3 us -> 25.4 us  [body(): pl.pallas_call(functools.partial(temporal_kernel, head_size), out_shape=j...]
    add x0 -> x6, other arithmetic: none -> 6.86 us  [after(): return array + earlier[(0,) * earlier.ndim] * jnp.zeros((), array.dtype)]
    slice x0 -> x7, local copies, waits for them, and re-layouts: none -> 5.86 us  [after(): return array + earlier[(0,) * earlier.ndim] * jnp.zeros((), array.dtype)]
  transfers between devices with their start and end apart: 3 -> 28, of which waited for: 3 -> 14; matrix products, arithmetic and copies ran while one was open for 1% -> 10% of each run, Pallas kernels for 0% -> 10%
where the time goes in v2:
time: 228 us; the launch traced here: 227 us
  waiting for transfers between devices  79.6 us (35%)
  starting transfers between devices  50.6 us (22%)
  Pallas kernels  48.1 us (21%)
  between operations  18.2 us (8%)
  local copies, waits for them, and re-layouts  17.1 us (8%)
  other arithmetic  13.4 us (6%)
    ppermute x12, waiting for transfers between devices, plane_step(): return lax.ppermute(array, ('seq', 'cfg'), pairs)  40.4 us
    pallas_call x1, Pallas kernels, body(): pl.pallas_call(functools.partial(temporal_kernel, head_size), out_shape=j...  25.4 us
    ppermute x12, starting transfers between devices, plane_step(): return lax.ppermute(array, ('seq', 'cfg'), pairs)  23.9 us
    ppermute x2, waiting for transfers between devices, replica_step(): return lax.ppermute(array, ('rep', 'cfg'), pairs)  23.5 us
    pallas_call x1, Pallas kernels, body(): pl.pallas_call(functools.partial(spatial_kernel, head_size), out_shape=ja...  22.7 us
    ppermute x11, starting transfers between devices, swap_cores(): return lax.ppermute(array, 'cfg', [(0, 1), (1, 0)])  15.4 us
    all_to_all x1, waiting for transfers between devices, body(): lax.all_to_all(residual, 'seq', split_axis=0, concat_axis=0, tiled=True)  11.7 us
    add x6, other arithmetic, after(): return array + earlier[(0,) * earlier.ndim] * jnp.zeros((), array.dtype)  6.86 us
  transfers between devices with their start and end apart: 28, of which 14 were waited for; matrix products, arithmetic and copies ran while one was open for 10% of the time, Pallas kernels for 10%

profile of v2, /device:TPU:1, one launch (start us, length us, event | category | flops | bytes accessed | tf_op | source)
XLA Modules:
  0.0 227.0 jit_solution(5002281308052246479)
XLA Ops:
  6.5 0.9 fusion.3
  7.5 0.6 pad.4
  8.1 1.0 pad_maximum_fusion.1
  9.1 3.3 %collective-permute-start = (bf16[72,1152]{1,0:T(8,128)(2,1)S(1)}, bf16[72,1152]{1,0:T(8,128)(2,1)S(1)}, u32[]{:S(2)}, u32[]{:S(2)}) collective-permute-start(bf16[72,1152]{1,0:T(8,128)(2,1)S(1)} %pad_maximum_fusion.1), channel_id=1, source_target_pairs={{0,1},{1,0},{2,3},{3,2},{4,5},{5,4},{6,7},{7,6},{8,9},{9,8},{10,11... | collective-permute-start | bytes 497672 | tf_op jit(solution)/shard_map/ppermute | solution.py:20
  12.4 1.0 collective-permute-done
  13.5 1.0 select_bitcast_fusion
  14.5 4.8 %collective-permute-start.7 = (bf16[2,72,768]{2,1,0:T(8,128)(2,1)S(1)}, bf16[2,72,768]{2,1,0:T(8,128)(2,1)S(1)}, u32[]{:S(2)}, u32[]{:S(2)}) collective-permute-start(bf16[2,72,768]{2,1,0:T(8,128)(2,1)S(1)} %get-tuple-element.6), channel_id=1, source_target_pairs={{0,6},{1,11},{2,8},{3,13},{4,10},{5,15},{6,12},{7,1},{8,14},{9,3},... | collective-permute-start | bytes 663560 | tf_op jit(solution)/shard_map/ppermute | solution.py:31
  19.3 0.3 collective-permute-start.6
  19.6 0.5 collective-permute-start.5
  20.1 2.6 %collective-permute-start.1 = (bf16[2,72,384]{2,1,0:T(8,128)(2,1)S(1)}, bf16[2,72,384]{2,1,0:T(8,128)(2,1)S(1)}, u32[]{:S(2)}, u32[]{:S(2)}) collective-permute-start(bf16[2,72,384]{2,1,0:T(8,128)(2,1)S(1)} %pad_maximum_fusion.2), channel_id=1, source_target_pairs={{0,16},{1,49},{2,18},{3,51},{4,20},{5,53},{6,22},{7,55},{8,24},{9,... | collective-permute-start | bytes 331784 | tf_op jit(solution)/shard_map/ppermute | solution.py:31
  22.7 4.6 %collective-permute-start.3 = (bf16[1,72,768]{2,1,0:T(8,128)(2,1)S(1)}, bf16[1,72,768]{2,1,0:T(8,128)(2,1)S(1)}, u32[]{:S(2)}, u32[]{:S(2)}) collective-permute-start(bf16[1,72,768]{2,1,0:T(8,128)(2,1)S(1)} %fusion), channel_id=1, source_target_pairs={{0,8},{1,9},{2,10},{3,11},{4,12},{5,13},{6,14},{7,15},{8,0},{9,1},... | collective-permute-start | bytes 331784 | tf_op jit(solution)/shard_map/ppermute | solution.py:31
  27.2 0.5 slice.73
  28.4 5.4 %collective-permute-done.3 = bf16[1,72,768]{2,1,0:T(8,128)(2,1)S(1)} collective-permute-done((bf16[1,72,768]{2,1,0:T(8,128)(2,1)S(1)}, bf16[1,72,768]{2,1,0:T(8,128)(2,1)S(1)}, u32[]{:S(2)}, u32[]{:S(2)}) %collective-permute-start.3) | collective-permute-done | bytes 110624 | tf_op jit(solution)/shard_map/ppermute | solution.py:31
  33.8 0.7 collective-permute-done.6
  34.5 5.2 %collective-permute-done.5 = bf16[2,72,768]{2,1,0:T(8,128)(2,1)S(1)} collective-permute-done((bf16[2,72,768]{2,1,0:T(8,128)(2,1)S(1)}, bf16[2,72,768]{2,1,0:T(8,128)(2,1)S(1)}, u32[]{:S(2)}, u32[]{:S(2)}) %collective-permute-start.5) | collective-permute-done | bytes 221216 | tf_op jit(solution)/shard_map/ppermute | solution.py:31
  39.8 3.1 %collective-permute-start.8 = (bf16[7,72,768]{2,1,0:T(8,128)(2,1)S(1)}, bf16[7,72,768]{2,1,0:T(8,128)(2,1)S(1)}, u32[]{:S(2)}, u32[]{:S(2)}) collective-permute-start(bf16[7,72,768]{2,1,0:T(8,128)(2,1)S(1)} %maximum_add_fusion), channel_id=1, source_target_pairs={{0,1},{1,0},{2,3},{3,2},{4,5},{5,4},{6,7},{7,6},{8,9},{9,8},{10,11... | collective-permute-start | bytes 2322440 | tf_op jit(solution)/shard_map/ppermute | solution.py:20
  42.9 2.9 %collective-permute-start.2 = (bf16[1,72,384]{2,1,0:T(8,128)(2,1)S(1)}, bf16[1,72,384]{2,1,0:T(8,128)(2,1)S(1)}, u32[]{:S(2)}, u32[]{:S(2)}) collective-permute-start(bf16[1,72,384]{2,1,0:T(8,128)(2,1)S(1)} %fusion.2), channel_id=1, source_target_pairs={{0,32},{1,33},{2,34},{3,35},{4,36},{5,37},{6,38},{7,39},{8,40},{9,... | collective-permute-start | bytes 165896 | tf_op jit(solution)/shard_map/ppermute | solution.py:31
  46.0 0.2 select_dynamic-update-slice_fusion
  46.3 1.5 collective-permute-start.11
  47.8 0.6 slice.68
  49.3 1.4 collective-permute-done.4
  50.7 0.6 slice.74
  52.1 0.8 copy-done.2
  52.9 0.6 collective-permute-start.9
  53.4 7.0 %collective-permute-done.9.refs_1_ = bf16[4,2,72,384]{3,2,1,0:T(8,128)(2,1)} collective-permute-done((bf16[4,2,72,384]{3,2,1,0:T(8,128)(2,1)S(1)}, bf16[4,2,72,384]{3,2,1,0:T(8,128)(2,1)}, u32[]{:S(2)}, u32[]{:S(2)}) %collective-permute-start.9) | collective-permute-done | bytes 442400 | tf_op jit(solution)/shard_map/ppermute | solution.py:31
  60.4 1.8 collective-permute-start.10
  62.2 8.3 %collective-permute-done.11.refs_10_ = bf16[8,2,72,768]{3,2,1,0:T(8,128)(2,1)} collective-permute-done((bf16[8,2,72,768]{3,2,1,0:T(8,128)(2,1)S(1)}, bf16[8,2,72,768]{3,2,1,0:T(8,128)(2,1)}, u32[]{:S(2)}, u32[]{:S(2)}) %collective-permute-start.11) | collective-permute-done | bytes 1769504 | tf_op jit(solution)/shard_map/ppermute | solution.py:31
  70.5 1.3 constant_dynamic-slice_fusion.2
  71.8 3.2 %collective-permute-start.18 = (bf16[4,2,72,768]{3,2,1,0:T(8,128)(2,1)S(1)}, bf16[4,2,72,768]{3,2,1,0:T(8,128)(2,1)}, u32[]{:S(2)}, u32[]{:S(2)}) collective-permute-start(bf16[4,2,72,768]{3,2,1,0:T(8,128)(2,1)S(1)} %constant_dynamic-slice_fusion.2), channel_id=1, source_target_pairs={{0,16},{1,49},{2,18},{3,51},{4,20},{5,53},{6,22},{7,55},{8,24},{9,... | collective-permute-start | bytes 2654216 | tf_op jit(solution)/shard_map/ppermute | solution.py:31
  75.0 1.2 slice.79
  77.1 10.2 %collective-permute-done.12.refs_3_ = bf16[4,2,72,384]{3,2,1,0:T(8,128)(2,1)S(1)} collective-permute-done((bf16[4,2,72,384]{3,2,1,0:T(8,128)(2,1)S(1)}, bf16[4,2,72,384]{3,2,1,0:T(8,128)(2,1)S(1)}, u32[]{:S(2)}, u32[]{:S(2)}) %collective-permute-start.12) | collective-permute-done | bytes 442400 | tf_op jit(solution)/shard_map/ppermute | solution.py:31
  87.3 1.2 collective-permute-start.13
  88.5 0.7 collective-permute-start.14
  89.3 3.5 %collective-permute-done.13.refs_4_ = bf16[2,2,72,384]{3,2,1,0:T(8,128)(2,1)S(1)} collective-permute-done((bf16[2,2,72,384]{3,2,1,0:T(8,128)(2,1)S(1)}, bf16[2,2,72,384]{3,2,1,0:T(8,128)(2,1)S(1)}, u32[]{:S(2)}, u32[]{:S(2)}) %collective-permute-start.13) | collective-permute-done | bytes 221216 | tf_op jit(solution)/shard_map/ppermute | solution.py:31
  92.8 0.5 slice.80
  94.0 1.2 slice.81
  95.8 3.3 %collective-permute-start.20 = (bf16[4,2,72,768]{3,2,1,0:T(8,128)(2,1)}, bf16[4,2,72,768]{3,2,1,0:T(8,128)(2,1)}, u32[]{:S(2)}, u32[]{:S(2)}) collective-permute-start(bf16[4,2,72,768]{3,2,1,0:T(8,128)(2,1)} %collective-permute-done.18.refs_11_), channel_id=1, source_target_pairs={{0,1},{1,0},{2,3},{3,2},{4,5},{5,4},{6,7},{7,6},{8,9},{9,8},{10,11... | collective-permute-start | bytes 2654216 | tf_op jit(solution)/shard_map/ppermute | solution.py:20
  99.1 4.3 %add_add_fusion = bf16[1536,1152]{1,0:T(8,128)(2,1)} fusion(bf16[1536,1152]{1,0:T(8,128)(2,1)} %all-gather.3.cloned.1.call-done, bf16[]{:T(256)} %bitcast.26, bf16[]{:T(256)} %bitcast.25), kind=kLoop, calls=%fused_computation | loop fusion | flops 3538944 | bytes 7077892 | tf_op jit(solution)/shard_map/add | solution.py:48
  103.4 2.8 %collective-permute-start.21 = (bf16[64,24,1152]{2,1,0:T(8,128)(2,1)}, bf16[64,24,1152]{2,1,0:T(8,128)(2,1)S(1)}, u32[]{:S(2)}, u32[]{:S(2)}) collective-permute-start(bf16[64,24,1152]{2,1,0:T(8,128)(2,1)} %bitcast.27.refs_0_), channel_id=1, source_target_pairs={{0,64},{1,193},{64,128},{65,1},{128,192},{129,65},{192,0},{193,129... | collective-permute-start | bytes 10616840 | tf_op jit(solution)/shard_map/ppermute | solution.py:40
  106.2 0.5 collective-permute-start.16
  106.7 1.4 copy.24
  108.1 0.7 copy.16
  108.9 0.6 dynamic_slice.29.length_ref
  109.5 0.7 pad_add_fusion.place
  110.1 0.5 collective-permute-done.17.refs_8_
  110.6 22.7 %spatial.1 = bf16[32,144,128]{2,1,0:T(8,128)(2,1)} custom-call(s32[4]{0:T(128)} %pad_add_fusion.place, s32[1]{0:T(128)} %dynamic_slice.29.length_ref, bf16[512,1152]{1,0:T(8,128)(2,1)} %bitcast.52, f32[6,1152]{1,0:T(8,128)} %bitcast.49, f32[72,4]{1,0:T(8,128)} %bitcast.47, bf16[4,2,72,384]{3,2,1,0:T(8,128)(2,1)} %copy-done.2, ...), custom_call_target="tpu_custom_call" | custom-call | flops 30000001024 | bytes 20000000 | tf_op jit(solution)/shard_map/spatial/pallas_call | solution.py:350
  133.3 1.2 slice.82
  135.2 9.7 %collective-permute-done.21 = bf16[64,24,1152]{2,1,0:T(8,128)(2,1)S(1)} collective-permute-done((bf16[64,24,1152]{2,1,0:T(8,128)(2,1)}, bf16[64,24,1152]{2,1,0:T(8,128)(2,1)S(1)}, u32[]{:S(2)}, u32[]{:S(2)}) %collective-permute-start.21) | collective-permute-done | bytes 3538976 | tf_op jit(solution)/shard_map/ppermute | solution.py:40
  144.9 1.7 copy-done.1
  146.7 2.3 %broadcast_add_fusion.refs_1_ = bf16[64,24,1152]{2,1,0:T(8,128)(2,1)S(1)} fusion(bf16[64,24,1152]{2,1,0:T(8,128)(2,1)} %copy-done.1, bf16[]{:T(256)} %bitcast.28), kind=kLoop, calls=%fused_computation.1 | loop fusion | flops 1769472 | bytes 7077890 | tf_op jit(solution)/shard_map/add | solution.py:48
  149.0 1.6 collective-permute-start.22
  150.6 1.3 constant_dynamic-slice_fusion.1
  151.9 2.4 %collective-permute-start.23 = (bf16[32,24,1152]{2,1,0:T(8,128)(2,1)}, bf16[32,24,1152]{2,1,0:T(8,128)(2,1)}, u32[]{:S(2)}, u32[]{:S(2)}) collective-permute-start(bf16[32,24,1152]{2,1,0:T(8,128)(2,1)} %constant_dynamic-slice_fusion.1), channel_id=1, source_target_pairs={{0,64},{1,193},{64,128},{65,1},{128,192},{129,65},{192,0},{193,129... | collective-permute-start | bytes 5308424 | tf_op jit(solution)/shard_map/ppermute | solution.py:40
  154.4 6.1 %all-to-all-start = ((bf16[32,144,128]{2,1,0:T(8,128)(2,1)}), bf16[32,144,128]{2,1,0:T(8,128)(2,1)}, u32[]{:S(2)}, u32[]{:S(2)}) async-start(bf16[32,144,128]{2,1,0:T(8,128)(2,1)} %spatial.1), calls=%async_computation | async-start | bytes 2359296 | tf_op jit(solution)/shard_map/all_to_all | solution.py:367
  160.4 13.7 %collective-permute-done.23.refs_3_ = bf16[32,24,1152]{2,1,0:T(8,128)(2,1)} collective-permute-done((bf16[32,24,1152]{2,1,0:T(8,128)(2,1)}, bf16[32,24,1152]{2,1,0:T(8,128)(2,1)}, u32[]{:S(2)}, u32[]{:S(2)}) %collective-permute-start.23) | collective-permute-done | bytes 1769504 | tf_op jit(solution)/shard_map/ppermute | solution.py:40
  174.1 2.8 %collective-permute-start.24 = (bf16[32,24,1152]{2,1,0:T(8,128)(2,1)}, bf16[32,24,1152]{2,1,0:T(8,128)(2,1)}, u32[]{:S(2)}, u32[]{:S(2)}) collective-permute-start(bf16[32,24,1152]{2,1,0:T(8,128)(2,1)} %collective-permute-done.23.refs_3_), channel_id=1, source_target_pairs={{0,1},{1,0},{2,3},{3,2},{4,5},{5,4},{6,7},{7,6},{8,9},{9,8},{10,11... | collective-permute-start | bytes 5308424 | tf_op jit(solution)/shard_map/ppermute | solution.py:20
  176.9 1.8 copy.15
  178.8 0.8 and_convert_fusion.allowed
  179.6 11.7 %all-to-all-done.received = bf16[32,144,128]{2,1,0:T(8,128)(2,1)} async-done(((bf16[32,144,128]{2,1,0:T(8,128)(2,1)}), bf16[32,144,128]{2,1,0:T(8,128)(2,1)}, u32[]{:S(2)}, u32[]{:S(2)}) %all-to-all-start) | async-done | bytes 1179680 | tf_op jit(solution)/shard_map/all_to_all | solution.py:367
  191.4 25.4 %temporal.1 = f32[16,512]{1,0:T(8,128)} custom-call(s32[4]{0:T(128)} %pad_add_fusion.place, bf16[32,144,128]{2,1,0:T(8,128)(2,1)} %all-to-all-done.received, f32[1152,6]{1,0:T(8,128)} %bitcast.40, f32[72,4]{1,0:T(8,128)} %bitcast.48, f32[256,256]{1,0:T(8,128)} %and_convert_fusion.allowed, bf16[16,1152]{1,0:T(8,128)(2,1)} %bitcast.53, ...), custom_call_target="tpu_custom_call" | custom-call | flops 30000001024 | bytes 20000000 | tf_op jit(solution)/shard_map/temporal/pallas_call | solution.py:368
  216.7 0.7 constant_dynamic-slice_fusion
  217.5 1.1 collective-permute-done.25
  218.6 0.7 multiply_add_fusion
  219.5 0.7 fusion.1
  (63 shorter events, 1.4 us)
Async XLA Ops:
  6.5 92.6 %all-gather.3.cloned.1.call-start = ((), (), s32[]{:S(2)}) async-start(), calls=%async_computation.1 | async-start | bytes 3594240 | tf_op jit(solution)/shard_map/all_gather | solution.py:340
  9.1 4.4 %collective-permute-start = (bf16[72,1152]{1,0:T(8,128)(2,1)S(1)}, bf16[72,1152]{1,0:T(8,128)(2,1)S(1)}, u32[]{:S(2)}, u32[]{:S(2)}) collective-permute-start(bf16[72,1152]{1,0:T(8,128)(2,1)S(1)} %pad_maximum_fusion.1), channel_id=1, source_target_pairs={{0,1},{1,0},{2,3},{3,2},{4,5},{5,4},{6,7},{7,6},{8,9},{9,8},{10,11... | collective-permute-start | bytes 497672 | tf_op jit(solution)/shard_map/ppermute | solution.py:20
  14.5 19.3 %collective-permute-start.7 = (bf16[2,72,768]{2,1,0:T(8,128)(2,1)S(1)}, bf16[2,72,768]{2,1,0:T(8,128)(2,1)S(1)}, u32[]{:S(2)}, u32[]{:S(2)}) collective-permute-start(bf16[2,72,768]{2,1,0:T(8,128)(2,1)S(1)} %get-tuple-element.6), channel_id=1, source_target_pairs={{0,6},{1,11},{2,8},{3,13},{4,10},{5,15},{6,12},{7,1},{8,14},{9,3},... | collective-permute-start | bytes 663560 | tf_op jit(solution)/shard_map/ppermute | solution.py:31
  19.3 15.2 %collective-permute-start.6 = (bf16[2,72,768]{2,1,0:T(8,128)(2,1)S(1)}, bf16[2,72,768]{2,1,0:T(8,128)(2,1)S(1)}, u32[]{:S(2)}, u32[]{:S(2)}) collective-permute-start(bf16[2,72,768]{2,1,0:T(8,128)(2,1)S(1)} %get-tuple-element.6), channel_id=1, source_target_pairs={{0,4},{1,13},{2,6},{3,15},{4,8},{5,1},{6,10},{7,3},{8,12},{9,5},{1... | collective-permute-start | bytes 663560 | tf_op jit(solution)/shard_map/ppermute | solution.py:31
  19.6 20.1 %collective-permute-start.5 = (bf16[2,72,768]{2,1,0:T(8,128)(2,1)S(1)}, bf16[2,72,768]{2,1,0:T(8,128)(2,1)S(1)}, u32[]{:S(2)}, u32[]{:S(2)}) collective-permute-start(bf16[2,72,768]{2,1,0:T(8,128)(2,1)S(1)} %get-tuple-element.6), channel_id=1, source_target_pairs={{0,2},{1,15},{2,4},{3,1},{4,6},{5,3},{6,8},{7,5},{8,10},{9,7},{10,... | collective-permute-start | bytes 663560 | tf_op jit(solution)/shard_map/ppermute | solution.py:31
  20.1 7.2 %collective-permute-start.1 = (bf16[2,72,384]{2,1,0:T(8,128)(2,1)S(1)}, bf16[2,72,384]{2,1,0:T(8,128)(2,1)S(1)}, u32[]{:S(2)}, u32[]{:S(2)}) collective-permute-start(bf16[2,72,384]{2,1,0:T(8,128)(2,1)S(1)} %pad_maximum_fusion.2), channel_id=1, source_target_pairs={{0,16},{1,49},{2,18},{3,51},{4,20},{5,53},{6,22},{7,55},{8,24},{9,... | collective-permute-start | bytes 331784 | tf_op jit(solution)/shard_map/ppermute | solution.py:31
  22.7 11.1 %collective-permute-start.3 = (bf16[1,72,768]{2,1,0:T(8,128)(2,1)S(1)}, bf16[1,72,768]{2,1,0:T(8,128)(2,1)S(1)}, u32[]{:S(2)}, u32[]{:S(2)}) collective-permute-start(bf16[1,72,768]{2,1,0:T(8,128)(2,1)S(1)} %fusion), channel_id=1, source_target_pairs={{0,8},{1,9},{2,10},{3,11},{4,12},{5,13},{6,14},{7,15},{8,0},{9,1},... | collective-permute-start | bytes 331784 | tf_op jit(solution)/shard_map/ppermute | solution.py:31
  39.8 6.0 %collective-permute-start.8 = (bf16[7,72,768]{2,1,0:T(8,128)(2,1)S(1)}, bf16[7,72,768]{2,1,0:T(8,128)(2,1)S(1)}, u32[]{:S(2)}, u32[]{:S(2)}) collective-permute-start(bf16[7,72,768]{2,1,0:T(8,128)(2,1)S(1)} %maximum_add_fusion), channel_id=1, source_target_pairs={{0,1},{1,0},{2,3},{3,2},{4,5},{5,4},{6,7},{7,6},{8,9},{9,8},{10,11... | collective-permute-start | bytes 2322440 | tf_op jit(solution)/shard_map/ppermute | solution.py:20
  42.9 6.2 %collective-permute-start.2 = (bf16[1,72,384]{2,1,0:T(8,128)(2,1)S(1)}, bf16[1,72,384]{2,1,0:T(8,128)(2,1)S(1)}, u32[]{:S(2)}, u32[]{:S(2)}) collective-permute-start(bf16[1,72,384]{2,1,0:T(8,128)(2,1)S(1)} %fusion.2), channel_id=1, source_target_pairs={{0,32},{1,33},{2,34},{3,35},{4,36},{5,37},{6,38},{7,39},{8,40},{9,... | collective-permute-start | bytes 165896 | tf_op jit(solution)/shard_map/ppermute | solution.py:31
  46.3 15.9 %copy-start.5 = (bf16[16,72,768]{2,1,0:T(8,128)(2,1)}, bf16[16,72,768]{2,1,0:T(8,128)(2,1)S(1)}, u32[]{:S(2)}) copy-start(bf16[16,72,768]{2,1,0:T(8,128)(2,1)S(1)} %select_dynamic-update-slice_fusion.2) | copy-start | bytes 5308420
  46.3 24.2 %collective-permute-start.11 = (bf16[8,2,72,768]{3,2,1,0:T(8,128)(2,1)S(1)}, bf16[8,2,72,768]{3,2,1,0:T(8,128)(2,1)}, u32[]{:S(2)}, u32[]{:S(2)}) collective-permute-start(bf16[8,2,72,768]{3,2,1,0:T(8,128)(2,1)S(1)} %bitcast.50), channel_id=1, source_target_pairs={{0,16},{1,49},{2,18},{3,51},{4,20},{5,53},{6,22},{7,55},{8,24},{9,... | collective-permute-start | bytes 5308424 | tf_op jit(solution)/shard_map/ppermute | solution.py:31
  49.1 1.5 collective-permute-start.4
  52.1 0.8 copy-start.2
  52.9 7.6 %collective-permute-start.9 = (bf16[4,2,72,384]{3,2,1,0:T(8,128)(2,1)S(1)}, bf16[4,2,72,384]{3,2,1,0:T(8,128)(2,1)}, u32[]{:S(2)}, u32[]{:S(2)}) collective-permute-start(bf16[4,2,72,384]{3,2,1,0:T(8,128)(2,1)S(1)} %maximum_add_fusion.1.refs_0_), channel_id=1, source_target_pairs={{0,2},{1,15},{2,4},{3,1},{4,6},{5,3},{6,8},{7,5},{8,10},{9,7},{10,... | collective-permute-start | bytes 1327112 | tf_op jit(solution)/shard_map/ppermute | solution.py:31
  60.4 16.5 %collective-permute-start.10 = (bf16[4,2,72,384]{3,2,1,0:T(8,128)(2,1)}, bf16[4,2,72,384]{3,2,1,0:T(8,128)(2,1)S(1)}, u32[]{:S(2)}, u32[]{:S(2)}) collective-permute-start(bf16[4,2,72,384]{3,2,1,0:T(8,128)(2,1)} %collective-permute-done.9.refs_1_), channel_id=1, source_target_pairs={{0,2},{1,15},{2,4},{3,1},{4,6},{5,3},{6,8},{7,5},{8,10},{9,7},{10,... | collective-permute-start | bytes 1327112 | tf_op jit(solution)/shard_map/ppermute | solution.py:31
  71.8 22.2 %collective-permute-start.18 = (bf16[4,2,72,768]{3,2,1,0:T(8,128)(2,1)S(1)}, bf16[4,2,72,768]{3,2,1,0:T(8,128)(2,1)}, u32[]{:S(2)}, u32[]{:S(2)}) collective-permute-start(bf16[4,2,72,768]{3,2,1,0:T(8,128)(2,1)S(1)} %constant_dynamic-slice_fusion.2), channel_id=1, source_target_pairs={{0,16},{1,49},{2,18},{3,51},{4,20},{5,53},{6,22},{7,55},{8,24},{9,... | collective-permute-start | bytes 2654216 | tf_op jit(solution)/shard_map/ppermute | solution.py:31
  76.9 26.5 %copy-start.3 = (bf16[4,2,72,384]{3,2,1,0:T(8,128)(2,1)}, bf16[4,2,72,384]{3,2,1,0:T(8,128)(2,1)S(1)}, u32[]{:S(2)}) copy-start(bf16[4,2,72,384]{3,2,1,0:T(8,128)(2,1)S(1)} %collective-permute-done.10.refs_2_) | copy-start | bytes 1327108
  77.0 10.3 %collective-permute-start.12 = (bf16[4,2,72,384]{3,2,1,0:T(8,128)(2,1)S(1)}, bf16[4,2,72,384]{3,2,1,0:T(8,128)(2,1)S(1)}, u32[]{:S(2)}, u32[]{:S(2)}) collective-permute-start(bf16[4,2,72,384]{3,2,1,0:T(8,128)(2,1)S(1)} %broadcast_add_fusion.1), channel_id=1, source_target_pairs={{0,2},{1,15},{2,4},{3,1},{4,6},{5,3},{6,8},{7,5},{8,10},{9,7},{10,... | collective-permute-start | bytes 1327112 | tf_op jit(solution)/shard_map/ppermute | solution.py:31
  87.3 16.1 %copy-start.4 = (bf16[4,2,72,384]{3,2,1,0:T(8,128)(2,1)}, bf16[4,2,72,384]{3,2,1,0:T(8,128)(2,1)S(1)}, u32[]{:S(2)}) copy-start(bf16[4,2,72,384]{3,2,1,0:T(8,128)(2,1)S(1)} %collective-permute-done.12.refs_3_) | copy-start | bytes 1327108
  87.3 5.5 %collective-permute-start.13 = (bf16[2,2,72,384]{3,2,1,0:T(8,128)(2,1)S(1)}, bf16[2,2,72,384]{3,2,1,0:T(8,128)(2,1)S(1)}, u32[]{:S(2)}, u32[]{:S(2)}) collective-permute-start(bf16[2,2,72,384]{3,2,1,0:T(8,128)(2,1)S(1)} %constant_dynamic-slice_fusion.3), channel_id=1, source_target_pairs={{0,2},{1,15},{2,4},{3,1},{4,6},{5,3},{6,8},{7,5},{8,10},{9,7},{10,... | collective-permute-start | bytes 663560 | tf_op jit(solution)/shard_map/ppermute | solution.py:31
  88.5 17.7 %collective-permute-start.14 = (bf16[4,2,72,384]{3,2,1,0:T(8,128)(2,1)}, bf16[4,2,72,384]{3,2,1,0:T(8,128)(2,1)}, u32[]{:S(2)}, u32[]{:S(2)}) collective-permute-start(bf16[4,2,72,384]{3,2,1,0:T(8,128)(2,1)} %collective-permute-done.9.refs_1_), channel_id=1, source_target_pairs={{0,1},{1,0},{2,3},{3,2},{4,5},{5,4},{6,7},{7,6},{8,9},{9,8},{10,11... | collective-permute-start | bytes 1327112 | tf_op jit(solution)/shard_map/ppermute | solution.py:20
  89.2 21.4 %collective-permute-start.19 = (bf16[8,2,72,768]{3,2,1,0:T(8,128)(2,1)}, bf16[8,2,72,768]{3,2,1,0:T(8,128)(2,1)}, u32[]{:S(2)}, u32[]{:S(2)}) collective-permute-start(bf16[8,2,72,768]{3,2,1,0:T(8,128)(2,1)} %collective-permute-done.11.refs_10_), channel_id=1, source_target_pairs={{0,1},{1,0},{2,3},{3,2},{4,5},{5,4},{6,7},{7,6},{8,9},{9,8},{10,11... | collective-permute-start | bytes 5308424 | tf_op jit(solution)/shard_map/ppermute | solution.py:20
  92.8 10.6 %copy-start.8 = (bf16[2,2,72,384]{3,2,1,0:T(8,128)(2,1)}, bf16[2,2,72,384]{3,2,1,0:T(8,128)(2,1)S(1)}, u32[]{:S(2)}) copy-start(bf16[2,2,72,384]{3,2,1,0:T(8,128)(2,1)S(1)} %collective-permute-done.13.refs_4_) | copy-start | bytes 663556
  95.8 14.8 %collective-permute-start.20 = (bf16[4,2,72,768]{3,2,1,0:T(8,128)(2,1)}, bf16[4,2,72,768]{3,2,1,0:T(8,128)(2,1)}, u32[]{:S(2)}, u32[]{:S(2)}) collective-permute-start(bf16[4,2,72,768]{3,2,1,0:T(8,128)(2,1)} %collective-permute-done.18.refs_11_), channel_id=1, source_target_pairs={{0,1},{1,0},{2,3},{3,2},{4,5},{5,4},{6,7},{7,6},{8,9},{9,8},{10,11... | collective-permute-start | bytes 2654216 | tf_op jit(solution)/shard_map/ppermute | solution.py:20
  99.1 8.9 %copy-start.6 = (f32[4,72]{1,0:T(4,128)S(1)}, f32[4,72]{1,0:T(4,128)}, u32[]{:S(2)}) copy-start(f32[4,72]{1,0:T(4,128)} %param.17) | copy-start | bytes 3460
  99.1 9.7 %copy-start.7 = (s32[32]{0:T(128)S(1)}, s32[32]{0:T(128)}, u32[]{:S(2)}) copy-start(s32[32]{0:T(128)} %param.19) | copy-start | bytes 388
  99.1 9.7 %copy-start.9 = (s32[8]{0:T(128)S(1)}, s32[8]{0:T(128)}, u32[]{:S(2)}) copy-start(s32[8]{0:T(128)} %param.18) | copy-start | bytes 100
  103.4 41.5 %collective-permute-start.21 = (bf16[64,24,1152]{2,1,0:T(8,128)(2,1)}, bf16[64,24,1152]{2,1,0:T(8,128)(2,1)S(1)}, u32[]{:S(2)}, u32[]{:S(2)}) collective-permute-start(bf16[64,24,1152]{2,1,0:T(8,128)(2,1)} %bitcast.27.refs_0_), channel_id=1, source_target_pairs={{0,64},{1,193},{64,128},{65,1},{128,192},{129,65},{192,0},{193,129... | collective-permute-start | bytes 10616840 | tf_op jit(solution)/shard_map/ppermute | solution.py:40
  106.2 2.6 %collective-permute-start.15 = (bf16[4,2,72,384]{3,2,1,0:T(8,128)(2,1)}, bf16[4,2,72,384]{3,2,1,0:T(8,128)(2,1)}, u32[]{:S(2)}, u32[]{:S(2)}) collective-permute-start(bf16[4,2,72,384]{3,2,1,0:T(8,128)(2,1)} %copy-done.3), channel_id=1, source_target_pairs={{0,1},{1,0},{2,3},{3,2},{4,5},{5,4},{6,7},{7,6},{8,9},{9,8},{10,11... | collective-permute-start | bytes 1327112 | tf_op jit(solution)/shard_map/ppermute | solution.py:20
  106.2 4.0 %collective-permute-start.16 = (bf16[4,2,72,384]{3,2,1,0:T(8,128)(2,1)}, bf16[4,2,72,384]{3,2,1,0:T(8,128)(2,1)}, u32[]{:S(2)}, u32[]{:S(2)}) collective-permute-start(bf16[4,2,72,384]{3,2,1,0:T(8,128)(2,1)} %copy-done.4), channel_id=1, source_target_pairs={{0,1},{1,0},{2,3},{3,2},{4,5},{5,4},{6,7},{7,6},{8,9},{9,8},{10,11... | collective-permute-start | bytes 1327112 | tf_op jit(solution)/shard_map/ppermute | solution.py:20
  108.8 1.8 collective-permute-start.17
  144.9 1.7 copy-start.1
  149.0 3.0 %copy-start = (bf16[64,24,1152]{2,1,0:T(8,128)(2,1)}, bf16[64,24,1152]{2,1,0:T(8,128)(2,1)S(1)}, u32[]{:S(2)}) copy-start(bf16[64,24,1152]{2,1,0:T(8,128)(2,1)S(1)} %broadcast_add_fusion.refs_1_) | copy-start | bytes 10616836
  149.0 42.4 %collective-permute-start.22 = (bf16[64,24,1152]{2,1,0:T(8,128)(2,1)S(1)}, bf16[64,24,1152]{2,1,0:T(8,128)(2,1)}, u32[]{:S(2)}, u32[]{:S(2)}) collective-permute-start(bf16[64,24,1152]{2,1,0:T(8,128)(2,1)S(1)} %broadcast_add_fusion.refs_1_), channel_id=1, source_target_pairs={{0,1},{1,0},{2,3},{3,2},{4,5},{5,4},{6,7},{7,6},{8,9},{9,8},{10,11... | collective-permute-start | bytes 10616840 | tf_op jit(solution)/shard_map/ppermute | solution.py:20
  151.9 22.2 %collective-permute-start.23 = (bf16[32,24,1152]{2,1,0:T(8,128)(2,1)}, bf16[32,24,1152]{2,1,0:T(8,128)(2,1)}, u32[]{:S(2)}, u32[]{:S(2)}) collective-permute-start(bf16[32,24,1152]{2,1,0:T(8,128)(2,1)} %constant_dynamic-slice_fusion.1), channel_id=1, source_target_pairs={{0,64},{1,193},{64,128},{65,1},{128,192},{129,65},{192,0},{193,129... | collective-permute-start | bytes 5308424 | tf_op jit(solution)/shard_map/ppermute | solution.py:40
  154.4 37.0 %all-to-all-start = ((bf16[32,144,128]{2,1,0:T(8,128)(2,1)}), bf16[32,144,128]{2,1,0:T(8,128)(2,1)}, u32[]{:S(2)}, u32[]{:S(2)}) async-start(bf16[32,144,128]{2,1,0:T(8,128)(2,1)} %spatial.1), calls=%async_computation | async-start | bytes 2359296 | tf_op jit(solution)/shard_map/all_to_all | solution.py:367
  174.1 17.2 %collective-permute-start.24 = (bf16[32,24,1152]{2,1,0:T(8,128)(2,1)}, bf16[32,24,1152]{2,1,0:T(8,128)(2,1)}, u32[]{:S(2)}, u32[]{:S(2)}) collective-permute-start(bf16[32,24,1152]{2,1,0:T(8,128)(2,1)} %collective-permute-done.23.refs_3_), channel_id=1, source_target_pairs={{0,1},{1,0},{2,3},{3,2},{4,5},{5,4},{6,7},{7,6},{8,9},{9,8},{10,11... | collective-permute-start | bytes 5308424 | tf_op jit(solution)/shard_map/ppermute | solution.py:20
  217.5 1.2 collective-permute-start.25
Sparse Core Ops, SparseCore 0:
  10.1 84.3 all-gather.2

commit v3 on v2

--- a/solution.py
+++ b/solution.py
@@ -12,7 +12,7 @@
 F32 = jnp.float32
 LANES = 128
 TEMPORAL_ROWS = 256
-X_RING, Z_RING, SPLIT = 4, 8, 384
+X_RING, Z_RING, SPLIT = 4, 8, 512
 X_SLOTS = (0, -1, 1, 2)
 Z_SLOTS = (0, -1, -2, -3, 1, 2, 3, 4)
 
@@ -31,21 +31,8 @@
     return lax.ppermute(array, ("seq", "cfg"), pairs)
 
 
-def replica_step(array):
-    size = lax.axis_size("rep")
-    pairs = []
-    for y in range(size):
-        for core in range(2):
-            pairs.append((2 * y + core, 2 * ((y + 1 - 2 * core) % size) + core))
-    return lax.ppermute(array, ("rep", "cfg"), pairs)
-
-
 def in_core_order(core, first, second):
     return jnp.where(core == 0, first, second), jnp.where(core == 0, second, first)
-
-
-def after(array, earlier):
-    return array + earlier[(0,) * earlier.ndim] * jnp.zeros((), array.dtype)
 
 
 def spread_in_plane(own, core):
@@ -58,23 +45,19 @@
     near = [plane_step(second, False, far) for far in (1, 2, 3)]
     near.append(plane_step(own_half(second), False, 4))
     mine = jnp.concatenate([plane_step(first, True), plane_step(own_half(first), True, 2)])
-    started = mine
-    mine = after(mine, near[3])
     theirs = swap_cores(mine)
     low, high = in_core_order(core, mine[:2], theirs[:2])
     opposite = jnp.concatenate(in_core_order(core, mine[2:], theirs[2:]))
-    row = [first, low, high, opposite]
-    mine = after(jnp.concatenate(near), started)
+    rows = [jnp.stack([first, low, high, opposite])]
+    for _ in range(3):
+        rows.append(plane_step(rows[-1], False))
+    mine = jnp.concatenate(near)
     theirs = swap_cores(mine)
     low, high = in_core_order(core, mine[:6], theirs[:6])
     opposite = jnp.concatenate(in_core_order(core, mine[6:], theirs[6:]))
     ring = jnp.concatenate([second, low, high, opposite]).reshape((Z_RING,) + second.shape)
-    row = after(jnp.stack(row), theirs)
     across = plane_step(ring, True)
     beyond = plane_step(lax.dynamic_slice_in_dim(across, 4 * core, 4, 0), True)
-    rows = [row]
-    for hop in range(3):
-        rows.append(plane_step(after(rows[-1], across) if hop == 2 else rows[-1], False))
     rows.append(plane_step(lax.dynamic_slice_in_dim(rows[3], 2 * core, 2, 0), False))
     rows += [swap_cores(part) for part in rows[1:]]
     return rows, [ring, across, beyond, swap_cores(across), swap_cores(beyond)]
@@ -87,8 +70,9 @@
     return found
 
 
-def plane_copies(place, rows, rings, landing, sem):
-    x, z, core = place[0], place[1], place[2]
+def plane_copies(rows, rings, landing, sem):
+    position, core = lax.axis_index("seq"), lax.axis_index("cfg")
+    x, z = position // Z_RING, position % Z_RING
     sign = 1 - 2 * core
     rest = landing.shape[2] - SPLIT
     copies = []
@@ -110,26 +94,6 @@
     return copies
 
 
-def replica_copies(place, parts, landing, sem):
-    core, y = place[2], place[3]
-    size = landing.shape[0]
-    sign = 1 - 2 * core
-    held, mine, theirs, mine_far, theirs_far = parts
-    far = mine_far.shape[0]
-
-    def to(part, dy, start=None):
-        slot = landing.at[lax.rem(y + dy + size, size)]
-        return pltpu.make_async_copy(part, slot if start is None else slot.at[pl.ds(start, far)], sem)
-
-    return [
-        to(held, 0),
-        to(mine, -sign),
-        to(theirs, sign),
-        to(mine_far, 2, far * core),
-        to(theirs_far, 2, far - far * core),
-    ]
-
-
 def dot_over(left, right, left_dim, right_dim):
     return lax.dot_general(
         left, right, (((left_dim,), (right_dim,)), ((), ())), preferred_element_type=F32
@@ -143,33 +107,15 @@
     return centred * lax.rsqrt(variance + 1e-06)
 
 
-def lay_out_weights(landing, columns, out_rows, head_size):
-    share = 3 * head_size // 4
+def lay_out(landing, target, first, count):
+    size = 8 * count
 
     def group(g, carry):
-        parts = [landing[8 * g + i] for i in range(8)]
-        for target, rows in (
-            (columns, [part[:share] for part in parts]),
-            (out_rows, [part[share:] for part in parts]),
-        ):
-            size = 8 * rows[0].shape[0]
-            target[pl.ds(pl.multiple_of(g * size, 16), size), :] = jnp.concatenate(rows, axis=0)
+        rows = [landing[8 * g + i][first : first + count] for i in range(8)]
+        target[pl.ds(pl.multiple_of(g * size, 16), size), :] = jnp.concatenate(rows, axis=0)
         return carry
 
     lax.fori_loop(0, landing.shape[0] // 8, group, 0)
-
-
-def lay_out_quarters(landing, columns, out_rows, head_size):
-    quarter = head_size // 4
-
-    def group(g, carry):
-        for target, kinds in ((columns, (0, 1, 2)), (out_rows, (3,))):
-            rows = [landing[kind, 8 * g + i][:quarter] for i in range(8) for kind in kinds]
-            size = quarter * len(rows)
-            target[pl.ds(pl.multiple_of(g * size, 16), size), :] = jnp.concatenate(rows, axis=0)
-        return carry
-
-    lax.fori_loop(0, landing.shape[1] // 8, group, 0)
 
 
 def project(columns, normed, projected):
@@ -227,27 +173,36 @@
     lax.fori_loop(0, width // (2 * head_size), pair, 0)
 
 
-def spatial_kernel(head_size, place, length_ref, tokens, levels, gains, *refs):
+def spatial_kernel(head_size, clip_tokens, block_clip, tokens, levels, gains, *refs):
     rows, rings = refs[:9], refs[9:14]
-    residual, landing, columns, out_rows, normed, projected, attended, sem = refs[14:]
-    arriving = plane_copies(place, rows, rings, landing, sem)
+    attended, landing, columns, normed, projected, sem = refs[14:]
+    arriving = plane_copies(rows, rings, landing, sem)
     for copy in arriving:
         copy.start()
-    row_count, width = tokens.shape
+    row_count = tokens.shape[0]
     for start in range(0, row_count, LANES):
         chunk = slice(start, start + LANES)
-        values_in = layer_norm(tokens[chunk, :].astype(F32), 1) * (1.0 + levels[1:2, :]) + levels[0:1, :]
+        values_in = layer_norm(tokens[chunk, :].astype(F32), 1) * (1.0 + levels[1]) + levels[0]
         normed[:, chunk] = values_in.astype(BF16).T
     for copy in arriving:
         copy.wait()
-    lay_out_weights(landing, columns, out_rows, head_size)
+    lay_out(landing, columns, 0, 3 * head_size // 4)
     project(columns, normed, projected)
-    inside = lax.broadcasted_iota(jnp.int32, (head_size + 8, row_count), 1) < length_ref[0]
+    length = clip_tokens[block_clip[lax.axis_index("seq")]]
+    inside = lax.broadcasted_iota(jnp.int32, (head_size + 8, row_count), 1) < length
     attend(projected, attended, gains, 0, inside, None, head_size)
-    for start in range(0, row_count, 256):
+
+
+def mixing_kernel(head_size, tokens, levels, attended, gathered, residual, landing, out_rows, sem):
+    first, kept = landing.shape[1] * 2, landing.shape[1]
+    arriving = pltpu.make_async_copy(gathered.at[:, pl.ds(first, kept), :], landing, sem)
+    arriving.start()
+    arriving.wait()
+    lay_out(landing, out_rows, head_size - first, head_size // 4)
+    for start in range(0, tokens.shape[0], 256):
         chunk = slice(start, start + 256)
         projection = dot_over(attended[:, chunk], out_rows[...], 0, 1)
-        updated = (tokens[chunk, :].astype(F32) + levels[2:3, :] * projection).astype(BF16)
+        updated = (tokens[chunk, :].astype(F32) + levels[2] * projection).astype(BF16)
         for d in range(16):
             for j in range(residual.shape[1] // 16):
                 residual[start // 16 + d, 16 * j : 16 * j + 16, :] = updated[
@@ -255,11 +210,10 @@
                 ]
 
 
-def temporal_kernel(head_size, place, received, levels, gains, allowed, w_final, *refs):
-    predicted, landing, columns, out_rows, normed, projected, attended, by_frame, by_slot, sem = refs[5:]
-    arriving = replica_copies(place, refs[:5], landing, sem)
-    for copy in arriving:
-        copy.start()
+def temporal_kernel(head_size, received, levels, gains, allowed, w_final, gathered, predicted,
+                    landing, columns, normed, projected, out_rows, attended, by_frame, by_slot, sem):
+    arriving = pltpu.make_async_copy(gathered.at[:, pl.ds(0, landing.shape[1]), :], landing, sem)
+    arriving.start()
     frames = received.shape[0]
     width, row_count = normed.shape
     locations = row_count // frames
@@ -279,9 +233,10 @@
         chunk = slice(start, start + LANES)
         values_in = layer_norm(by_slot[:, chunk].astype(F32), 0)
         normed[:, chunk] = (values_in * (1.0 + levels[:, 4:5]) + levels[:, 3:4]).astype(BF16)
-    for copy in arriving:
-        copy.wait()
-    lay_out_quarters(landing, columns, out_rows, head_size)
+    arriving.wait()
+    share = 3 * head_size // 4
+    lay_out(landing, columns, 0, share)
+    lay_out(landing, out_rows, share, head_size // 4)
     project(columns, normed, projected)
     attend(projected, attended, gains, 2, None, allowed, head_size)
     projected[0:width, :] = jnp.dot(out_rows[...], attended[...], preferred_element_type=F32)
@@ -292,14 +247,12 @@
     predicted[...] = jnp.dot(w_final[...], normed[...], preferred_element_type=F32)
 
 
-def weight_scratch(landing_shape, rows, width):
+def projection_scratch(landing_shape, rows, width):
     return [
         pltpu.VMEM(landing_shape, BF16),
         pltpu.VMEM((3 * width, width), BF16),
-        pltpu.VMEM((width, width), BF16),
         pltpu.VMEM((width, rows), BF16),
         pltpu.VMEM((3 * width, rows), F32),
-        pltpu.VMEM((width, rows), BF16),
     ]
 
 
@@ -322,62 +275,69 @@
     locations = rows // seq
     position = lax.axis_index("seq")
     branch_index = lax.axis_index("cfg")
-    levels = modulation[0]
+    levels = modulation.transpose(1, 0, 2)
     member = block_clip[:, None] == jnp.arange(clip_tokens.shape[0], dtype=jnp.int32)[None, :]
     lengths = jnp.sum(jnp.where(member, clip_tokens[None, :], 0), axis=1)
-    own_length = lax.dynamic_slice_in_dim(lengths, position, 1)
     gains = norm_gains.T
     slot_of = jnp.arange(TEMPORAL_ROWS, dtype=jnp.int32) // frames
     clip_of = jnp.tile(block_clip, TEMPORAL_ROWS // frames)
     allowed = ((slot_of[:, None] == slot_of[None, :]) & (clip_of[:, None] == clip_of[None, :])).astype(F32)
 
-    y = lax.axis_index("rep")
-    place = jnp.stack([position // Z_RING, position % Z_RING, branch_index, y]).astype(jnp.int32)
-    later = jnp.concatenate([w_qkv_t.T, w_out_t.T], axis=0)
-    quarter_rows = later.shape[0] // lax.axis_size("rep")
-    own_quarter = lax.dynamic_slice_in_dim(later, y * quarter_rows, quarter_rows, 0)
-    own_quarter = jnp.pad(own_quarter, ((0, -quarter_rows % 8), (0, 0)))
-    quarter = lax.all_gather(own_quarter, ("seq", "cfg"), axis=0, tiled=False)
-    row_parts, ring_parts = spread_in_plane(jnp.concatenate([w_qkv_s.T, w_out_s.T], axis=0), branch_index)
-    shards = quarter.shape[0]
-    quarter = after(after(quarter, row_parts[4]), ring_parts[2])
+    first_rows = jnp.pad(w_qkv_s.T, ((0, -w_qkv_s.shape[1] % 8), (0, 0)))
+    later_rows = jnp.concatenate([w_qkv_t.T, w_out_t.T, w_out_s.T], axis=0)
+    later_rows = jnp.pad(later_rows, ((0, -later_rows.shape[0] % 32), (0, 0)))
+    gathered = lax.all_gather(later_rows, ("seq", "cfg"), axis=0, tiled=False)
+    shards = gathered.shape[0]
+    row_parts, ring_parts = spread_in_plane(first_rows, branch_index)
     params = pltpu.CompilerParams(vmem_limit_bytes=58 * 2**20)
     vmem = pl.BlockSpec(memory_space=pltpu.VMEM)
     smem = pl.BlockSpec(memory_space=pltpu.SMEM)
     anywhere = pl.BlockSpec(memory_space=pl.ANY)
     tile_rows = locations * width // LANES
-    cost = pl.CostEstimate(flops=30_000_000_000, bytes_accessed=20_000_000, transcendentals=0)
-    residual = pl.pallas_call(
+    cost = pl.CostEstimate(flops=20_000_000_000, bytes_accessed=20_000_000, transcendentals=0)
+    attended = pl.pallas_call(
         functools.partial(spatial_kernel, head_size),
-        out_shape=jax.ShapeDtypeStruct((seq, tile_rows, LANES), BF16),
+        out_shape=jax.ShapeDtypeStruct((width, rows), BF16),
         in_specs=[smem, smem, vmem, vmem, vmem] + [anywhere] * 14,
         out_specs=vmem,
-        scratch_shapes=weight_scratch((shards, later.shape[0], width), rows, width)
+        scratch_shapes=projection_scratch((shards,) + first_rows.shape, rows, width)
         + [pltpu.SemaphoreType.DMA],
         compiler_params=params,
         cost_estimate=cost,
         name="spatial",
-    )(place, own_length, tokens[0], levels, gains, *row_parts, *ring_parts)
-    next_quarter = replica_step(quarter)
-    next_quarter = after(next_quarter, residual)
-    far_quarter = replica_step(
-        lax.dynamic_slice_in_dim(next_quarter, branch_index * (shards // 2), shards // 2, 0)
-    )
-    quarters = (quarter, next_quarter, swap_cores(next_quarter), far_quarter, swap_cores(far_quarter))
+    )(clip_tokens, block_clip, tokens[0], levels, gains, *row_parts, *ring_parts)
+    residual = pl.pallas_call(
+        functools.partial(mixing_kernel, head_size),
+        out_shape=jax.ShapeDtypeStruct((seq, tile_rows, LANES), BF16),
+        in_specs=[vmem, vmem, vmem, anywhere],
+        out_specs=vmem,
+        scratch_shapes=[
+            pltpu.VMEM((shards, 32, width), BF16),
+            pltpu.VMEM((width, width), BF16),
+            pltpu.SemaphoreType.DMA,
+        ],
+        compiler_params=params,
+        cost_estimate=cost,
+        name="mixing",
+    )(tokens[0], levels, attended, gathered)
     received = lax.all_to_all(residual, "seq", split_axis=0, concat_axis=0, tiled=True)
     predicted = pl.pallas_call(
         functools.partial(temporal_kernel, head_size),
         out_shape=jax.ShapeDtypeStruct((w_final.shape[1], rows), F32),
-        in_specs=[smem, vmem, vmem, vmem, vmem, vmem] + [anywhere] * 5,
+        in_specs=[vmem] * 5 + [anywhere],
         out_specs=vmem,
-        scratch_shapes=weight_scratch(
-            (lax.axis_size("rep"), shards, quarter.shape[1], width), rows, width
-        )
-        + [pltpu.VMEM((rows, width), BF16), pltpu.VMEM((width, rows), BF16), pltpu.SemaphoreType.DMA],
+        scratch_shapes=projection_scratch((shards, 80, width), rows, width)
+        + [
+            pltpu.VMEM((width, width), BF16),
+            pltpu.VMEM((width, rows), BF16),
+            pltpu.VMEM((rows, width), BF16),
+            pltpu.VMEM((width, rows), BF16),
+            pltpu.SemaphoreType.DMA,
+        ],
         compiler_params=params,
         cost_estimate=cost,
         name="temporal",
-    )(place, received, levels.T, gains, allowed, w_final.T, *quarters)
+    )(received, modulation[0].T, gains, allowed, w_final.T, gathered)
 
     half = predicted.shape[0] // 2
     outgoing = lax.dynamic_slice_in_dim(predicted, (1 - branch_index) * half, half, 0)

time: 228 us -> 199 us (0.87)
  waiting for transfers between devices: 79.6 us -> 63.5 us
  local copies, waits for them, and re-layouts: 17.1 us -> 5.57 us
  starting transfers between devices: 50.6 us -> 58.5 us
  other arithmetic: 13.4 us -> 5.72 us
  between operations: 18.2 us -> 13.7 us
  Pallas kernels: 48.1 us -> 50.9 us
    ppermute x2 -> x0, waiting for transfers between devices: 23.5 us -> none  [replica_step(): return lax.ppermute(array, ('rep', 'cfg'), pairs)]
    all_to_all x1, waiting for transfers between devices: 11.7 us -> 25 us  [body(): lax.all_to_all(residual, 'seq', split_axis=0, concat_axis=0, tiled=True)]
    pallas_call x0 -> x1, Pallas kernels: none -> 7.36 us  [body(): pl.pallas_call(functools.partial(mixing_kernel, head_size), out_shape=jax...]
    add x6 -> x0, other arithmetic: 6.86 us -> none  [after(): return array + earlier[(0,) * earlier.ndim] * jnp.zeros((), array.dtype)]
    ppermute x12, waiting for transfers between devices: 40.4 us -> 34.4 us  [plane_step(): return lax.ppermute(array, ('seq', 'cfg'), pairs)]
    slice x7 -> x0, local copies, waits for them, and re-layouts: 5.86 us -> none  [after(): return array + earlier[(0,) * earlier.ndim] * jnp.zeros((), array.dtype)]
    ppermute x2 -> x0, starting transfers between devices: 5.19 us -> none  [replica_step(): return lax.ppermute(array, ('rep', 'cfg'), pairs)]
    ppermute x1, starting transfers between devices: 0.01 us -> 4.93 us  [body(): other = lax.ppermute(outgoing, 'cfg', [(0, 1), (1, 0)])]
  transfers between devices with their start and end apart: 28 -> 24, of which waited for: 14 -> 12; matrix products, arithmetic and copies ran while one was open for 10% -> 3% of each run, Pallas kernels for 10% -> 10%
where the time goes in v3:
time: 199 us; the launch traced here: 198 us
  waiting for transfers between devices  63.5 us (32%)
  starting transfers between devices  58.5 us (29%)
  Pallas kernels  50.9 us (26%)
  between operations  13.7 us (7%)
  other arithmetic  5.72 us (3%)
  local copies, waits for them, and re-layouts  5.57 us (3%)
    ppermute x12, waiting for transfers between devices, plane_step(): return lax.ppermute(array, ('seq', 'cfg'), pairs)  34.4 us
    ppermute x12, starting transfers between devices, plane_step(): return lax.ppermute(array, ('seq', 'cfg'), pairs)  28.6 us
    all_to_all x1, waiting for transfers between devices, body(): lax.all_to_all(residual, 'seq', split_axis=0, concat_axis=0, tiled=True)  25 us
    pallas_call x1, Pallas kernels, body(): pl.pallas_call(functools.partial(temporal_kernel, head_size), out_shape=j...  24.3 us
    ppermute x9, starting transfers between devices, swap_cores(): return lax.ppermute(array, 'cfg', [(0, 1), (1, 0)])  20.1 us
    pallas_call x1, Pallas kernels, body(): pl.pallas_call(functools.partial(spatial_kernel, head_size), out_shape=ja...  19.3 us
    pallas_call x1, Pallas kernels, body(): pl.pallas_call(functools.partial(mixing_kernel, head_size), out_shape=jax...  7.36 us
    ppermute x1, starting transfers between devices, body(): other = lax.ppermute(outgoing, 'cfg', [(0, 1), (1, 0)])  4.93 us
  transfers between devices with their start and end apart: 24, of which 12 were waited for; matrix products, arithmetic and copies ran while one was open for 3% of the time, Pallas kernels for 10%

profile of v3, /device:TPU:1, one launch (start us, length us, event | category | flops | bytes accessed | tf_op | source)
XLA Modules:
  0.0 197.8 jit_solution(16012701155210506240)
XLA Ops:
  6.5 1.7 fusion.4
  8.2 0.0 all-gather.3.cloned.1.call-update
  8.3 0.9 pad.8
  9.2 3.3 %collective-permute-start = (bf16[56,1152]{1,0:T(8,128)(2,1)S(1)}, bf16[56,1152]{1,0:T(8,128)(2,1)S(1)}, u32[]{:S(2)}, u32[]{:S(2)}) collective-permute-start(bf16[56,1152]{1,0:T(8,128)(2,1)S(1)} %pad.8), channel_id=1, source_target_pairs={{0,1},{1,0},{2,3},{3,2},{4,5},{5,4},{6,7},{7,6},{8,9},{9,8},{10,11... | collective-permute-start | bytes 387080 | tf_op jit(solution)/shard_map/ppermute | solution.py:20
  12.5 1.0 collective-permute-done
  13.5 1.0 select_bitcast_fusion
  14.5 3.9 %collective-permute-start.12 = (bf16[2,56,640]{2,1,0:T(8,128)(2,1)S(1)}, bf16[2,56,640]{2,1,0:T(8,128)(2,1)S(1)}, u32[]{:S(2)}, u32[]{:S(2)}) collective-permute-start(bf16[2,56,640]{2,1,0:T(8,128)(2,1)S(1)} %get-tuple-element.6), channel_id=1, source_target_pairs={{0,2},{1,15},{2,4},{3,1},{4,6},{5,3},{6,8},{7,5},{8,10},{9,7},{10,... | collective-permute-start | bytes 430088 | tf_op jit(solution)/shard_map/ppermute | solution.py:31
  18.4 1.2 collective-permute-start.13
  19.6 0.4 collective-permute-start.14
  20.0 2.6 %collective-permute-start.1 = (bf16[2,56,512]{2,1,0:T(8,128)(2,1)S(1)}, bf16[2,56,512]{2,1,0:T(8,128)(2,1)S(1)}, u32[]{:S(2)}, u32[]{:S(2)}) collective-permute-start(bf16[2,56,512]{2,1,0:T(8,128)(2,1)S(1)} %pad_maximum_fusion.4), channel_id=1, source_target_pairs={{0,16},{1,49},{2,18},{3,51},{4,20},{5,53},{6,22},{7,55},{8,24},{9,... | collective-permute-start | bytes 344072 | tf_op jit(solution)/shard_map/ppermute | solution.py:31
  22.7 0.6 collective-permute-start.2
  23.3 4.3 %collective-permute-done.2 = bf16[1,56,512]{2,1,0:T(8,128)(2,1)S(1)} collective-permute-done((bf16[1,56,512]{2,1,0:T(8,128)(2,1)S(1)}, bf16[1,56,512]{2,1,0:T(8,128)(2,1)S(1)}, u32[]{:S(2)}, u32[]{:S(2)}) %collective-permute-start.2) | collective-permute-done | bytes 57376 | tf_op jit(solution)/shard_map/ppermute | solution.py:31
  27.6 4.5 %collective-permute-start.15 = (bf16[1,56,640]{2,1,0:T(8,128)(2,1)S(1)}, bf16[1,56,640]{2,1,0:T(8,128)(2,1)S(1)}, u32[]{:S(2)}, u32[]{:S(2)}) collective-permute-start(bf16[1,56,640]{2,1,0:T(8,128)(2,1)S(1)} %fusion.5), channel_id=1, source_target_pairs={{0,8},{1,9},{2,10},{3,11},{4,12},{5,13},{6,14},{7,15},{8,0},{9,1},... | collective-permute-start | bytes 215048 | tf_op jit(solution)/shard_map/ppermute | solution.py:31
  32.1 0.1 collective-permute-start.3
  32.2 4.2 %collective-permute-done.15 = bf16[1,56,640]{2,1,0:T(8,128)(2,1)S(1)} collective-permute-done((bf16[1,56,640]{2,1,0:T(8,128)(2,1)S(1)}, bf16[1,56,640]{2,1,0:T(8,128)(2,1)S(1)}, u32[]{:S(2)}, u32[]{:S(2)}) %collective-permute-start.15) | collective-permute-done | bytes 71712 | tf_op jit(solution)/shard_map/ppermute | solution.py:31
  36.4 0.1 pad_maximum_fusion
  36.5 2.5 %collective-permute-start.16 = (bf16[7,56,640]{2,1,0:T(8,128)(2,1)S(1)}, bf16[7,56,640]{2,1,0:T(8,128)(2,1)S(1)}, u32[]{:S(2)}, u32[]{:S(2)}) collective-permute-start(bf16[7,56,640]{2,1,0:T(8,128)(2,1)S(1)} %pad_maximum_fusion), channel_id=1, source_target_pairs={{0,1},{1,0},{2,3},{3,2},{4,5},{5,4},{6,7},{7,6},{8,9},{9,8},{10,11... | collective-permute-start | bytes 1505288 | tf_op jit(solution)/shard_map/ppermute | solution.py:20
  39.1 1.4 collective-permute-done.16
  40.5 0.1 select_dynamic-update-slice_fusion.1
  40.6 0.1 select_dynamic-update-slice_fusion
  40.8 1.3 collective-permute-start.17
  42.2 0.0 copy-start.6
  42.2 0.1 pad_maximum_fusion.1.refs_0_
  42.3 2.0 %collective-permute-start.4 = (bf16[4,2,56,512]{3,2,1,0:T(8,128)(2,1)S(1)}, bf16[4,2,56,512]{3,2,1,0:T(8,128)(2,1)}, u32[]{:S(2)}, u32[]{:S(2)}) collective-permute-start(bf16[4,2,56,512]{3,2,1,0:T(8,128)(2,1)S(1)} %pad_maximum_fusion.1.refs_0_), channel_id=1, source_target_pairs={{0,2},{1,15},{2,4},{3,1},{4,6},{5,3},{6,8},{7,5},{8,10},{9,7},{10,... | collective-permute-start | bytes 1376264 | tf_op jit(solution)/shard_map/ppermute | solution.py:31
  44.3 8.4 %collective-permute-done.4.refs_1_ = bf16[4,2,56,512]{3,2,1,0:T(8,128)(2,1)} collective-permute-done((bf16[4,2,56,512]{3,2,1,0:T(8,128)(2,1)S(1)}, bf16[4,2,56,512]{3,2,1,0:T(8,128)(2,1)}, u32[]{:S(2)}, u32[]{:S(2)}) %collective-permute-start.4) | collective-permute-done | bytes 458784 | tf_op jit(solution)/shard_map/ppermute | solution.py:31
  52.7 3.1 %collective-permute-start.5 = (bf16[4,2,56,512]{3,2,1,0:T(8,128)(2,1)}, bf16[4,2,56,512]{3,2,1,0:T(8,128)(2,1)}, u32[]{:S(2)}, u32[]{:S(2)}) collective-permute-start(bf16[4,2,56,512]{3,2,1,0:T(8,128)(2,1)} %collective-permute-done.4.refs_1_), channel_id=1, source_target_pairs={{0,2},{1,15},{2,4},{3,1},{4,6},{5,3},{6,8},{7,5},{8,10},{9,7},{10,... | collective-permute-start | bytes 1376264 | tf_op jit(solution)/shard_map/ppermute | solution.py:31
  55.8 0.2 collective-permute-done.17.refs_10_
  56.0 0.1 constant_dynamic-slice_fusion.1
  56.1 2.4 %collective-permute-start.18 = (bf16[4,2,56,640]{3,2,1,0:T(8,128)(2,1)S(1)}, bf16[4,2,56,640]{3,2,1,0:T(8,128)(2,1)S(1)}, u32[]{:S(2)}, u32[]{:S(2)}) collective-permute-start(bf16[4,2,56,640]{3,2,1,0:T(8,128)(2,1)S(1)} %constant_dynamic-slice_fusion.1), channel_id=1, source_target_pairs={{0,16},{1,49},{2,18},{3,51},{4,20},{5,53},{6,22},{7,55},{8,24},{9,... | collective-permute-start | bytes 1720328 | tf_op jit(solution)/shard_map/ppermute | solution.py:31
  58.5 0.4 collective-permute-start.19
  58.9 2.6 %collective-permute-done.5.refs_2_ = bf16[4,2,56,512]{3,2,1,0:T(8,128)(2,1)} collective-permute-done((bf16[4,2,56,512]{3,2,1,0:T(8,128)(2,1)}, bf16[4,2,56,512]{3,2,1,0:T(8,128)(2,1)}, u32[]{:S(2)}, u32[]{:S(2)}) %collective-permute-start.5) | collective-permute-done | bytes 458784 | tf_op jit(solution)/shard_map/ppermute | solution.py:31
  61.5 3.1 %collective-permute-start.6 = (bf16[4,2,56,512]{3,2,1,0:T(8,128)(2,1)}, bf16[4,2,56,512]{3,2,1,0:T(8,128)(2,1)S(1)}, u32[]{:S(2)}, u32[]{:S(2)}) collective-permute-start(bf16[4,2,56,512]{3,2,1,0:T(8,128)(2,1)} %collective-permute-done.5.refs_2_), channel_id=1, source_target_pairs={{0,2},{1,15},{2,4},{3,1},{4,6},{5,3},{6,8},{7,5},{8,10},{9,7},{10,... | collective-permute-start | bytes 1376264 | tf_op jit(solution)/shard_map/ppermute | solution.py:31
  64.7 0.3 collective-permute-start.8
  65.0 0.2 collective-permute-start.9
  65.2 0.0 collective-permute-done.18.refs_11_
  65.2 5.5 %collective-permute-start.20 = (bf16[4,2,56,640]{3,2,1,0:T(8,128)(2,1)S(1)}, bf16[4,2,56,640]{3,2,1,0:T(8,128)(2,1)S(1)}, u32[]{:S(2)}, u32[]{:S(2)}) collective-permute-start(bf16[4,2,56,640]{3,2,1,0:T(8,128)(2,1)S(1)} %collective-permute-done.18.refs_11_), channel_id=1, source_target_pairs={{0,1},{1,0},{2,3},{3,2},{4,5},{5,4},{6,7},{7,6},{8,9},{9,8},{10,11... | collective-permute-start | bytes 1720328 | tf_op jit(solution)/shard_map/ppermute | solution.py:20
  70.7 8.7 %collective-permute-done.6.refs_3_ = bf16[4,2,56,512]{3,2,1,0:T(8,128)(2,1)S(1)} collective-permute-done((bf16[4,2,56,512]{3,2,1,0:T(8,128)(2,1)}, bf16[4,2,56,512]{3,2,1,0:T(8,128)(2,1)S(1)}, u32[]{:S(2)}, u32[]{:S(2)}) %collective-permute-start.6) | collective-permute-done | bytes 458784 | tf_op jit(solution)/shard_map/ppermute | solution.py:31
  79.4 3.5 %collective-permute-start.7 = (bf16[2,2,56,512]{3,2,1,0:T(8,128)(2,1)S(1)}, bf16[2,2,56,512]{3,2,1,0:T(8,128)(2,1)}, u32[]{:S(2)}, u32[]{:S(2)}) collective-permute-start(bf16[2,2,56,512]{3,2,1,0:T(8,128)(2,1)S(1)} %constant_dynamic-slice_fusion.2), channel_id=1, source_target_pairs={{0,2},{1,15},{2,4},{3,1},{4,6},{5,3},{6,8},{7,5},{8,10},{9,7},{10,... | collective-permute-start | bytes 688136 | tf_op jit(solution)/shard_map/ppermute | solution.py:31
  82.9 1.6 collective-permute-start.10
  84.5 5.9 %collective-permute-done.7.refs_4_ = bf16[2,2,56,512]{3,2,1,0:T(8,128)(2,1)} collective-permute-done((bf16[2,2,56,512]{3,2,1,0:T(8,128)(2,1)S(1)}, bf16[2,2,56,512]{3,2,1,0:T(8,128)(2,1)}, u32[]{:S(2)}, u32[]{:S(2)}) %collective-permute-start.7) | collective-permute-done | bytes 229408 | tf_op jit(solution)/shard_map/ppermute | solution.py:31
  90.4 6.2 %collective-permute-start.11 = (bf16[2,2,56,512]{3,2,1,0:T(8,128)(2,1)}, bf16[2,2,56,512]{3,2,1,0:T(8,128)(2,1)}, u32[]{:S(2)}, u32[]{:S(2)}) collective-permute-start(bf16[2,2,56,512]{3,2,1,0:T(8,128)(2,1)} %collective-permute-done.7.refs_4_), channel_id=1, source_target_pairs={{0,1},{1,0},{2,3},{3,2},{4,5},{5,4},{6,7},{7,6},{8,9},{9,8},{10,11... | collective-permute-start | bytes 688136 | tf_op jit(solution)/shard_map/ppermute | solution.py:20
  96.7 0.7 copy.14
  97.4 0.8 collective-permute-done.11.refs_8_
  98.3 0.8 copy-done.9
  99.0 19.3 %spatial.1.attended = bf16[1152,512]{1,0:T(8,128)(2,1)} custom-call(s32[8]{0:T(128)} %clip_tokens.1, s32[32]{0:T(128)} %block_clip.1, bf16[512,1152]{1,0:T(8,128)(2,1)} %bitcast.41, f32[6,1,1152]{2,1,0:T(1,128)} %bitcast.35, f32[72,4]{1,0:T(8,128)} %bitcast.33, bf16[4,2,56,512]{3,2,1,0:T(8,128)(2,1)} %copy-done.1, ...), custom_call_target="tpu_custom_call" | custom-call | flops 20000000000 | bytes 20000000 | tf_op jit(solution)/shard_map/spatial/pallas_call | solution.py:298
  118.3 0.0 all-gather.3.cloned.1.call-done
  118.3 7.4 %mixing.1 = bf16[32,144,128]{2,1,0:T(8,128)(2,1)} custom-call(bf16[512,1152]{1,0:T(8,128)(2,1)} %bitcast.42, f32[6,1,1152]{2,1,0:T(1,128)} %bitcast.36, bf16[1152,512]{1,0:T(8,128)(2,1)} %spatial.1.attended, bf16[64,96,1152]{2,1,0:T(8,128)(2,1)} %bitcast.39), custom_call_target="tpu_custom_call" | custom-call | flops 20000000000 | bytes 20000000 | tf_op jit(solution)/shard_map/mixing/pallas_call | solution.py:309
  125.7 0.0 copy-start.4
  125.7 0.0 copy-start.10
  125.7 4.8 %all-to-all-start = ((bf16[32,144,128]{2,1,0:T(8,128)(2,1)}), bf16[32,144,128]{2,1,0:T(8,128)(2,1)S(1)}, u32[]{:S(2)}, u32[]{:S(2)}) async-start(bf16[32,144,128]{2,1,0:T(8,128)(2,1)} %mixing.1), calls=%async_computation | async-start | bytes 2359296 | tf_op jit(solution)/shard_map/all_to_all | solution.py:323
  130.5 1.1 copy.15
  131.6 0.1 eq.29
  131.7 0.1 select_reduce_fusion
  131.8 0.8 and_convert_fusion.allowed
  132.6 25.0 %all-to-all-done.received = bf16[32,144,128]{2,1,0:T(8,128)(2,1)S(1)} async-done(((bf16[32,144,128]{2,1,0:T(8,128)(2,1)}), bf16[32,144,128]{2,1,0:T(8,128)(2,1)S(1)}, u32[]{:S(2)}, u32[]{:S(2)}) %all-to-all-start) | async-done | bytes 1179680 | tf_op jit(solution)/shard_map/all_to_all | solution.py:323
  157.7 1.0 copy-done
  158.7 24.3 %temporal.1 = f32[16,512]{1,0:T(8,128)} custom-call(bf16[32,144,128]{2,1,0:T(8,128)(2,1)} %copy-done, f32[1152,6]{1,0:T(8,128)} %bitcast.27, f32[72,4]{1,0:T(8,128)} %bitcast.34, f32[256,256]{1,0:T(8,128)} %and_convert_fusion.allowed, bf16[16,1152]{1,0:T(8,128)(2,1)} %bitcast.43, bf16[64,96,1152]{2,1,0:T(8,128)(2,1)} %bitcast.40), custom_call_target="tpu_custom_call" | custom-call | flops 20000000000 | bytes 20000000 | tf_op jit(solution)/shard_map/temporal/pallas_call | solution.py:324
  183.0 0.7 constant_dynamic-slice_fusion
  183.7 4.9 %collective-permute-start.21 = (f32[8,512]{1,0:T(8,128)S(1)}, f32[8,512]{1,0:T(8,128)S(1)}, u32[]{:S(2)}, u32[]{:S(2)}) collective-permute-start(f32[8,512]{1,0:T(8,128)S(1)} %constant_dynamic-slice_fusion), channel_id=1, source_target_pairs={{0,1},{1,0},{2,3},{3,2},{4,5},{5,4},{6,7},{7,6},{8,9},{9,8},{10,11... | collective-permute-start | bytes 49160 | tf_op jit(solution)/shard_map/ppermute | solution.py:344
  188.7 0.1 broadcast_compare_fusion
  188.7 0.8 collective-permute-done.21
  189.5 0.7 multiply_add_fusion
  190.2 0.1 reshape.70
  190.3 0.7 fusion.6
  (46 shorter events, 0.4 us)
Async XLA Ops:
  6.5 111.8 %all-gather.3.cloned.1.call-start = ((), (), s32[]{:S(2)}) async-start(), calls=%async_computation.1 | async-start | bytes 14376960 | tf_op jit(solution)/shard_map/all_gather | solution.py:289
  9.2 4.3 %collective-permute-start = (bf16[56,1152]{1,0:T(8,128)(2,1)S(1)}, bf16[56,1152]{1,0:T(8,128)(2,1)S(1)}, u32[]{:S(2)}, u32[]{:S(2)}) collective-permute-start(bf16[56,1152]{1,0:T(8,128)(2,1)S(1)} %pad.8), channel_id=1, source_target_pairs={{0,1},{1,0},{2,3},{3,2},{4,5},{5,4},{6,7},{7,6},{8,9},{9,8},{10,11... | collective-permute-start | bytes 387080 | tf_op jit(solution)/shard_map/ppermute | solution.py:20
  14.5 21.9 %collective-permute-start.12 = (bf16[2,56,640]{2,1,0:T(8,128)(2,1)S(1)}, bf16[2,56,640]{2,1,0:T(8,128)(2,1)S(1)}, u32[]{:S(2)}, u32[]{:S(2)}) collective-permute-start(bf16[2,56,640]{2,1,0:T(8,128)(2,1)S(1)} %get-tuple-element.6), channel_id=1, source_target_pairs={{0,2},{1,15},{2,4},{3,1},{4,6},{5,3},{6,8},{7,5},{8,10},{9,7},{10,... | collective-permute-start | bytes 430088 | tf_op jit(solution)/shard_map/ppermute | solution.py:31
  18.4 18.0 %collective-permute-start.13 = (bf16[2,56,640]{2,1,0:T(8,128)(2,1)S(1)}, bf16[2,56,640]{2,1,0:T(8,128)(2,1)S(1)}, u32[]{:S(2)}, u32[]{:S(2)}) collective-permute-start(bf16[2,56,640]{2,1,0:T(8,128)(2,1)S(1)} %get-tuple-element.6), channel_id=1, source_target_pairs={{0,4},{1,13},{2,6},{3,15},{4,8},{5,1},{6,10},{7,3},{8,12},{9,5},{1... | collective-permute-start | bytes 430088 | tf_op jit(solution)/shard_map/ppermute | solution.py:31
  19.6 16.8 %collective-permute-start.14 = (bf16[2,56,640]{2,1,0:T(8,128)(2,1)S(1)}, bf16[2,56,640]{2,1,0:T(8,128)(2,1)S(1)}, u32[]{:S(2)}, u32[]{:S(2)}) collective-permute-start(bf16[2,56,640]{2,1,0:T(8,128)(2,1)S(1)} %get-tuple-element.6), channel_id=1, source_target_pairs={{0,6},{1,11},{2,8},{3,13},{4,10},{5,15},{6,12},{7,1},{8,14},{9,3},... | collective-permute-start | bytes 430088 | tf_op jit(solution)/shard_map/ppermute | solution.py:31
  20.0 12.0 %collective-permute-start.1 = (bf16[2,56,512]{2,1,0:T(8,128)(2,1)S(1)}, bf16[2,56,512]{2,1,0:T(8,128)(2,1)S(1)}, u32[]{:S(2)}, u32[]{:S(2)}) collective-permute-start(bf16[2,56,512]{2,1,0:T(8,128)(2,1)S(1)} %pad_maximum_fusion.4), channel_id=1, source_target_pairs={{0,16},{1,49},{2,18},{3,51},{4,20},{5,53},{6,22},{7,55},{8,24},{9,... | collective-permute-start | bytes 344072 | tf_op jit(solution)/shard_map/ppermute | solution.py:31
  22.7 4.9 %collective-permute-start.2 = (bf16[1,56,512]{2,1,0:T(8,128)(2,1)S(1)}, bf16[1,56,512]{2,1,0:T(8,128)(2,1)S(1)}, u32[]{:S(2)}, u32[]{:S(2)}) collective-permute-start(bf16[1,56,512]{2,1,0:T(8,128)(2,1)S(1)} %fusion.7), channel_id=1, source_target_pairs={{0,32},{1,33},{2,34},{3,35},{4,36},{5,37},{6,38},{7,39},{8,40},{9,... | collective-permute-start | bytes 172040 | tf_op jit(solution)/shard_map/ppermute | solution.py:31
  27.6 8.8 %collective-permute-start.15 = (bf16[1,56,640]{2,1,0:T(8,128)(2,1)S(1)}, bf16[1,56,640]{2,1,0:T(8,128)(2,1)S(1)}, u32[]{:S(2)}, u32[]{:S(2)}) collective-permute-start(bf16[1,56,640]{2,1,0:T(8,128)(2,1)S(1)} %fusion.5), channel_id=1, source_target_pairs={{0,8},{1,9},{2,10},{3,11},{4,12},{5,13},{6,14},{7,15},{8,0},{9,1},... | collective-permute-start | bytes 215048 | tf_op jit(solution)/shard_map/ppermute | solution.py:31
  32.1 7.0 %collective-permute-start.3 = (bf16[3,56,512]{2,1,0:T(8,128)(2,1)S(1)}, bf16[3,56,512]{2,1,0:T(8,128)(2,1)S(1)}, u32[]{:S(2)}, u32[]{:S(2)}) collective-permute-start(bf16[3,56,512]{2,1,0:T(8,128)(2,1)S(1)} %pad_maximum_fusion.2), channel_id=1, source_target_pairs={{0,1},{1,0},{2,3},{3,2},{4,5},{5,4},{6,7},{7,6},{8,9},{9,8},{10,11... | collective-permute-start | bytes 516104 | tf_op jit(solution)/shard_map/ppermute | solution.py:20
  36.5 4.0 %collective-permute-start.16 = (bf16[7,56,640]{2,1,0:T(8,128)(2,1)S(1)}, bf16[7,56,640]{2,1,0:T(8,128)(2,1)S(1)}, u32[]{:S(2)}, u32[]{:S(2)}) collective-permute-start(bf16[7,56,640]{2,1,0:T(8,128)(2,1)S(1)} %pad_maximum_fusion), channel_id=1, source_target_pairs={{0,1},{1,0},{2,3},{3,2},{4,5},{5,4},{6,7},{7,6},{8,9},{9,8},{10,11... | collective-permute-start | bytes 1505288 | tf_op jit(solution)/shard_map/ppermute | solution.py:20
  40.8 15.0 %copy-start.5 = (bf16[16,56,640]{2,1,0:T(8,128)(2,1)}, bf16[16,56,640]{2,1,0:T(8,128)(2,1)S(1)}, u32[]{:S(2)}) copy-start(bf16[16,56,640]{2,1,0:T(8,128)(2,1)S(1)} %select_dynamic-update-slice_fusion.2) | copy-start | bytes 3440644
  40.8 15.2 %collective-permute-start.17 = (bf16[8,2,56,640]{3,2,1,0:T(8,128)(2,1)S(1)}, bf16[8,2,56,640]{3,2,1,0:T(8,128)(2,1)S(1)}, u32[]{:S(2)}, u32[]{:S(2)}) collective-permute-start(bf16[8,2,56,640]{3,2,1,0:T(8,128)(2,1)S(1)} %bitcast.37), channel_id=1, source_target_pairs={{0,16},{1,49},{2,18},{3,51},{4,20},{5,53},{6,22},{7,55},{8,24},{9,... | collective-permute-start | bytes 3440648 | tf_op jit(solution)/shard_map/ppermute | solution.py:31
  42.2 54.5 %copy-start.6 = (f32[4,72]{1,0:T(4,128)S(1)}, f32[4,72]{1,0:T(4,128)}, u32[]{:S(2)}) copy-start(f32[4,72]{1,0:T(4,128)} %param.17) | copy-start | bytes 3460
  42.3 56.0 %copy-start.1 = (bf16[4,2,56,512]{3,2,1,0:T(8,128)(2,1)}, bf16[4,2,56,512]{3,2,1,0:T(8,128)(2,1)S(1)}, u32[]{:S(2)}) copy-start(bf16[4,2,56,512]{3,2,1,0:T(8,128)(2,1)S(1)} %pad_maximum_fusion.1.refs_0_) | copy-start | bytes 1376260
  42.3 10.5 %collective-permute-start.4 = (bf16[4,2,56,512]{3,2,1,0:T(8,128)(2,1)S(1)}, bf16[4,2,56,512]{3,2,1,0:T(8,128)(2,1)}, u32[]{:S(2)}, u32[]{:S(2)}) collective-permute-start(bf16[4,2,56,512]{3,2,1,0:T(8,128)(2,1)S(1)} %pad_maximum_fusion.1.refs_0_), channel_id=1, source_target_pairs={{0,2},{1,15},{2,4},{3,1},{4,6},{5,3},{6,8},{7,5},{8,10},{9,7},{10,... | collective-permute-start | bytes 1376264 | tf_op jit(solution)/shard_map/ppermute | solution.py:31
  52.7 8.8 %collective-permute-start.5 = (bf16[4,2,56,512]{3,2,1,0:T(8,128)(2,1)}, bf16[4,2,56,512]{3,2,1,0:T(8,128)(2,1)}, u32[]{:S(2)}, u32[]{:S(2)}) collective-permute-start(bf16[4,2,56,512]{3,2,1,0:T(8,128)(2,1)} %collective-permute-done.4.refs_1_), channel_id=1, source_target_pairs={{0,2},{1,15},{2,4},{3,1},{4,6},{5,3},{6,8},{7,5},{8,10},{9,7},{10,... | collective-permute-start | bytes 1376264 | tf_op jit(solution)/shard_map/ppermute | solution.py:31
  56.0 42.2 %copy-start.2 = (bf16[8,2,56,640]{3,2,1,0:T(8,128)(2,1)}, bf16[8,2,56,640]{3,2,1,0:T(8,128)(2,1)S(1)}, u32[]{:S(2)}) copy-start(bf16[8,2,56,640]{3,2,1,0:T(8,128)(2,1)S(1)} %collective-permute-done.17.refs_10_) | copy-start | bytes 3440644
  56.1 9.1 %collective-permute-start.18 = (bf16[4,2,56,640]{3,2,1,0:T(8,128)(2,1)S(1)}, bf16[4,2,56,640]{3,2,1,0:T(8,128)(2,1)S(1)}, u32[]{:S(2)}, u32[]{:S(2)}) collective-permute-start(bf16[4,2,56,640]{3,2,1,0:T(8,128)(2,1)S(1)} %constant_dynamic-slice_fusion.1), channel_id=1, source_target_pairs={{0,16},{1,49},{2,18},{3,51},{4,20},{5,53},{6,22},{7,55},{8,24},{9,... | collective-permute-start | bytes 1720328 | tf_op jit(solution)/shard_map/ppermute | solution.py:31
  58.5 39.7 %collective-permute-start.19 = (bf16[8,2,56,640]{3,2,1,0:T(8,128)(2,1)S(1)}, bf16[8,2,56,640]{3,2,1,0:T(8,128)(2,1)}, u32[]{:S(2)}, u32[]{:S(2)}) collective-permute-start(bf16[8,2,56,640]{3,2,1,0:T(8,128)(2,1)S(1)} %collective-permute-done.17.refs_10_), channel_id=1, source_target_pairs={{0,1},{1,0},{2,3},{3,2},{4,5},{5,4},{6,7},{7,6},{8,9},{9,8},{10,11... | collective-permute-start | bytes 3440648 | tf_op jit(solution)/shard_map/ppermute | solution.py:20
  61.5 17.8 %collective-permute-start.6 = (bf16[4,2,56,512]{3,2,1,0:T(8,128)(2,1)}, bf16[4,2,56,512]{3,2,1,0:T(8,128)(2,1)S(1)}, u32[]{:S(2)}, u32[]{:S(2)}) collective-permute-start(bf16[4,2,56,512]{3,2,1,0:T(8,128)(2,1)} %collective-permute-done.5.refs_2_), channel_id=1, source_target_pairs={{0,2},{1,15},{2,4},{3,1},{4,6},{5,3},{6,8},{7,5},{8,10},{9,7},{10,... | collective-permute-start | bytes 1376264 | tf_op jit(solution)/shard_map/ppermute | solution.py:31
  64.7 18.2 %collective-permute-start.8 = (bf16[4,2,56,512]{3,2,1,0:T(8,128)(2,1)}, bf16[4,2,56,512]{3,2,1,0:T(8,128)(2,1)}, u32[]{:S(2)}, u32[]{:S(2)}) collective-permute-start(bf16[4,2,56,512]{3,2,1,0:T(8,128)(2,1)} %collective-permute-done.4.refs_1_), channel_id=1, source_target_pairs={{0,1},{1,0},{2,3},{3,2},{4,5},{5,4},{6,7},{7,6},{8,9},{9,8},{10,11... | collective-permute-start | bytes 1376264 | tf_op jit(solution)/shard_map/ppermute | solution.py:20
  65.0 32.4 %collective-permute-start.9 = (bf16[4,2,56,512]{3,2,1,0:T(8,128)(2,1)}, bf16[4,2,56,512]{3,2,1,0:T(8,128)(2,1)}, u32[]{:S(2)}, u32[]{:S(2)}) collective-permute-start(bf16[4,2,56,512]{3,2,1,0:T(8,128)(2,1)} %collective-permute-done.5.refs_2_), channel_id=1, source_target_pairs={{0,1},{1,0},{2,3},{3,2},{4,5},{5,4},{6,7},{7,6},{8,9},{9,8},{10,11... | collective-permute-start | bytes 1376264 | tf_op jit(solution)/shard_map/ppermute | solution.py:20
  65.2 33.0 %copy-start.8 = (bf16[4,2,56,640]{3,2,1,0:T(8,128)(2,1)}, bf16[4,2,56,640]{3,2,1,0:T(8,128)(2,1)S(1)}, u32[]{:S(2)}) copy-start(bf16[4,2,56,640]{3,2,1,0:T(8,128)(2,1)S(1)} %collective-permute-done.18.refs_11_) | copy-start | bytes 1720324
  65.2 33.0 %collective-permute-start.20 = (bf16[4,2,56,640]{3,2,1,0:T(8,128)(2,1)S(1)}, bf16[4,2,56,640]{3,2,1,0:T(8,128)(2,1)S(1)}, u32[]{:S(2)}, u32[]{:S(2)}) collective-permute-start(bf16[4,2,56,640]{3,2,1,0:T(8,128)(2,1)S(1)} %collective-permute-done.18.refs_11_), channel_id=1, source_target_pairs={{0,1},{1,0},{2,3},{3,2},{4,5},{5,4},{6,7},{7,6},{8,9},{9,8},{10,11... | collective-permute-start | bytes 1720328 | tf_op jit(solution)/shard_map/ppermute | solution.py:20
  79.4 18.9 %copy-start.3 = (bf16[4,2,56,512]{3,2,1,0:T(8,128)(2,1)}, bf16[4,2,56,512]{3,2,1,0:T(8,128)(2,1)S(1)}, u32[]{:S(2)}) copy-start(bf16[4,2,56,512]{3,2,1,0:T(8,128)(2,1)S(1)} %collective-permute-done.6.refs_3_) | copy-start | bytes 1376260
  79.4 11.0 %collective-permute-start.7 = (bf16[2,2,56,512]{3,2,1,0:T(8,128)(2,1)S(1)}, bf16[2,2,56,512]{3,2,1,0:T(8,128)(2,1)}, u32[]{:S(2)}, u32[]{:S(2)}) collective-permute-start(bf16[2,2,56,512]{3,2,1,0:T(8,128)(2,1)S(1)} %constant_dynamic-slice_fusion.2), channel_id=1, source_target_pairs={{0,2},{1,15},{2,4},{3,1},{4,6},{5,3},{6,8},{7,5},{8,10},{9,7},{10,... | collective-permute-start | bytes 688136 | tf_op jit(solution)/shard_map/ppermute | solution.py:31
  82.9 15.3 %collective-permute-start.10 = (bf16[4,2,56,512]{3,2,1,0:T(8,128)(2,1)S(1)}, bf16[4,2,56,512]{3,2,1,0:T(8,128)(2,1)}, u32[]{:S(2)}, u32[]{:S(2)}) collective-permute-start(bf16[4,2,56,512]{3,2,1,0:T(8,128)(2,1)S(1)} %collective-permute-done.6.refs_3_), channel_id=1, source_target_pairs={{0,1},{1,0},{2,3},{3,2},{4,5},{5,4},{6,7},{7,6},{8,9},{9,8},{10,11... | collective-permute-start | bytes 1376264 | tf_op jit(solution)/shard_map/ppermute | solution.py:20
  90.4 7.8 %collective-permute-start.11 = (bf16[2,2,56,512]{3,2,1,0:T(8,128)(2,1)}, bf16[2,2,56,512]{3,2,1,0:T(8,128)(2,1)}, u32[]{:S(2)}, u32[]{:S(2)}) collective-permute-start(bf16[2,2,56,512]{3,2,1,0:T(8,128)(2,1)} %collective-permute-done.7.refs_4_), channel_id=1, source_target_pairs={{0,1},{1,0},{2,3},{3,2},{4,5},{5,4},{6,7},{7,6},{8,9},{9,8},{10,11... | collective-permute-start | bytes 688136 | tf_op jit(solution)/shard_map/ppermute | solution.py:20
  98.2 0.8 copy-start.9
  125.7 4.8 %copy-start.4 = (f32[1,6,1152]{2,0,1:T(1,128)S(1)}, f32[1,6,1152]{2,0,1:T(1,128)}, u32[]{:S(2)}) copy-start(f32[1,6,1152]{2,0,1:T(1,128)} %param.11) | copy-start | bytes 82948
  125.7 5.9 %copy-start.7 = (s32[32]{0:T(128)S(1)}, s32[32]{0:T(128)}, u32[]{:S(2)}) copy-start(s32[32]{0:T(128)} %block_clip.1) | copy-start | bytes 388
  125.7 6.0 %copy-start.10 = (s32[8]{0:T(128)S(1)}, s32[8]{0:T(128)}, u32[]{:S(2)}) copy-start(s32[8]{0:T(128)} %clip_tokens.1) | copy-start | bytes 100
  125.7 32.0 %all-to-all-start = ((bf16[32,144,128]{2,1,0:T(8,128)(2,1)}), bf16[32,144,128]{2,1,0:T(8,128)(2,1)S(1)}, u32[]{:S(2)}, u32[]{:S(2)}) async-start(bf16[32,144,128]{2,1,0:T(8,128)(2,1)} %mixing.1), calls=%async_computation | async-start | bytes 2359296 | tf_op jit(solution)/shard_map/all_to_all | solution.py:323
  157.7 1.0 copy-start
  183.7 5.8 %collective-permute-start.21 = (f32[8,512]{1,0:T(8,128)S(1)}, f32[8,512]{1,0:T(8,128)S(1)}, u32[]{:S(2)}, u32[]{:S(2)}) collective-permute-start(f32[8,512]{1,0:T(8,128)S(1)} %constant_dynamic-slice_fusion), channel_id=1, source_target_pairs={{0,1},{1,0},{2,3},{3,2},{4,5},{5,4},{6,7},{7,6},{8,9},{9,8},{10,11... | collective-permute-start | bytes 49160 | tf_op jit(solution)/shard_map/ppermute | solution.py:344
Sparse Core Ops, SparseCore 0:
  10.1 101.5 all-gather.2

commit v4 on v3

--- a/solution.py
+++ b/solution.py
@@ -11,7 +11,7 @@
 BF16 = jnp.bfloat16
 F32 = jnp.float32
 LANES = 128
-TEMPORAL_ROWS = 256
+PIECES = 2
 X_RING, Z_RING, SPLIT = 4, 8, 512
 X_SLOTS = (0, -1, 1, 2)
 Z_SLOTS = (0, -1, -2, -3, 1, 2, 3, 4)
@@ -173,6 +173,12 @@
     lax.fori_loop(0, width // (2 * head_size), pair, 0)
 
 
+def piece_rows(values_in, piece):
+    rows, width = values_in.shape
+    split = values_in.reshape(rows // (8 * PIECES), PIECES, 8, width)
+    return split[:, piece].reshape(rows // PIECES, width)
+
+
 def spatial_kernel(head_size, clip_tokens, block_clip, tokens, levels, gains, *refs):
     rows, rings = refs[:9], refs[9:14]
     attended, landing, columns, normed, projected, sem = refs[14:]
@@ -180,65 +186,84 @@
     for copy in arriving:
         copy.start()
     row_count = tokens.shape[0]
-    for start in range(0, row_count, LANES):
-        chunk = slice(start, start + LANES)
+    for start in range(0, row_count, 2 * LANES):
+        chunk = slice(start, start + 2 * LANES)
         values_in = layer_norm(tokens[chunk, :].astype(F32), 1) * (1.0 + levels[1]) + levels[0]
-        normed[:, chunk] = values_in.astype(BF16).T
+        for piece in range(PIECES):
+            first = (piece * row_count + start) // PIECES
+            normed[:, first : first + LANES] = piece_rows(values_in, piece).astype(BF16).T
     for copy in arriving:
         copy.wait()
     lay_out(landing, columns, 0, 3 * head_size // 4)
     project(columns, normed, projected)
     length = clip_tokens[block_clip[lax.axis_index("seq")]]
-    inside = lax.broadcasted_iota(jnp.int32, (head_size + 8, row_count), 1) < length
+    lane = lax.broadcasted_iota(jnp.int32, (head_size + 8, row_count), 1)
+    place = lane % (row_count // PIECES)
+    inside = place // 8 * (8 * PIECES) + lane // (row_count // PIECES) * 8 + place % 8 < length
     attend(projected, attended, gains, 0, inside, None, head_size)
 
 
-def mixing_kernel(head_size, tokens, levels, attended, gathered, residual, landing, out_rows, sem):
+def mixing_kernel(head_size, tokens, levels, attended, gathered, *refs):
+    pieces, (landing, out_rows, sem) = refs[:PIECES], refs[PIECES:]
     first, kept = landing.shape[1] * 2, landing.shape[1]
     arriving = pltpu.make_async_copy(gathered.at[:, pl.ds(first, kept), :], landing, sem)
     arriving.start()
     arriving.wait()
     lay_out(landing, out_rows, head_size - first, head_size // 4)
-    for start in range(0, tokens.shape[0], 256):
-        chunk = slice(start, start + 256)
-        projection = dot_over(attended[:, chunk], out_rows[...], 0, 1)
-        updated = (tokens[chunk, :].astype(F32) + levels[2] * projection).astype(BF16)
-        for d in range(16):
-            for j in range(residual.shape[1] // 16):
-                residual[start // 16 + d, 16 * j : 16 * j + 16, :] = updated[
-                    16 * d : 16 * d + 16, LANES * j : LANES * (j + 1)
-                ]
-
-
-def temporal_kernel(head_size, received, levels, gains, allowed, w_final, gathered, predicted,
-                    landing, columns, normed, projected, out_rows, attended, by_frame, by_slot, sem):
+    row_count, width = tokens.shape
+    size = row_count // PIECES
+    for piece in range(PIECES):
+        projection = dot_over(attended[:, piece * size : (piece + 1) * size], out_rows[...], 0, 1)
+        for start in range(0, size, LANES):
+            own = piece_rows(tokens[start * PIECES : (start + LANES) * PIECES, :].astype(F32), piece)
+            updated = own + levels[2] * projection[start : start + LANES]
+            for d in range(LANES // 8):
+                rows = slice(8 * d, 8 * d + 8)
+                tiles = [updated[rows, LANES * j : LANES * (j + 1)] for j in range(width // LANES)]
+                pieces[piece][start // 8 + d] = jnp.concatenate(tiles, axis=0).astype(BF16)
+
+
+def prepare_kernel(head_size, gathered, columns, out_rows, landing, sem):
     arriving = pltpu.make_async_copy(gathered.at[:, pl.ds(0, landing.shape[1]), :], landing, sem)
     arriving.start()
+    arriving.wait()
+    share = 3 * head_size // 4
+    lay_out(landing, columns, 0, share)
+    lay_out(landing, out_rows, share, head_size // 4)
+
+
+def temporal_kernel(head_size, received, levels, gains, allowed, w_final, held_columns, held_rows, predicted,
+                    columns, normed, projected, out_rows, attended, by_frame, by_slot, sems):
+    arriving = [
+        pltpu.make_async_copy(held_columns, columns, sems.at[0]),
+        pltpu.make_async_copy(held_rows, out_rows, sems.at[1]),
+    ]
+    for copy in arriving:
+        copy.start()
     frames = received.shape[0]
     width, row_count = normed.shape
     locations = row_count // frames
 
     def unpack(b, carry):
-        rows = pl.ds(pl.multiple_of(b * locations, 16), locations)
+        rows = pl.ds(pl.multiple_of(b * locations, 8), locations)
+        values_in = received[b].astype(F32)
         for j in range(width // LANES):
-            by_frame[rows, LANES * j : LANES * (j + 1)] = received[b, 16 * j : 16 * j + 16, :]
+            by_frame[rows, LANES * j : LANES * (j + 1)] = values_in[locations * j : locations * (j + 1)]
         return carry
 
     lax.fori_loop(0, frames, unpack, 0)
     row = lax.broadcasted_iota(jnp.int32, (row_count, row_count), 0)
     column = lax.broadcasted_iota(jnp.int32, (row_count, row_count), 1)
     moved = (row == (column % frames) * locations + column // frames).astype(F32).astype(BF16)
-    by_slot[...] = dot_over(by_frame[...], moved, 0, 0).astype(BF16)
+    by_slot[...] = dot_over(by_frame[...].astype(BF16), moved, 0, 0).astype(BF16)
     for start in range(0, row_count, LANES):
         chunk = slice(start, start + LANES)
         values_in = layer_norm(by_slot[:, chunk].astype(F32), 0)
         normed[:, chunk] = (values_in * (1.0 + levels[:, 4:5]) + levels[:, 3:4]).astype(BF16)
-    arriving.wait()
-    share = 3 * head_size // 4
-    lay_out(landing, columns, 0, share)
-    lay_out(landing, out_rows, share, head_size // 4)
+    arriving[0].wait()
     project(columns, normed, projected)
     attend(projected, attended, gains, 2, None, allowed, head_size)
+    arriving[1].wait()
     projected[0:width, :] = jnp.dot(out_rows[...], attended[...], preferred_element_type=F32)
     for start in range(0, row_count, LANES):
         chunk = slice(start, start + LANES)
@@ -247,9 +272,8 @@
     predicted[...] = jnp.dot(w_final[...], normed[...], preferred_element_type=F32)
 
 
-def projection_scratch(landing_shape, rows, width):
+def projection_scratch(rows, width):
     return [
-        pltpu.VMEM(landing_shape, BF16),
         pltpu.VMEM((3 * width, width), BF16),
         pltpu.VMEM((width, rows), BF16),
         pltpu.VMEM((3 * width, rows), F32),
@@ -279,8 +303,8 @@
     member = block_clip[:, None] == jnp.arange(clip_tokens.shape[0], dtype=jnp.int32)[None, :]
     lengths = jnp.sum(jnp.where(member, clip_tokens[None, :], 0), axis=1)
     gains = norm_gains.T
-    slot_of = jnp.arange(TEMPORAL_ROWS, dtype=jnp.int32) // frames
-    clip_of = jnp.tile(block_clip, TEMPORAL_ROWS // frames)
+    slot_of = jnp.arange(rows // PIECES, dtype=jnp.int32) // frames
+    clip_of = jnp.tile(block_clip, rows // PIECES // frames)
     allowed = ((slot_of[:, None] == slot_of[None, :]) & (clip_of[:, None] == clip_of[None, :])).astype(F32)
 
     first_rows = jnp.pad(w_qkv_s.T, ((0, -w_qkv_s.shape[1] % 8), (0, 0)))
@@ -300,17 +324,19 @@
         out_shape=jax.ShapeDtypeStruct((width, rows), BF16),
         in_specs=[smem, smem, vmem, vmem, vmem] + [anywhere] * 14,
         out_specs=vmem,
-        scratch_shapes=projection_scratch((shards,) + first_rows.shape, rows, width)
+        scratch_shapes=[pltpu.VMEM((shards,) + first_rows.shape, BF16)]
+        + projection_scratch(rows, width)
         + [pltpu.SemaphoreType.DMA],
         compiler_params=params,
         cost_estimate=cost,
         name="spatial",
     )(clip_tokens, block_clip, tokens[0], levels, gains, *row_parts, *ring_parts)
-    residual = pl.pallas_call(
+    size = rows // PIECES
+    residuals = pl.pallas_call(
         functools.partial(mixing_kernel, head_size),
-        out_shape=jax.ShapeDtypeStruct((seq, tile_rows, LANES), BF16),
+        out_shape=[jax.ShapeDtypeStruct((seq, tile_rows // PIECES, LANES), BF16)] * PIECES,
         in_specs=[vmem, vmem, vmem, anywhere],
-        out_specs=vmem,
+        out_specs=[vmem] * PIECES,
         scratch_shapes=[
             pltpu.VMEM((shards, 32, width), BF16),
             pltpu.VMEM((width, width), BF16),
@@ -320,24 +346,42 @@
         cost_estimate=cost,
         name="mixing",
     )(tokens[0], levels, attended, gathered)
-    received = lax.all_to_all(residual, "seq", split_axis=0, concat_axis=0, tiled=True)
-    predicted = pl.pallas_call(
-        functools.partial(temporal_kernel, head_size),
-        out_shape=jax.ShapeDtypeStruct((w_final.shape[1], rows), F32),
-        in_specs=[vmem] * 5 + [anywhere],
-        out_specs=vmem,
-        scratch_shapes=projection_scratch((shards, 80, width), rows, width)
-        + [
-            pltpu.VMEM((width, width), BF16),
-            pltpu.VMEM((width, rows), BF16),
-            pltpu.VMEM((rows, width), BF16),
-            pltpu.VMEM((width, rows), BF16),
-            pltpu.SemaphoreType.DMA,
+    held = pl.pallas_call(
+        functools.partial(prepare_kernel, head_size),
+        out_shape=[
+            jax.ShapeDtypeStruct((3 * width, width), BF16),
+            jax.ShapeDtypeStruct((width, width), BF16),
         ],
+        in_specs=[anywhere],
+        out_specs=[vmem] * 2,
+        scratch_shapes=[pltpu.VMEM((shards, 80, width), BF16), pltpu.SemaphoreType.DMA],
         compiler_params=params,
-        cost_estimate=cost,
-        name="temporal",
-    )(received, modulation[0].T, gains, allowed, w_final.T, gathered)
+        cost_estimate=pl.CostEstimate(flops=0, bytes_accessed=30_000_000, transcendentals=0),
+        name="prepare",
+    )(gathered)
+    found = []
+    for residual in residuals:
+        received = lax.all_to_all(residual, "seq", split_axis=0, concat_axis=0, tiled=True)
+        found.append(
+            pl.pallas_call(
+                functools.partial(temporal_kernel, head_size),
+                out_shape=jax.ShapeDtypeStruct((w_final.shape[1], size), F32),
+                in_specs=[vmem] * 5 + [anywhere] * 2,
+                out_specs=vmem,
+                scratch_shapes=projection_scratch(size, width)
+                + [
+                    pltpu.VMEM((width, width), BF16),
+                    pltpu.VMEM((width, size), BF16),
+                    pltpu.VMEM((size, width), F32),
+                    pltpu.VMEM((width, size), BF16),
+                    pltpu.SemaphoreType.DMA((2,)),
+                ],
+                compiler_params=params,
+                cost_estimate=cost,
+                name="temporal",
+            )(received, modulation[0].T, gains, allowed, w_final.T, *held)
+        )
+    predicted = jnp.concatenate(found, axis=1)
 
     half = predicted.shape[0] // 2
     outgoing = lax.dynamic_slice_in_dim(predicted, (1 - branch_index) * half, half, 0)

time: 199 us -> 200 us (level)
  waiting for transfers between devices: 63.5 us -> 42.8 us
  Pallas kernels: 50.9 us -> 65.7 us
  starting transfers between devices: 58.5 us -> 65.6 us
    all_to_all x1 -> x2, waiting for transfers between devices: 25 us -> 4.47 us  [body(): lax.all_to_all(residual, 'seq', split_axis=0, concat_axis=0, tiled=True)]
    pallas_call x1 -> x2, Pallas kernels: 7.36 us -> 16.7 us  [the longest x1 9.53 us: body(): pl.pallas_call(functools.partial(prepare_kernel, head_size), out_shape=[j...]
    all_to_all x1 -> x2, starting transfers between devices: 4.8 us -> 12.7 us  [body(): lax.all_to_all(residual, 'seq', split_axis=0, concat_axis=0, tiled=True)]
    pallas_call x1 -> x2, Pallas kernels: 24.3 us -> 29.8 us  [body(): pl.pallas_call(functools.partial(temporal_kernel, head_size), out_shape=j...]
  transfers between devices with their start and end apart: 24 -> 25, of which waited for: 12 -> 13; matrix products, arithmetic and copies ran while one was open for 3% -> 3% of each run, Pallas kernels for 10% -> 22%
where the time goes in v4:
time: 200 us; the launch traced here: 199 us
  Pallas kernels  65.7 us (33%)
  starting transfers between devices  65.6 us (33%)
  waiting for transfers between devices  42.8 us (21%)
  between operations  13.7 us (7%)
  other arithmetic  6.43 us (3%)
  local copies, waits for them, and re-layouts  4.72 us (2%)
    ppermute x12, waiting for transfers between devices, plane_step(): return lax.ppermute(array, ('seq', 'cfg'), pairs)  34.4 us
    pallas_call x2, Pallas kernels, body(): pl.pallas_call(functools.partial(temporal_kernel, head_size), out_shape=j...  29.8 us
    ppermute x12, starting transfers between devices, plane_step(): return lax.ppermute(array, ('seq', 'cfg'), pairs)  28.7 us
    ppermute x9, starting transfers between devices, swap_cores(): return lax.ppermute(array, 'cfg', [(0, 1), (1, 0)])  20.3 us
    pallas_call x1, Pallas kernels, body(): pl.pallas_call(functools.partial(spatial_kernel, head_size), out_shape=ja...  19.3 us
    all_to_all x2, starting transfers between devices, body(): lax.all_to_all(residual, 'seq', split_axis=0, concat_axis=0, tiled=True)  12.7 us
    pallas_call x1, Pallas kernels, body(): pl.pallas_call(functools.partial(prepare_kernel, head_size), out_shape=[j...  9.53 us
    pallas_call x1, Pallas kernels, body(): pl.pallas_call(functools.partial(mixing_kernel, head_size), out_shape=[ja...  7.15 us
  transfers between devices with their start and end apart: 25, of which 13 were waited for; matrix products, arithmetic and copies ran while one was open for 3% of the time, Pallas kernels for 22%

profile of v4, /device:TPU:1, one launch (start us, length us, event | category | flops | bytes accessed | tf_op | source)
XLA Modules:
  0.0 199.1 jit_solution(16562589834055712088)
XLA Ops:
  6.5 1.7 fusion.4
  8.2 0.0 all-gather.3.cloned.1.call-update
  8.2 0.9 pad.8
  9.2 3.3 %collective-permute-start = (bf16[56,1152]{1,0:T(8,128)(2,1)S(1)}, bf16[56,1152]{1,0:T(8,128)(2,1)S(1)}, u32[]{:S(2)}, u32[]{:S(2)}) collective-permute-start(bf16[56,1152]{1,0:T(8,128)(2,1)S(1)} %pad.8), channel_id=1, source_target_pairs={{0,1},{1,0},{2,3},{3,2},{4,5},{5,4},{6,7},{7,6},{8,9},{9,8},{10,11... | collective-permute-start | bytes 387080 | tf_op jit(solution)/shard_map/ppermute | solution.py:20
  12.5 1.0 collective-permute-done
  13.5 1.0 select_bitcast_fusion
  14.5 3.9 %collective-permute-start.12 = (bf16[2,56,640]{2,1,0:T(8,128)(2,1)S(1)}, bf16[2,56,640]{2,1,0:T(8,128)(2,1)S(1)}, u32[]{:S(2)}, u32[]{:S(2)}) collective-permute-start(bf16[2,56,640]{2,1,0:T(8,128)(2,1)S(1)} %get-tuple-element.14), channel_id=1, source_target_pairs={{0,2},{1,15},{2,4},{3,1},{4,6},{5,3},{6,8},{7,5},{8,10},{9,7},{10,... | collective-permute-start | bytes 430088 | tf_op jit(solution)/shard_map/ppermute | solution.py:31
  18.4 1.2 collective-permute-start.13
  19.6 0.4 collective-permute-start.14
  20.0 2.6 %collective-permute-start.1 = (bf16[2,56,512]{2,1,0:T(8,128)(2,1)S(1)}, bf16[2,56,512]{2,1,0:T(8,128)(2,1)S(1)}, u32[]{:S(2)}, u32[]{:S(2)}) collective-permute-start(bf16[2,56,512]{2,1,0:T(8,128)(2,1)S(1)} %pad_maximum_fusion.4), channel_id=1, source_target_pairs={{0,16},{1,49},{2,18},{3,51},{4,20},{5,53},{6,22},{7,55},{8,24},{9,... | collective-permute-start | bytes 344072 | tf_op jit(solution)/shard_map/ppermute | solution.py:31
  22.6 0.6 collective-permute-start.2
  23.3 4.3 %collective-permute-done.2 = bf16[1,56,512]{2,1,0:T(8,128)(2,1)S(1)} collective-permute-done((bf16[1,56,512]{2,1,0:T(8,128)(2,1)S(1)}, bf16[1,56,512]{2,1,0:T(8,128)(2,1)S(1)}, u32[]{:S(2)}, u32[]{:S(2)}) %collective-permute-start.2) | collective-permute-done | bytes 57376 | tf_op jit(solution)/shard_map/ppermute | solution.py:31
  27.6 4.5 %collective-permute-start.15 = (bf16[1,56,640]{2,1,0:T(8,128)(2,1)S(1)}, bf16[1,56,640]{2,1,0:T(8,128)(2,1)S(1)}, u32[]{:S(2)}, u32[]{:S(2)}) collective-permute-start(bf16[1,56,640]{2,1,0:T(8,128)(2,1)S(1)} %fusion.5), channel_id=1, source_target_pairs={{0,8},{1,9},{2,10},{3,11},{4,12},{5,13},{6,14},{7,15},{8,0},{9,1},... | collective-permute-start | bytes 215048 | tf_op jit(solution)/shard_map/ppermute | solution.py:31
  32.1 0.1 collective-permute-start.3
  32.2 4.2 %collective-permute-done.15 = bf16[1,56,640]{2,1,0:T(8,128)(2,1)S(1)} collective-permute-done((bf16[1,56,640]{2,1,0:T(8,128)(2,1)S(1)}, bf16[1,56,640]{2,1,0:T(8,128)(2,1)S(1)}, u32[]{:S(2)}, u32[]{:S(2)}) %collective-permute-start.15) | collective-permute-done | bytes 71712 | tf_op jit(solution)/shard_map/ppermute | solution.py:31
  36.4 0.1 pad_maximum_fusion
  36.5 2.4 %collective-permute-start.16 = (bf16[7,56,640]{2,1,0:T(8,128)(2,1)S(1)}, bf16[7,56,640]{2,1,0:T(8,128)(2,1)S(1)}, u32[]{:S(2)}, u32[]{:S(2)}) collective-permute-start(bf16[7,56,640]{2,1,0:T(8,128)(2,1)S(1)} %pad_maximum_fusion), channel_id=1, source_target_pairs={{0,1},{1,0},{2,3},{3,2},{4,5},{5,4},{6,7},{7,6},{8,9},{9,8},{10,11... | collective-permute-start | bytes 1505288 | tf_op jit(solution)/shard_map/ppermute | solution.py:20
  39.0 1.4 collective-permute-done.16
  40.4 0.1 select_dynamic-update-slice_fusion.1
  40.6 0.1 select_dynamic-update-slice_fusion
  40.8 1.3 collective-permute-start.17
  42.2 0.0 copy-start.8
  42.2 0.1 pad_maximum_fusion.1.refs_0_
  42.3 2.0 %collective-permute-start.4 = (bf16[4,2,56,512]{3,2,1,0:T(8,128)(2,1)S(1)}, bf16[4,2,56,512]{3,2,1,0:T(8,128)(2,1)}, u32[]{:S(2)}, u32[]{:S(2)}) collective-permute-start(bf16[4,2,56,512]{3,2,1,0:T(8,128)(2,1)S(1)} %pad_maximum_fusion.1.refs_0_), channel_id=1, source_target_pairs={{0,2},{1,15},{2,4},{3,1},{4,6},{5,3},{6,8},{7,5},{8,10},{9,7},{10,... | collective-permute-start | bytes 1376264 | tf_op jit(solution)/shard_map/ppermute | solution.py:31
  44.3 8.4 %collective-permute-done.4.refs_1_ = bf16[4,2,56,512]{3,2,1,0:T(8,128)(2,1)} collective-permute-done((bf16[4,2,56,512]{3,2,1,0:T(8,128)(2,1)S(1)}, bf16[4,2,56,512]{3,2,1,0:T(8,128)(2,1)}, u32[]{:S(2)}, u32[]{:S(2)}) %collective-permute-start.4) | collective-permute-done | bytes 458784 | tf_op jit(solution)/shard_map/ppermute | solution.py:31
  52.7 3.1 %collective-permute-start.5 = (bf16[4,2,56,512]{3,2,1,0:T(8,128)(2,1)}, bf16[4,2,56,512]{3,2,1,0:T(8,128)(2,1)}, u32[]{:S(2)}, u32[]{:S(2)}) collective-permute-start(bf16[4,2,56,512]{3,2,1,0:T(8,128)(2,1)} %collective-permute-done.4.refs_1_), channel_id=1, source_target_pairs={{0,2},{1,15},{2,4},{3,1},{4,6},{5,3},{6,8},{7,5},{8,10},{9,7},{10,... | collective-permute-start | bytes 1376264 | tf_op jit(solution)/shard_map/ppermute | solution.py:31
  55.8 0.2 collective-permute-done.17.refs_10_
  56.0 0.1 constant_dynamic-slice_fusion
  56.1 2.4 %collective-permute-start.18 = (bf16[4,2,56,640]{3,2,1,0:T(8,128)(2,1)S(1)}, bf16[4,2,56,640]{3,2,1,0:T(8,128)(2,1)S(1)}, u32[]{:S(2)}, u32[]{:S(2)}) collective-permute-start(bf16[4,2,56,640]{3,2,1,0:T(8,128)(2,1)S(1)} %constant_dynamic-slice_fusion), channel_id=1, source_target_pairs={{0,16},{1,49},{2,18},{3,51},{4,20},{5,53},{6,22},{7,55},{8,24},{9,... | collective-permute-start | bytes 1720328 | tf_op jit(solution)/shard_map/ppermute | solution.py:31
  58.5 0.4 collective-permute-start.19
  58.9 2.7 %collective-permute-done.5.refs_2_ = bf16[4,2,56,512]{3,2,1,0:T(8,128)(2,1)} collective-permute-done((bf16[4,2,56,512]{3,2,1,0:T(8,128)(2,1)}, bf16[4,2,56,512]{3,2,1,0:T(8,128)(2,1)}, u32[]{:S(2)}, u32[]{:S(2)}) %collective-permute-start.5) | collective-permute-done | bytes 458784 | tf_op jit(solution)/shard_map/ppermute | solution.py:31
  61.6 3.1 %collective-permute-start.6 = (bf16[4,2,56,512]{3,2,1,0:T(8,128)(2,1)}, bf16[4,2,56,512]{3,2,1,0:T(8,128)(2,1)S(1)}, u32[]{:S(2)}, u32[]{:S(2)}) collective-permute-start(bf16[4,2,56,512]{3,2,1,0:T(8,128)(2,1)} %collective-permute-done.5.refs_2_), channel_id=1, source_target_pairs={{0,2},{1,15},{2,4},{3,1},{4,6},{5,3},{6,8},{7,5},{8,10},{9,7},{10,... | collective-permute-start | bytes 1376264 | tf_op jit(solution)/shard_map/ppermute | solution.py:31
  64.7 0.6 collective-permute-start.8
  65.3 5.1 %collective-permute-start.20 = (bf16[4,2,56,640]{3,2,1,0:T(8,128)(2,1)S(1)}, bf16[4,2,56,640]{3,2,1,0:T(8,128)(2,1)S(1)}, u32[]{:S(2)}, u32[]{:S(2)}) collective-permute-start(bf16[4,2,56,640]{3,2,1,0:T(8,128)(2,1)S(1)} %collective-permute-done.18.refs_11_), channel_id=1, source_target_pairs={{0,1},{1,0},{2,3},{3,2},{4,5},{5,4},{6,7},{7,6},{8,9},{9,8},{10,11... | collective-permute-start | bytes 1720328 | tf_op jit(solution)/shard_map/ppermute | solution.py:20
  70.4 9.1 %collective-permute-done.6.refs_3_ = bf16[4,2,56,512]{3,2,1,0:T(8,128)(2,1)S(1)} collective-permute-done((bf16[4,2,56,512]{3,2,1,0:T(8,128)(2,1)}, bf16[4,2,56,512]{3,2,1,0:T(8,128)(2,1)S(1)}, u32[]{:S(2)}, u32[]{:S(2)}) %collective-permute-start.6) | collective-permute-done | bytes 458784 | tf_op jit(solution)/shard_map/ppermute | solution.py:31
  79.5 3.5 %collective-permute-start.7 = (bf16[2,2,56,512]{3,2,1,0:T(8,128)(2,1)S(1)}, bf16[2,2,56,512]{3,2,1,0:T(8,128)(2,1)}, u32[]{:S(2)}, u32[]{:S(2)}) collective-permute-start(bf16[2,2,56,512]{3,2,1,0:T(8,128)(2,1)S(1)} %constant_dynamic-slice_fusion.1), channel_id=1, source_target_pairs={{0,2},{1,15},{2,4},{3,1},{4,6},{5,3},{6,8},{7,5},{8,10},{9,7},{10,... | collective-permute-start | bytes 688136 | tf_op jit(solution)/shard_map/ppermute | solution.py:31
  83.0 1.8 collective-permute-start.10
  84.8 5.6 %collective-permute-done.7.refs_4_ = bf16[2,2,56,512]{3,2,1,0:T(8,128)(2,1)} collective-permute-done((bf16[2,2,56,512]{3,2,1,0:T(8,128)(2,1)S(1)}, bf16[2,2,56,512]{3,2,1,0:T(8,128)(2,1)}, u32[]{:S(2)}, u32[]{:S(2)}) %collective-permute-start.7) | collective-permute-done | bytes 229408 | tf_op jit(solution)/shard_map/ppermute | solution.py:31
  90.4 6.5 %collective-permute-start.11 = (bf16[2,2,56,512]{3,2,1,0:T(8,128)(2,1)}, bf16[2,2,56,512]{3,2,1,0:T(8,128)(2,1)}, u32[]{:S(2)}, u32[]{:S(2)}) collective-permute-start(bf16[2,2,56,512]{3,2,1,0:T(8,128)(2,1)} %collective-permute-done.7.refs_4_), channel_id=1, source_target_pairs={{0,1},{1,0},{2,3},{3,2},{4,5},{5,4},{6,7},{7,6},{8,9},{9,8},{10,11... | collective-permute-start | bytes 688136 | tf_op jit(solution)/shard_map/ppermute | solution.py:20
  96.9 0.7 copy.14
  97.6 0.7 collective-permute-done.11.refs_8_
  98.4 0.8 copy-done.11
  99.2 19.3 %spatial.1.attended = bf16[1152,512]{1,0:T(8,128)(2,1)} custom-call(s32[8]{0:T(128)} %clip_tokens.1, s32[32]{0:T(128)} %block_clip.1, bf16[512,1152]{1,0:T(8,128)(2,1)} %bitcast.43, f32[6,1,1152]{2,1,0:T(1,128)} %bitcast.39, f32[72,4]{1,0:T(8,128)} %bitcast.36, bf16[4,2,56,512]{3,2,1,0:T(8,128)(2,1)} %copy-done.2, ...), custom_call_target="tpu_custom_call" | custom-call | flops 20000000000 | bytes 20000000 | tf_op jit(solution)/shard_map/spatial/pallas_call | solution.py:322
  118.5 0.0 all-gather.3.cloned.1.call-done
  118.5 7.2 %mixing.1 = (bf16[32,72,128]{2,1,0:T(8,128)(2,1)}, bf16[32,72,128]{2,1,0:T(8,128)(2,1)}) custom-call(bf16[512,1152]{1,0:T(8,128)(2,1)} %bitcast.44, f32[6,1,1152]{2,1,0:T(1,128)} %bitcast.40, bf16[1152,512]{1,0:T(8,128)(2,1)} %spatial.1.attended, bf16[64,96,1152]{2,1,0:T(8,128)(2,1)} %bitcast.27), custom_call_target="tpu_custom_call" | custom-call | flops 20000000000 | bytes 20000000 | tf_op jit(solution)/shard_map/mixing/pallas_call | solution.py:335
  125.7 4.4 %all-to-all-start.1 = ((bf16[32,72,128]{2,1,0:T(8,128)(2,1)}), bf16[32,72,128]{2,1,0:T(8,128)(2,1)S(1)}, u32[]{:S(2)}, u32[]{:S(2)}) async-start(bf16[32,72,128]{2,1,0:T(8,128)(2,1)} %get-tuple-element.12), calls=%async_computation.1 | async-start | bytes 1179648 | tf_op jit(solution)/shard_map/all_to_all | solution.py:364
  130.1 1.1 copy.15
  131.3 0.1 eq.29
  131.4 0.1 select_reduce_fusion
  131.4 0.9 and_convert_fusion.allowed
  132.3 9.5 %prepare.1 = (bf16[3456,1152]{1,0:T(8,128)(2,1)}, bf16[1152,1152]{1,0:T(8,128)(2,1)}) custom-call(bf16[64,96,1152]{2,1,0:T(8,128)(2,1)} %bitcast.28), custom_call_target="tpu_custom_call" | custom-call | bytes 30000000 | tf_op jit(solution)/shard_map/prepare/pallas_call | solution.py:349
  141.8 3.8 %all-to-all-done.1.received = bf16[32,72,128]{2,1,0:T(8,128)(2,1)S(1)} async-done(((bf16[32,72,128]{2,1,0:T(8,128)(2,1)}), bf16[32,72,128]{2,1,0:T(8,128)(2,1)S(1)}, u32[]{:S(2)}, u32[]{:S(2)}) %all-to-all-start.1) | async-done | bytes 589856 | tf_op jit(solution)/shard_map/all_to_all | solution.py:364
  145.7 8.3 %all-to-all-start = ((bf16[32,72,128]{2,1,0:T(8,128)(2,1)}), bf16[32,72,128]{2,1,0:T(8,128)(2,1)S(1)}, u32[]{:S(2)}, u32[]{:S(2)}) async-start(bf16[32,72,128]{2,1,0:T(8,128)(2,1)} %get-tuple-element.9), calls=%async_computation | async-start | bytes 1179648 | tf_op jit(solution)/shard_map/all_to_all | solution.py:364
  154.0 14.9 %temporal.3 = f32[16,256]{1,0:T(8,128)} custom-call(bf16[32,72,128]{2,1,0:T(8,128)(2,1)} %copy-done, f32[1152,6]{1,0:T(8,128)} %bitcast.29, f32[72,4]{1,0:T(8,128)} %bitcast.37, f32[256,256]{1,0:T(8,128)} %and_convert_fusion.allowed, bf16[16,1152]{1,0:T(8,128)(2,1)} %bitcast.45, bf16[3456,1152]{1,0:T(8,128)(2,1)} %get-tuple-element.10.held_columns, ...), custom_call_target="tpu_custom_call" | custom-call | flops 20000000000 | bytes 20000000 | tf_op jit(solution)/shard_map/temporal/pallas_call | solution.py:366
  168.9 0.6 all-to-all-done.received
  169.5 0.8 copy-done.1
  170.4 14.9 %temporal.2 = f32[16,256]{1,0:T(8,128)} custom-call(bf16[32,72,128]{2,1,0:T(8,128)(2,1)} %copy-done.1, f32[1152,6]{1,0:T(8,128)} %bitcast.30, f32[72,4]{1,0:T(8,128)} %bitcast.38, f32[256,256]{1,0:T(8,128)} %and_convert_fusion.allowed, bf16[16,1152]{1,0:T(8,128)(2,1)} %bitcast.46, bf16[3456,1152]{1,0:T(8,128)(2,1)} %get-tuple-element.10.held_columns, ...), custom_call_target="tpu_custom_call" | custom-call | flops 20000000000 | bytes 20000000 | tf_op jit(solution)/shard_map/temporal/pallas_call | solution.py:366
  185.3 0.7 fusion.9
  186.0 3.9 %collective-permute-start.21 = (f32[8,512]{1,0:T(8,128)S(1)}, f32[8,512]{1,0:T(8,128)S(1)}, u32[]{:S(2)}, u32[]{:S(2)}) collective-permute-start(f32[8,512]{1,0:T(8,128)S(1)} %fusion.9), channel_id=1, source_target_pairs={{0,1},{1,0},{2,3},{3,2},{4,5},{5,4},{6,7},{7,6},{8,9},{9,8},{10,11... | collective-permute-start | bytes 49160 | tf_op jit(solution)/shard_map/ppermute | solution.py:388
  189.9 0.1 broadcast_compare_fusion
  190.0 0.8 collective-permute-done.21
  190.8 0.7 multiply_add_fusion
  191.5 0.1 reshape.70
  191.5 0.7 fusion.6
  (54 shorter events, 0.4 us)
Async XLA Ops:
  6.5 112.0 %all-gather.3.cloned.1.call-start = ((), (), s32[]{:S(2)}) async-start(), calls=%async_computation.2 | async-start | bytes 14376960 | tf_op jit(solution)/shard_map/all_gather | solution.py:313
  9.2 4.3 %collective-permute-start = (bf16[56,1152]{1,0:T(8,128)(2,1)S(1)}, bf16[56,1152]{1,0:T(8,128)(2,1)S(1)}, u32[]{:S(2)}, u32[]{:S(2)}) collective-permute-start(bf16[56,1152]{1,0:T(8,128)(2,1)S(1)} %pad.8), channel_id=1, source_target_pairs={{0,1},{1,0},{2,3},{3,2},{4,5},{5,4},{6,7},{7,6},{8,9},{9,8},{10,11... | collective-permute-start | bytes 387080 | tf_op jit(solution)/shard_map/ppermute | solution.py:20
  14.5 21.9 %collective-permute-start.12 = (bf16[2,56,640]{2,1,0:T(8,128)(2,1)S(1)}, bf16[2,56,640]{2,1,0:T(8,128)(2,1)S(1)}, u32[]{:S(2)}, u32[]{:S(2)}) collective-permute-start(bf16[2,56,640]{2,1,0:T(8,128)(2,1)S(1)} %get-tuple-element.14), channel_id=1, source_target_pairs={{0,2},{1,15},{2,4},{3,1},{4,6},{5,3},{6,8},{7,5},{8,10},{9,7},{10,... | collective-permute-start | bytes 430088 | tf_op jit(solution)/shard_map/ppermute | solution.py:31
  18.4 18.0 %collective-permute-start.13 = (bf16[2,56,640]{2,1,0:T(8,128)(2,1)S(1)}, bf16[2,56,640]{2,1,0:T(8,128)(2,1)S(1)}, u32[]{:S(2)}, u32[]{:S(2)}) collective-permute-start(bf16[2,56,640]{2,1,0:T(8,128)(2,1)S(1)} %get-tuple-element.14), channel_id=1, source_target_pairs={{0,4},{1,13},{2,6},{3,15},{4,8},{5,1},{6,10},{7,3},{8,12},{9,5},{1... | collective-permute-start | bytes 430088 | tf_op jit(solution)/shard_map/ppermute | solution.py:31
  19.6 16.8 %collective-permute-start.14 = (bf16[2,56,640]{2,1,0:T(8,128)(2,1)S(1)}, bf16[2,56,640]{2,1,0:T(8,128)(2,1)S(1)}, u32[]{:S(2)}, u32[]{:S(2)}) collective-permute-start(bf16[2,56,640]{2,1,0:T(8,128)(2,1)S(1)} %get-tuple-element.14), channel_id=1, source_target_pairs={{0,6},{1,11},{2,8},{3,13},{4,10},{5,15},{6,12},{7,1},{8,14},{9,3},... | collective-permute-start | bytes 430088 | tf_op jit(solution)/shard_map/ppermute | solution.py:31
  20.0 12.0 %collective-permute-start.1 = (bf16[2,56,512]{2,1,0:T(8,128)(2,1)S(1)}, bf16[2,56,512]{2,1,0:T(8,128)(2,1)S(1)}, u32[]{:S(2)}, u32[]{:S(2)}) collective-permute-start(bf16[2,56,512]{2,1,0:T(8,128)(2,1)S(1)} %pad_maximum_fusion.4), channel_id=1, source_target_pairs={{0,16},{1,49},{2,18},{3,51},{4,20},{5,53},{6,22},{7,55},{8,24},{9,... | collective-permute-start | bytes 344072 | tf_op jit(solution)/shard_map/ppermute | solution.py:31
  22.6 4.9 %collective-permute-start.2 = (bf16[1,56,512]{2,1,0:T(8,128)(2,1)S(1)}, bf16[1,56,512]{2,1,0:T(8,128)(2,1)S(1)}, u32[]{:S(2)}, u32[]{:S(2)}) collective-permute-start(bf16[1,56,512]{2,1,0:T(8,128)(2,1)S(1)} %fusion.7), channel_id=1, source_target_pairs={{0,32},{1,33},{2,34},{3,35},{4,36},{5,37},{6,38},{7,39},{8,40},{9,... | collective-permute-start | bytes 172040 | tf_op jit(solution)/shard_map/ppermute | solution.py:31
  27.6 8.8 %collective-permute-start.15 = (bf16[1,56,640]{2,1,0:T(8,128)(2,1)S(1)}, bf16[1,56,640]{2,1,0:T(8,128)(2,1)S(1)}, u32[]{:S(2)}, u32[]{:S(2)}) collective-permute-start(bf16[1,56,640]{2,1,0:T(8,128)(2,1)S(1)} %fusion.5), channel_id=1, source_target_pairs={{0,8},{1,9},{2,10},{3,11},{4,12},{5,13},{6,14},{7,15},{8,0},{9,1},... | collective-permute-start | bytes 215048 | tf_op jit(solution)/shard_map/ppermute | solution.py:31
  32.1 7.0 %collective-permute-start.3 = (bf16[3,56,512]{2,1,0:T(8,128)(2,1)S(1)}, bf16[3,56,512]{2,1,0:T(8,128)(2,1)S(1)}, u32[]{:S(2)}, u32[]{:S(2)}) collective-permute-start(bf16[3,56,512]{2,1,0:T(8,128)(2,1)S(1)} %pad_maximum_fusion.2), channel_id=1, source_target_pairs={{0,1},{1,0},{2,3},{3,2},{4,5},{5,4},{6,7},{7,6},{8,9},{9,8},{10,11... | collective-permute-start | bytes 516104 | tf_op jit(solution)/shard_map/ppermute | solution.py:20
  36.5 3.9 %collective-permute-start.16 = (bf16[7,56,640]{2,1,0:T(8,128)(2,1)S(1)}, bf16[7,56,640]{2,1,0:T(8,128)(2,1)S(1)}, u32[]{:S(2)}, u32[]{:S(2)}) collective-permute-start(bf16[7,56,640]{2,1,0:T(8,128)(2,1)S(1)} %pad_maximum_fusion), channel_id=1, source_target_pairs={{0,1},{1,0},{2,3},{3,2},{4,5},{5,4},{6,7},{7,6},{8,9},{9,8},{10,11... | collective-permute-start | bytes 1505288 | tf_op jit(solution)/shard_map/ppermute | solution.py:20
  40.8 15.0 %copy-start.7 = (bf16[16,56,640]{2,1,0:T(8,128)(2,1)}, bf16[16,56,640]{2,1,0:T(8,128)(2,1)S(1)}, u32[]{:S(2)}) copy-start(bf16[16,56,640]{2,1,0:T(8,128)(2,1)S(1)} %select_dynamic-update-slice_fusion.2) | copy-start | bytes 3440644
  40.8 15.2 %collective-permute-start.17 = (bf16[8,2,56,640]{3,2,1,0:T(8,128)(2,1)S(1)}, bf16[8,2,56,640]{3,2,1,0:T(8,128)(2,1)S(1)}, u32[]{:S(2)}, u32[]{:S(2)}) collective-permute-start(bf16[8,2,56,640]{3,2,1,0:T(8,128)(2,1)S(1)} %bitcast.41), channel_id=1, source_target_pairs={{0,16},{1,49},{2,18},{3,51},{4,20},{5,53},{6,22},{7,55},{8,24},{9,... | collective-permute-start | bytes 3440648 | tf_op jit(solution)/shard_map/ppermute | solution.py:31
  42.2 54.7 %copy-start.8 = (f32[4,72]{1,0:T(4,128)S(1)}, f32[4,72]{1,0:T(4,128)}, u32[]{:S(2)}) copy-start(f32[4,72]{1,0:T(4,128)} %param.17) | copy-start | bytes 3460
  42.3 56.1 %copy-start.2 = (bf16[4,2,56,512]{3,2,1,0:T(8,128)(2,1)}, bf16[4,2,56,512]{3,2,1,0:T(8,128)(2,1)S(1)}, u32[]{:S(2)}) copy-start(bf16[4,2,56,512]{3,2,1,0:T(8,128)(2,1)S(1)} %pad_maximum_fusion.1.refs_0_) | copy-start | bytes 1376260
  42.3 10.4 %collective-permute-start.4 = (bf16[4,2,56,512]{3,2,1,0:T(8,128)(2,1)S(1)}, bf16[4,2,56,512]{3,2,1,0:T(8,128)(2,1)}, u32[]{:S(2)}, u32[]{:S(2)}) collective-permute-start(bf16[4,2,56,512]{3,2,1,0:T(8,128)(2,1)S(1)} %pad_maximum_fusion.1.refs_0_), channel_id=1, source_target_pairs={{0,2},{1,15},{2,4},{3,1},{4,6},{5,3},{6,8},{7,5},{8,10},{9,7},{10,... | collective-permute-start | bytes 1376264 | tf_op jit(solution)/shard_map/ppermute | solution.py:31
  52.7 8.9 %collective-permute-start.5 = (bf16[4,2,56,512]{3,2,1,0:T(8,128)(2,1)}, bf16[4,2,56,512]{3,2,1,0:T(8,128)(2,1)}, u32[]{:S(2)}, u32[]{:S(2)}) collective-permute-start(bf16[4,2,56,512]{3,2,1,0:T(8,128)(2,1)} %collective-permute-done.4.refs_1_), channel_id=1, source_target_pairs={{0,2},{1,15},{2,4},{3,1},{4,6},{5,3},{6,8},{7,5},{8,10},{9,7},{10,... | collective-permute-start | bytes 1376264 | tf_op jit(solution)/shard_map/ppermute | solution.py:31
  56.0 42.4 %copy-start.3 = (bf16[8,2,56,640]{3,2,1,0:T(8,128)(2,1)}, bf16[8,2,56,640]{3,2,1,0:T(8,128)(2,1)S(1)}, u32[]{:S(2)}) copy-start(bf16[8,2,56,640]{3,2,1,0:T(8,128)(2,1)S(1)} %collective-permute-done.17.refs_10_) | copy-start | bytes 3440644
  56.1 9.2 %collective-permute-start.18 = (bf16[4,2,56,640]{3,2,1,0:T(8,128)(2,1)S(1)}, bf16[4,2,56,640]{3,2,1,0:T(8,128)(2,1)S(1)}, u32[]{:S(2)}, u32[]{:S(2)}) collective-permute-start(bf16[4,2,56,640]{3,2,1,0:T(8,128)(2,1)S(1)} %constant_dynamic-slice_fusion), channel_id=1, source_target_pairs={{0,16},{1,49},{2,18},{3,51},{4,20},{5,53},{6,22},{7,55},{8,24},{9,... | collective-permute-start | bytes 1720328 | tf_op jit(solution)/shard_map/ppermute | solution.py:31
  58.5 39.9 %collective-permute-start.19 = (bf16[8,2,56,640]{3,2,1,0:T(8,128)(2,1)S(1)}, bf16[8,2,56,640]{3,2,1,0:T(8,128)(2,1)}, u32[]{:S(2)}, u32[]{:S(2)}) collective-permute-start(bf16[8,2,56,640]{3,2,1,0:T(8,128)(2,1)S(1)} %collective-permute-done.17.refs_10_), channel_id=1, source_target_pairs={{0,1},{1,0},{2,3},{3,2},{4,5},{5,4},{6,7},{7,6},{8,9},{9,8},{10,11... | collective-permute-start | bytes 3440648 | tf_op jit(solution)/shard_map/ppermute | solution.py:20
  61.6 17.9 %collective-permute-start.6 = (bf16[4,2,56,512]{3,2,1,0:T(8,128)(2,1)}, bf16[4,2,56,512]{3,2,1,0:T(8,128)(2,1)S(1)}, u32[]{:S(2)}, u32[]{:S(2)}) collective-permute-start(bf16[4,2,56,512]{3,2,1,0:T(8,128)(2,1)} %collective-permute-done.5.refs_2_), channel_id=1, source_target_pairs={{0,2},{1,15},{2,4},{3,1},{4,6},{5,3},{6,8},{7,5},{8,10},{9,7},{10,... | collective-permute-start | bytes 1376264 | tf_op jit(solution)/shard_map/ppermute | solution.py:31
  64.7 18.3 %collective-permute-start.8 = (bf16[4,2,56,512]{3,2,1,0:T(8,128)(2,1)}, bf16[4,2,56,512]{3,2,1,0:T(8,128)(2,1)}, u32[]{:S(2)}, u32[]{:S(2)}) collective-permute-start(bf16[4,2,56,512]{3,2,1,0:T(8,128)(2,1)} %collective-permute-done.4.refs_1_), channel_id=1, source_target_pairs={{0,1},{1,0},{2,3},{3,2},{4,5},{5,4},{6,7},{7,6},{8,9},{9,8},{10,11... | collective-permute-start | bytes 1376264 | tf_op jit(solution)/shard_map/ppermute | solution.py:20
  65.2 32.4 %collective-permute-start.9 = (bf16[4,2,56,512]{3,2,1,0:T(8,128)(2,1)}, bf16[4,2,56,512]{3,2,1,0:T(8,128)(2,1)}, u32[]{:S(2)}, u32[]{:S(2)}) collective-permute-start(bf16[4,2,56,512]{3,2,1,0:T(8,128)(2,1)} %collective-permute-done.5.refs_2_), channel_id=1, source_target_pairs={{0,1},{1,0},{2,3},{3,2},{4,5},{5,4},{6,7},{7,6},{8,9},{9,8},{10,11... | collective-permute-start | bytes 1376264 | tf_op jit(solution)/shard_map/ppermute | solution.py:20
  65.3 33.2 %copy-start.10 = (bf16[4,2,56,640]{3,2,1,0:T(8,128)(2,1)}, bf16[4,2,56,640]{3,2,1,0:T(8,128)(2,1)S(1)}, u32[]{:S(2)}) copy-start(bf16[4,2,56,640]{3,2,1,0:T(8,128)(2,1)S(1)} %collective-permute-done.18.refs_11_) | copy-start | bytes 1720324
  65.3 33.1 %collective-permute-start.20 = (bf16[4,2,56,640]{3,2,1,0:T(8,128)(2,1)S(1)}, bf16[4,2,56,640]{3,2,1,0:T(8,128)(2,1)S(1)}, u32[]{:S(2)}, u32[]{:S(2)}) collective-permute-start(bf16[4,2,56,640]{3,2,1,0:T(8,128)(2,1)S(1)} %collective-permute-done.18.refs_11_), channel_id=1, source_target_pairs={{0,1},{1,0},{2,3},{3,2},{4,5},{5,4},{6,7},{7,6},{8,9},{9,8},{10,11... | collective-permute-start | bytes 1720328 | tf_op jit(solution)/shard_map/ppermute | solution.py:20
  79.5 19.0 %copy-start.4 = (bf16[4,2,56,512]{3,2,1,0:T(8,128)(2,1)}, bf16[4,2,56,512]{3,2,1,0:T(8,128)(2,1)S(1)}, u32[]{:S(2)}) copy-start(bf16[4,2,56,512]{3,2,1,0:T(8,128)(2,1)S(1)} %collective-permute-done.6.refs_3_) | copy-start | bytes 1376260
  79.5 10.9 %collective-permute-start.7 = (bf16[2,2,56,512]{3,2,1,0:T(8,128)(2,1)S(1)}, bf16[2,2,56,512]{3,2,1,0:T(8,128)(2,1)}, u32[]{:S(2)}, u32[]{:S(2)}) collective-permute-start(bf16[2,2,56,512]{3,2,1,0:T(8,128)(2,1)S(1)} %constant_dynamic-slice_fusion.1), channel_id=1, source_target_pairs={{0,2},{1,15},{2,4},{3,1},{4,6},{5,3},{6,8},{7,5},{8,10},{9,7},{10,... | collective-permute-start | bytes 688136 | tf_op jit(solution)/shard_map/ppermute | solution.py:31
  83.0 15.4 %collective-permute-start.10 = (bf16[4,2,56,512]{3,2,1,0:T(8,128)(2,1)S(1)}, bf16[4,2,56,512]{3,2,1,0:T(8,128)(2,1)}, u32[]{:S(2)}, u32[]{:S(2)}) collective-permute-start(bf16[4,2,56,512]{3,2,1,0:T(8,128)(2,1)S(1)} %collective-permute-done.6.refs_3_), channel_id=1, source_target_pairs={{0,1},{1,0},{2,3},{3,2},{4,5},{5,4},{6,7},{7,6},{8,9},{9,8},{10,11... | collective-permute-start | bytes 1376264 | tf_op jit(solution)/shard_map/ppermute | solution.py:20
  90.4 8.0 %collective-permute-start.11 = (bf16[2,2,56,512]{3,2,1,0:T(8,128)(2,1)}, bf16[2,2,56,512]{3,2,1,0:T(8,128)(2,1)}, u32[]{:S(2)}, u32[]{:S(2)}) collective-permute-start(bf16[2,2,56,512]{3,2,1,0:T(8,128)(2,1)} %collective-permute-done.7.refs_4_), channel_id=1, source_target_pairs={{0,1},{1,0},{2,3},{3,2},{4,5},{5,4},{6,7},{7,6},{8,9},{9,8},{10,11... | collective-permute-start | bytes 688136 | tf_op jit(solution)/shard_map/ppermute | solution.py:20
  98.4 0.8 copy-start.11
  125.7 4.4 %copy-start.6 = (f32[1,6,1152]{2,0,1:T(1,128)S(1)}, f32[1,6,1152]{2,0,1:T(1,128)}, u32[]{:S(2)}) copy-start(f32[1,6,1152]{2,0,1:T(1,128)} %param.11) | copy-start | bytes 82948
  125.7 5.6 %copy-start.9 = (s32[32]{0:T(128)S(1)}, s32[32]{0:T(128)}, u32[]{:S(2)}) copy-start(s32[32]{0:T(128)} %block_clip.1) | copy-start | bytes 388
  125.7 5.7 %copy-start.12 = (s32[8]{0:T(128)S(1)}, s32[8]{0:T(128)}, u32[]{:S(2)}) copy-start(s32[8]{0:T(128)} %clip_tokens.1) | copy-start | bytes 100
  125.7 20.0 %all-to-all-start.1 = ((bf16[32,72,128]{2,1,0:T(8,128)(2,1)}), bf16[32,72,128]{2,1,0:T(8,128)(2,1)S(1)}, u32[]{:S(2)}, u32[]{:S(2)}) async-start(bf16[32,72,128]{2,1,0:T(8,128)(2,1)} %get-tuple-element.12), calls=%async_computation.1 | async-start | bytes 1179648 | tf_op jit(solution)/shard_map/all_to_all | solution.py:364
  145.7 8.3 %copy-start = (bf16[32,72,128]{2,1,0:T(8,128)(2,1)}, bf16[32,72,128]{2,1,0:T(8,128)(2,1)S(1)}, u32[]{:S(2)}) copy-start(bf16[32,72,128]{2,1,0:T(8,128)(2,1)S(1)} %all-to-all-done.1.received) | copy-start | bytes 1769476
  145.7 23.9 %all-to-all-start = ((bf16[32,72,128]{2,1,0:T(8,128)(2,1)}), bf16[32,72,128]{2,1,0:T(8,128)(2,1)S(1)}, u32[]{:S(2)}, u32[]{:S(2)}) async-start(bf16[32,72,128]{2,1,0:T(8,128)(2,1)} %get-tuple-element.9), calls=%async_computation | async-start | bytes 1179648 | tf_op jit(solution)/shard_map/all_to_all | solution.py:364
  168.9 16.4 %copy-start.5 = (f32[16,256]{1,0:T(8,128)S(1)}, f32[16,256]{1,0:T(8,128)}, u32[]{:S(2)}) copy-start(f32[16,256]{1,0:T(8,128)} %temporal.3) | copy-start | bytes 49156
  169.5 0.8 copy-start.1
  186.0 4.8 %collective-permute-start.21 = (f32[8,512]{1,0:T(8,128)S(1)}, f32[8,512]{1,0:T(8,128)S(1)}, u32[]{:S(2)}, u32[]{:S(2)}) collective-permute-start(f32[8,512]{1,0:T(8,128)S(1)} %fusion.9), channel_id=1, source_target_pairs={{0,1},{1,0},{2,3},{3,2},{4,5},{5,4},{6,7},{7,6},{8,9},{9,8},{10,11... | collective-permute-start | bytes 49160 | tf_op jit(solution)/shard_map/ppermute | solution.py:388
Sparse Core Ops, SparseCore 0:
  10.1 101.7 all-gather.2

commit v5 on v3

--- a/solution.py
+++ b/solution.py
@@ -12,7 +12,7 @@
 F32 = jnp.float32
 LANES = 128
 TEMPORAL_ROWS = 256
-X_RING, Z_RING, SPLIT = 4, 8, 512
+X_RING, Z_RING, SPLIT = 4, 8, 384
 X_SLOTS = (0, -1, 1, 2)
 Z_SLOTS = (0, -1, -2, -3, 1, 2, 3, 4)
 
@@ -45,22 +45,26 @@
     near = [plane_step(second, False, far) for far in (1, 2, 3)]
     near.append(plane_step(own_half(second), False, 4))
     mine = jnp.concatenate([plane_step(first, True), plane_step(own_half(first), True, 2)])
+    started = jnp.concatenate([mine[:1], mine[2:]], axis=2)
     theirs = swap_cores(mine)
     low, high = in_core_order(core, mine[:2], theirs[:2])
     opposite = jnp.concatenate(in_core_order(core, mine[2:], theirs[2:]))
-    rows = [jnp.stack([first, low, high, opposite])]
+    row = jnp.stack([first, low, high, opposite])
+    rows = [row]
     for _ in range(3):
         rows.append(plane_step(rows[-1], False))
-    mine = jnp.concatenate(near)
+    mine = jnp.concatenate(near) + started * jnp.zeros((), BF16)
     theirs = swap_cores(mine)
     low, high = in_core_order(core, mine[:6], theirs[:6])
     opposite = jnp.concatenate(in_core_order(core, mine[6:], theirs[6:]))
     ring = jnp.concatenate([second, low, high, opposite]).reshape((Z_RING,) + second.shape)
     across = plane_step(ring, True)
-    beyond = plane_step(lax.dynamic_slice_in_dim(across, 4 * core, 4, 0), True)
+    second_step = jnp.concatenate([rows[2]] * 2, axis=3) * jnp.zeros((), BF16)
+    beyond = plane_step(lax.dynamic_slice_in_dim(across, 4 * core, 4, 0) + second_step, True)
     rows.append(plane_step(lax.dynamic_slice_in_dim(rows[3], 2 * core, 2, 0), False))
+    last_step = jnp.concatenate([jnp.concatenate([rows[4]] * 2, axis=3)] * 2) * jnp.zeros((), BF16)
     rows += [swap_cores(part) for part in rows[1:]]
-    return rows, [ring, across, beyond, swap_cores(across), swap_cores(beyond)]
+    return rows, [ring, across, beyond, swap_cores(across), swap_cores(beyond + last_step)]
 
 
 def pick(table, index):
@@ -210,10 +214,23 @@
                 ]
 
 
-def temporal_kernel(head_size, received, levels, gains, allowed, w_final, gathered, predicted,
-                    landing, columns, normed, projected, out_rows, attended, by_frame, by_slot, sem):
+def prepare_kernel(head_size, gathered, columns, out_rows, landing, sem):
     arriving = pltpu.make_async_copy(gathered.at[:, pl.ds(0, landing.shape[1]), :], landing, sem)
     arriving.start()
+    arriving.wait()
+    share = 3 * head_size // 4
+    lay_out(landing, columns, 0, share)
+    lay_out(landing, out_rows, share, head_size // 4)
+
+
+def temporal_kernel(head_size, received, levels, gains, allowed, w_final, held_columns, held_rows, predicted,
+                    columns, normed, projected, out_rows, attended, by_frame, by_slot, sems):
+    arriving = [
+        pltpu.make_async_copy(held_columns, columns, sems.at[0]),
+        pltpu.make_async_copy(held_rows, out_rows, sems.at[1]),
+    ]
+    for copy in arriving:
+        copy.start()
     frames = received.shape[0]
     width, row_count = normed.shape
     locations = row_count // frames
@@ -233,12 +250,10 @@
         chunk = slice(start, start + LANES)
         values_in = layer_norm(by_slot[:, chunk].astype(F32), 0)
         normed[:, chunk] = (values_in * (1.0 + levels[:, 4:5]) + levels[:, 3:4]).astype(BF16)
-    arriving.wait()
-    share = 3 * head_size // 4
-    lay_out(landing, columns, 0, share)
-    lay_out(landing, out_rows, share, head_size // 4)
+    arriving[0].wait()
     project(columns, normed, projected)
     attend(projected, attended, gains, 2, None, allowed, head_size)
+    arriving[1].wait()
     projected[0:width, :] = jnp.dot(out_rows[...], attended[...], preferred_element_type=F32)
     for start in range(0, row_count, LANES):
         chunk = slice(start, start + LANES)
@@ -247,9 +262,8 @@
     predicted[...] = jnp.dot(w_final[...], normed[...], preferred_element_type=F32)
 
 
-def projection_scratch(landing_shape, rows, width):
+def projection_scratch(rows, width):
     return [
-        pltpu.VMEM(landing_shape, BF16),
         pltpu.VMEM((3 * width, width), BF16),
         pltpu.VMEM((width, rows), BF16),
         pltpu.VMEM((3 * width, rows), F32),
@@ -300,7 +314,8 @@
         out_shape=jax.ShapeDtypeStruct((width, rows), BF16),
         in_specs=[smem, smem, vmem, vmem, vmem] + [anywhere] * 14,
         out_specs=vmem,
-        scratch_shapes=projection_scratch((shards,) + first_rows.shape, rows, width)
+        scratch_shapes=[pltpu.VMEM((shards,) + first_rows.shape, BF16)]
+        + projection_scratch(rows, width)
         + [pltpu.SemaphoreType.DMA],
         compiler_params=params,
         cost_estimate=cost,
@@ -321,23 +336,36 @@
         name="mixing",
     )(tokens[0], levels, attended, gathered)
     received = lax.all_to_all(residual, "seq", split_axis=0, concat_axis=0, tiled=True)
+    held = pl.pallas_call(
+        functools.partial(prepare_kernel, head_size),
+        out_shape=[
+            jax.ShapeDtypeStruct((3 * width, width), BF16),
+            jax.ShapeDtypeStruct((width, width), BF16),
+        ],
+        in_specs=[anywhere],
+        out_specs=[vmem] * 2,
+        scratch_shapes=[pltpu.VMEM((shards, 80, width), BF16), pltpu.SemaphoreType.DMA],
+        compiler_params=params,
+        cost_estimate=pl.CostEstimate(flops=0, bytes_accessed=30_000_000, transcendentals=0),
+        name="prepare",
+    )(gathered)
     predicted = pl.pallas_call(
         functools.partial(temporal_kernel, head_size),
         out_shape=jax.ShapeDtypeStruct((w_final.shape[1], rows), F32),
-        in_specs=[vmem] * 5 + [anywhere],
+        in_specs=[vmem] * 5 + [anywhere] * 2,
         out_specs=vmem,
-        scratch_shapes=projection_scratch((shards, 80, width), rows, width)
+        scratch_shapes=projection_scratch(rows, width)
         + [
             pltpu.VMEM((width, width), BF16),
             pltpu.VMEM((width, rows), BF16),
             pltpu.VMEM((rows, width), BF16),
             pltpu.VMEM((width, rows), BF16),
-            pltpu.SemaphoreType.DMA,
+            pltpu.SemaphoreType.DMA((2,)),
         ],
         compiler_params=params,
         cost_estimate=cost,
         name="temporal",
-    )(received, modulation[0].T, gains, allowed, w_final.T, gathered)
+    )(received, modulation[0].T, gains, allowed, w_final.T, *held)
 
     half = predicted.shape[0] // 2
     outgoing = lax.dynamic_slice_in_dim(predicted, (1 - branch_index) * half, half, 0)

time: 199 us -> 200 us (level)
  starting transfers between devices: 58.5 us -> 50.1 us
  Pallas kernels: 50.9 us -> 58.1 us
  other arithmetic: 5.72 us -> 11.1 us
  waiting for transfers between devices: 63.5 us -> 60.9 us
    all_to_all x1, waiting for transfers between devices: 25 us -> 15.5 us  [body(): lax.all_to_all(residual, 'seq', split_axis=0, concat_axis=0, tiled=True)]
    pallas_call x0 -> x1, Pallas kernels: none -> 9.51 us  [body(): pl.pallas_call(functools.partial(prepare_kernel, head_size), out_shape=[j...]
    ppermute x12, starting transfers between devices: 28.6 us -> 21.3 us  [plane_step(): return lax.ppermute(array, ('seq', 'cfg'), pairs)]
    ppermute x12, waiting for transfers between devices: 34.4 us -> 38.3 us  [plane_step(): return lax.ppermute(array, ('seq', 'cfg'), pairs)]
    ppermute x9, waiting for transfers between devices: 3.23 us -> 6.32 us  [swap_cores(): return lax.ppermute(array, 'cfg', [(0, 1), (1, 0)])]
    unnamed x4, other arithmetic: 0.35 us -> 3.22 us
    ppermute x9, starting transfers between devices: 20.1 us -> 17.3 us  [swap_cores(): return lax.ppermute(array, 'cfg', [(0, 1), (1, 0)])]
    pallas_call x1, Pallas kernels: 24.3 us -> 21.9 us  [body(): pl.pallas_call(functools.partial(temporal_kernel, head_size), out_shape=j...]
  transfers between devices with their start and end apart: 24 -> 24, of which waited for: 12 -> 14; matrix products, arithmetic and copies ran while one was open for 3% -> 6% of each run, Pallas kernels for 10% -> 14%
where the time goes in v5:
time: 200 us
  waiting for transfers between devices  60.9 us (30%)
  Pallas kernels  58.1 us (29%)
  starting transfers between devices  50.1 us (25%)
  between operations  13.6 us (7%)
  other arithmetic  11.1 us (6%)
  local copies, waits for them, and re-layouts  5.63 us (3%)
    ppermute x12, waiting for transfers between devices, plane_step(): return lax.ppermute(array, ('seq', 'cfg'), pairs)  38.3 us
    pallas_call x1, Pallas kernels, body(): pl.pallas_call(functools.partial(temporal_kernel, head_size), out_shape=j...  21.9 us
    ppermute x12, starting transfers between devices, plane_step(): return lax.ppermute(array, ('seq', 'cfg'), pairs)  21.3 us
    pallas_call x1, Pallas kernels, body(): pl.pallas_call(functools.partial(spatial_kernel, head_size), out_shape=ja...  19.3 us
    ppermute x9, starting transfers between devices, swap_cores(): return lax.ppermute(array, 'cfg', [(0, 1), (1, 0)])  17.3 us
    all_to_all x1, waiting for transfers between devices, body(): lax.all_to_all(residual, 'seq', split_axis=0, concat_axis=0, tiled=True)  15.5 us
    pallas_call x1, Pallas kernels, body(): pl.pallas_call(functools.partial(prepare_kernel, head_size), out_shape=[j...  9.51 us
    pallas_call x1, Pallas kernels, body(): pl.pallas_call(functools.partial(mixing_kernel, head_size), out_shape=jax...  7.46 us
  transfers between devices with their start and end apart: 24, of which 14 were waited for; matrix products, arithmetic and copies ran while one was open for 6% of the time, Pallas kernels for 14%

profile of v5, /device:TPU:1, one launch (start us, length us, event | category | flops | bytes accessed | tf_op | source)
XLA Modules:
  0.0 199.5 jit_solution(12271572256986578578)
XLA Ops:
  6.5 1.7 fusion.6
  8.3 0.9 pad.8
  9.2 3.3 %collective-permute-start = (bf16[56,1152]{1,0:T(8,128)(2,1)S(1)}, bf16[56,1152]{1,0:T(8,128)(2,1)S(1)}, u32[]{:S(2)}, u32[]{:S(2)}) collective-permute-start(bf16[56,1152]{1,0:T(8,128)(2,1)S(1)} %pad.8), channel_id=1, source_target_pairs={{0,1},{1,0},{2,3},{3,2},{4,5},{5,4},{6,7},{7,6},{8,9},{9,8},{10,11... | collective-permute-start | bytes 387080 | tf_op jit(solution)/shard_map/ppermute | solution.py:20
  12.5 1.0 collective-permute-done
  13.5 1.0 select_bitcast_fusion
  14.4 0.7 constant_dynamic-update-slice_fusion
  15.1 3.8 %collective-permute-start.12 = (bf16[2,56,768]{2,1,0:T(8,128)(2,1)S(1)}, bf16[2,56,768]{2,1,0:T(8,128)(2,1)S(1)}, u32[]{:S(2)}, u32[]{:S(2)}) collective-permute-start(bf16[2,56,768]{2,1,0:T(8,128)(2,1)S(1)} %get-tuple-element.10), channel_id=1, source_target_pairs={{0,2},{1,15},{2,4},{3,1},{4,6},{5,3},{6,8},{7,5},{8,10},{9,7},{10,... | collective-permute-start | bytes 516104 | tf_op jit(solution)/shard_map/ppermute | solution.py:31
  19.0 1.2 collective-permute-start.13
  20.1 0.4 collective-permute-start.14
  20.6 2.8 %collective-permute-start.2 = (bf16[1,56,384]{2,1,0:T(8,128)(2,1)S(1)}, bf16[1,56,384]{2,1,0:T(8,128)(2,1)S(1)}, u32[]{:S(2)}, u32[]{:S(2)}) collective-permute-start(bf16[1,56,384]{2,1,0:T(8,128)(2,1)S(1)} %fusion.9), channel_id=1, source_target_pairs={{0,32},{1,33},{2,34},{3,35},{4,36},{5,37},{6,38},{7,39},{8,40},{9,... | collective-permute-start | bytes 129032 | tf_op jit(solution)/shard_map/ppermute | solution.py:31
  23.5 0.9 collective-permute-start.1
  24.4 2.4 %collective-permute-done.1 = bf16[2,56,384]{2,1,0:T(8,128)(2,1)S(1)} collective-permute-done((bf16[2,56,384]{2,1,0:T(8,128)(2,1)S(1)}, bf16[2,56,384]{2,1,0:T(8,128)(2,1)S(1)}, u32[]{:S(2)}, u32[]{:S(2)}) %collective-permute-start.1) | collective-permute-done | bytes 86048 | tf_op jit(solution)/shard_map/ppermute | solution.py:31
  26.9 4.8 %collective-permute-start.15 = (bf16[1,56,768]{2,1,0:T(8,128)(2,1)S(1)}, bf16[1,56,768]{2,1,0:T(8,128)(2,1)S(1)}, u32[]{:S(2)}, u32[]{:S(2)}) collective-permute-start(bf16[1,56,768]{2,1,0:T(8,128)(2,1)S(1)} %fusion.7), channel_id=1, source_target_pairs={{0,8},{1,9},{2,10},{3,11},{4,12},{5,13},{6,14},{7,15},{8,0},{9,1},... | collective-permute-start | bytes 258056 | tf_op jit(solution)/shard_map/ppermute | solution.py:31
  31.7 4.6 %collective-permute-done.15 = bf16[1,56,768]{2,1,0:T(8,128)(2,1)S(1)} collective-permute-done((bf16[1,56,768]{2,1,0:T(8,128)(2,1)S(1)}, bf16[1,56,768]{2,1,0:T(8,128)(2,1)S(1)}, u32[]{:S(2)}, u32[]{:S(2)}) %collective-permute-start.15) | collective-permute-done | bytes 86048 | tf_op jit(solution)/shard_map/ppermute | solution.py:31
  36.3 0.1 maximum_add_fusion
  36.4 5.4 %collective-permute-start.16 = (bf16[7,56,768]{2,1,0:T(8,128)(2,1)S(1)}, bf16[7,56,768]{2,1,0:T(8,128)(2,1)S(1)}, u32[]{:S(2)}, u32[]{:S(2)}) collective-permute-start(bf16[7,56,768]{2,1,0:T(8,128)(2,1)S(1)} %maximum_add_fusion), channel_id=1, source_target_pairs={{0,1},{1,0},{2,3},{3,2},{4,5},{5,4},{6,7},{7,6},{8,9},{9,8},{10,11... | collective-permute-start | bytes 1806344 | tf_op jit(solution)/shard_map/ppermute | solution.py:20
  41.8 0.1 collective-permute-start.3
  41.9 1.5 collective-permute-done.16
  43.4 0.9 select_dynamic-update-slice_fusion.1
  44.4 0.9 select_dynamic-update-slice_fusion
  45.3 0.6 select_dynamic-update-slice_fusion.3
  46.0 0.6 select_dynamic-update-slice_fusion.2
  46.7 0.1 pad_maximum_fusion.refs_0_
  46.8 1.6 collective-permute-start.4
  48.4 7.0 %collective-permute-done.4.refs_1_ = bf16[4,2,56,384]{3,2,1,0:T(8,128)(2,1)S(1)} collective-permute-done((bf16[4,2,56,384]{3,2,1,0:T(8,128)(2,1)S(1)}, bf16[4,2,56,384]{3,2,1,0:T(8,128)(2,1)S(1)}, u32[]{:S(2)}, u32[]{:S(2)}) %collective-permute-start.4) | collective-permute-done | bytes 344096 | tf_op jit(solution)/shard_map/ppermute | solution.py:31
  55.4 1.6 collective-permute-start.5
  57.0 4.8 %collective-permute-done.5.refs_2_ = bf16[4,2,56,384]{3,2,1,0:T(8,128)(2,1)S(1)} collective-permute-done((bf16[4,2,56,384]{3,2,1,0:T(8,128)(2,1)S(1)}, bf16[4,2,56,384]{3,2,1,0:T(8,128)(2,1)S(1)}, u32[]{:S(2)}, u32[]{:S(2)}) %collective-permute-start.5) | collective-permute-done | bytes 344096 | tf_op jit(solution)/shard_map/ppermute | solution.py:31
  61.8 2.5 %collective-permute-done.17.refs_10_ = bf16[8,2,56,768]{3,2,1,0:T(8,128)(2,1)S(1)} collective-permute-done((bf16[8,2,56,768]{3,2,1,0:T(8,128)(2,1)}, bf16[8,2,56,768]{3,2,1,0:T(8,128)(2,1)S(1)}, u32[]{:S(2)}, u32[]{:S(2)}) %collective-permute-start.17) | collective-permute-done | bytes 1376288 | tf_op jit(solution)/shard_map/ppermute | solution.py:31
  64.3 0.2 fusion
  64.5 1.3 collective-permute-start.18
  65.8 1.2 collective-permute-start.6
  67.0 1.4 collective-permute-start.19
  68.5 11.1 %collective-permute-done.6.refs_3_ = bf16[4,2,56,384]{3,2,1,0:T(8,128)(2,1)} collective-permute-done((bf16[4,2,56,384]{3,2,1,0:T(8,128)(2,1)S(1)}, bf16[4,2,56,384]{3,2,1,0:T(8,128)(2,1)}, u32[]{:S(2)}, u32[]{:S(2)}) %collective-permute-start.6) | collective-permute-done | bytes 344096 | tf_op jit(solution)/shard_map/ppermute | solution.py:31
  79.6 0.9 constant_dynamic-slice_fusion.1
  80.5 1.5 collective-permute-start.7
  82.0 3.9 %collective-permute-done.7.refs_4_ = bf16[2,2,56,384]{3,2,1,0:T(8,128)(2,1)} collective-permute-done((bf16[2,2,56,384]{3,2,1,0:T(8,128)(2,1)S(1)}, bf16[2,2,56,384]{3,2,1,0:T(8,128)(2,1)}, u32[]{:S(2)}, u32[]{:S(2)}) %collective-permute-start.7) | collective-permute-done | bytes 172064 | tf_op jit(solution)/shard_map/ppermute | solution.py:31
  85.9 1.9 collective-permute-done.18.refs_11_
  87.9 1.6 fusion.1
  89.5 6.1 %collective-permute-start.20 = (bf16[4,2,56,768]{3,2,1,0:T(8,128)(2,1)S(1)}, bf16[4,2,56,768]{3,2,1,0:T(8,128)(2,1)}, u32[]{:S(2)}, u32[]{:S(2)}) collective-permute-start(bf16[4,2,56,768]{3,2,1,0:T(8,128)(2,1)S(1)} %fusion.1), channel_id=1, source_target_pairs={{0,1},{1,0},{2,3},{3,2},{4,5},{5,4},{6,7},{7,6},{8,9},{9,8},{10,11... | collective-permute-start | bytes 2064392 | tf_op jit(solution)/shard_map/ppermute | solution.py:20
  95.6 0.1 collective-permute-start.8
  95.7 0.4 collective-permute-start.9
  96.1 0.1 collective-permute-start.10
  96.2 3.1 %collective-permute-done.8.refs_5_ = bf16[4,2,56,384]{3,2,1,0:T(8,128)(2,1)S(1)} collective-permute-done((bf16[4,2,56,384]{3,2,1,0:T(8,128)(2,1)S(1)}, bf16[4,2,56,384]{3,2,1,0:T(8,128)(2,1)S(1)}, u32[]{:S(2)}, u32[]{:S(2)}) %collective-permute-start.8) | collective-permute-done | bytes 344096 | tf_op jit(solution)/shard_map/ppermute | solution.py:20
  99.3 0.4 collective-permute-start.11
  99.7 0.7 copy.14
  100.4 0.7 collective-permute-done.11.refs_8_
  101.2 19.3 %spatial.1.attended = bf16[1152,512]{1,0:T(8,128)(2,1)} custom-call(s32[8]{0:T(128)} %clip_tokens.1, s32[32]{0:T(128)} %block_clip.1, bf16[512,1152]{1,0:T(8,128)(2,1)} %bitcast.43, f32[6,1,1152]{2,1,0:T(1,128)} %bitcast.41, f32[72,4]{1,0:T(8,128)} %bitcast.39, bf16[4,2,56,384]{3,2,1,0:T(8,128)(2,1)} %copy-done.3, bf16[4,2,56,384]{3,2,1,0:T(8,128)(2,1)} %copy-done.8, ...), custom_call_target="tpu_custom_call" | custom-call | flops 20000000000 | bytes 20000000 | tf_op jit(solution)/shard_map/spatial/pallas_call | solution.py:312
  120.5 7.5 %mixing.1 = bf16[32,144,128]{2,1,0:T(8,128)(2,1)} custom-call(bf16[512,1152]{1,0:T(8,128)(2,1)} %bitcast.44, f32[6,1,1152]{2,1,0:T(1,128)} %bitcast.42, bf16[1152,512]{1,0:T(8,128)(2,1)} %spatial.1.attended, bf16[64,96,1152]{2,1,0:T(8,128)(2,1)} %bitcast.30), custom_call_target="tpu_custom_call" | custom-call | flops 20000000000 | bytes 20000000 | tf_op jit(solution)/shard_map/mixing/pallas_call | solution.py:324
  128.0 6.6 %all-to-all-start = ((bf16[32,144,128]{2,1,0:T(8,128)(2,1)}), bf16[32,144,128]{2,1,0:T(8,128)(2,1)S(1)}, u32[]{:S(2)}, u32[]{:S(2)}) async-start(bf16[32,144,128]{2,1,0:T(8,128)(2,1)} %mixing.1), calls=%async_computation | async-start | bytes 2359296 | tf_op jit(solution)/shard_map/all_to_all | solution.py:338
  134.6 1.1 copy.15
  135.7 0.1 eq.29
  135.8 0.1 select_reduce_fusion
  135.9 0.9 and_convert_fusion.allowed
  136.8 9.5 %prepare.1 = (bf16[3456,1152]{1,0:T(8,128)(2,1)}, bf16[1152,1152]{1,0:T(8,128)(2,1)}) custom-call(bf16[64,96,1152]{2,1,0:T(8,128)(2,1)} %bitcast.31), custom_call_target="tpu_custom_call" | custom-call | bytes 30000000 | tf_op jit(solution)/shard_map/prepare/pallas_call | solution.py:339
  146.3 15.5 %all-to-all-done.received = bf16[32,144,128]{2,1,0:T(8,128)(2,1)S(1)} async-done(((bf16[32,144,128]{2,1,0:T(8,128)(2,1)}), bf16[32,144,128]{2,1,0:T(8,128)(2,1)S(1)}, u32[]{:S(2)}, u32[]{:S(2)}) %all-to-all-start) | async-done | bytes 1179680 | tf_op jit(solution)/shard_map/all_to_all | solution.py:338
  161.8 1.0 copy-done
  162.8 21.9 %temporal.1 = f32[16,512]{1,0:T(8,128)} custom-call(bf16[32,144,128]{2,1,0:T(8,128)(2,1)} %copy-done, f32[1152,6]{1,0:T(8,128)} %bitcast.32, f32[72,4]{1,0:T(8,128)} %bitcast.40, f32[256,256]{1,0:T(8,128)} %and_convert_fusion.allowed, bf16[16,1152]{1,0:T(8,128)(2,1)} %bitcast.45, bf16[3456,1152]{1,0:T(8,128)(2,1)} %get-tuple-element.7.held_columns, ...), custom_call_target="tpu_custom_call" | custom-call | flops 20000000000 | bytes 20000000 | tf_op jit(solution)/shard_map/temporal/pallas_call | solution.py:352
  184.7 0.7 constant_dynamic-slice_fusion
  185.4 4.9 %collective-permute-start.21 = (f32[8,512]{1,0:T(8,128)S(1)}, f32[8,512]{1,0:T(8,128)S(1)}, u32[]{:S(2)}, u32[]{:S(2)}) collective-permute-start(f32[8,512]{1,0:T(8,128)S(1)} %constant_dynamic-slice_fusion), channel_id=1, source_target_pairs={{0,1},{1,0},{2,3},{3,2},{4,5},{5,4},{6,7},{7,6},{8,9},{9,8},{10,11... | collective-permute-start | bytes 49160 | tf_op jit(solution)/shard_map/ppermute | solution.py:372
  190.4 0.1 broadcast_compare_fusion
  190.4 0.8 collective-permute-done.21
  191.2 0.7 multiply_add_fusion
  191.9 0.1 reshape.88
  192.0 0.7 fusion.8
  (49 shorter events, 0.3 us)
Async XLA Ops:
  6.5 113.9 %all-gather.3.cloned.1.call-start = ((), (), s32[]{:S(2)}) async-start(), calls=%async_computation.1 | async-start | bytes 14376960 | tf_op jit(solution)/shard_map/all_gather | solution.py:303
  9.2 4.3 %collective-permute-start = (bf16[56,1152]{1,0:T(8,128)(2,1)S(1)}, bf16[56,1152]{1,0:T(8,128)(2,1)S(1)}, u32[]{:S(2)}, u32[]{:S(2)}) collective-permute-start(bf16[56,1152]{1,0:T(8,128)(2,1)S(1)} %pad.8), channel_id=1, source_target_pairs={{0,1},{1,0},{2,3},{3,2},{4,5},{5,4},{6,7},{7,6},{8,9},{9,8},{10,11... | collective-permute-start | bytes 387080 | tf_op jit(solution)/shard_map/ppermute | solution.py:20
  15.1 21.2 %collective-permute-start.12 = (bf16[2,56,768]{2,1,0:T(8,128)(2,1)S(1)}, bf16[2,56,768]{2,1,0:T(8,128)(2,1)S(1)}, u32[]{:S(2)}, u32[]{:S(2)}) collective-permute-start(bf16[2,56,768]{2,1,0:T(8,128)(2,1)S(1)} %get-tuple-element.10), channel_id=1, source_target_pairs={{0,2},{1,15},{2,4},{3,1},{4,6},{5,3},{6,8},{7,5},{8,10},{9,7},{10,... | collective-permute-start | bytes 516104 | tf_op jit(solution)/shard_map/ppermute | solution.py:31
  19.0 17.4 %collective-permute-start.13 = (bf16[2,56,768]{2,1,0:T(8,128)(2,1)S(1)}, bf16[2,56,768]{2,1,0:T(8,128)(2,1)S(1)}, u32[]{:S(2)}, u32[]{:S(2)}) collective-permute-start(bf16[2,56,768]{2,1,0:T(8,128)(2,1)S(1)} %get-tuple-element.10), channel_id=1, source_target_pairs={{0,4},{1,13},{2,6},{3,15},{4,8},{5,1},{6,10},{7,3},{8,12},{9,5},{1... | collective-permute-start | bytes 516104 | tf_op jit(solution)/shard_map/ppermute | solution.py:31
  20.1 16.2 %collective-permute-start.14 = (bf16[2,56,768]{2,1,0:T(8,128)(2,1)S(1)}, bf16[2,56,768]{2,1,0:T(8,128)(2,1)S(1)}, u32[]{:S(2)}, u32[]{:S(2)}) collective-permute-start(bf16[2,56,768]{2,1,0:T(8,128)(2,1)S(1)} %get-tuple-element.10), channel_id=1, source_target_pairs={{0,6},{1,11},{2,8},{3,13},{4,10},{5,15},{6,12},{7,1},{8,14},{9,3},... | collective-permute-start | bytes 516104 | tf_op jit(solution)/shard_map/ppermute | solution.py:31
  20.6 11.0 %collective-permute-start.2 = (bf16[1,56,384]{2,1,0:T(8,128)(2,1)S(1)}, bf16[1,56,384]{2,1,0:T(8,128)(2,1)S(1)}, u32[]{:S(2)}, u32[]{:S(2)}) collective-permute-start(bf16[1,56,384]{2,1,0:T(8,128)(2,1)S(1)} %fusion.9), channel_id=1, source_target_pairs={{0,32},{1,33},{2,34},{3,35},{4,36},{5,37},{6,38},{7,39},{8,40},{9,... | collective-permute-start | bytes 129032 | tf_op jit(solution)/shard_map/ppermute | solution.py:31
  23.5 3.4 %collective-permute-start.1 = (bf16[2,56,384]{2,1,0:T(8,128)(2,1)S(1)}, bf16[2,56,384]{2,1,0:T(8,128)(2,1)S(1)}, u32[]{:S(2)}, u32[]{:S(2)}) collective-permute-start(bf16[2,56,384]{2,1,0:T(8,128)(2,1)S(1)} %pad_maximum_fusion.3), channel_id=1, source_target_pairs={{0,16},{1,49},{2,18},{3,51},{4,20},{5,53},{6,22},{7,55},{8,24},{9,... | collective-permute-start | bytes 258056 | tf_op jit(solution)/shard_map/ppermute | solution.py:31
  26.9 9.4 %collective-permute-start.15 = (bf16[1,56,768]{2,1,0:T(8,128)(2,1)S(1)}, bf16[1,56,768]{2,1,0:T(8,128)(2,1)S(1)}, u32[]{:S(2)}, u32[]{:S(2)}) collective-permute-start(bf16[1,56,768]{2,1,0:T(8,128)(2,1)S(1)} %fusion.7), channel_id=1, source_target_pairs={{0,8},{1,9},{2,10},{3,11},{4,12},{5,13},{6,14},{7,15},{8,0},{9,1},... | collective-permute-start | bytes 258056 | tf_op jit(solution)/shard_map/ppermute | solution.py:31
  36.4 7.0 %collective-permute-start.16 = (bf16[7,56,768]{2,1,0:T(8,128)(2,1)S(1)}, bf16[7,56,768]{2,1,0:T(8,128)(2,1)S(1)}, u32[]{:S(2)}, u32[]{:S(2)}) collective-permute-start(bf16[7,56,768]{2,1,0:T(8,128)(2,1)S(1)} %maximum_add_fusion), channel_id=1, source_target_pairs={{0,1},{1,0},{2,3},{3,2},{4,5},{5,4},{6,7},{7,6},{8,9},{9,8},{10,11... | collective-permute-start | bytes 1806344 | tf_op jit(solution)/shard_map/ppermute | solution.py:20
  41.8 4.8 %collective-permute-start.3 = (bf16[3,56,384]{2,1,0:T(8,128)(2,1)S(1)}, bf16[3,56,384]{2,1,0:T(8,128)(2,1)S(1)}, u32[]{:S(2)}, u32[]{:S(2)}) collective-permute-start(bf16[3,56,384]{2,1,0:T(8,128)(2,1)S(1)} %pad_maximum_fusion.2), channel_id=1, source_target_pairs={{0,1},{1,0},{2,3},{3,2},{4,5},{5,4},{6,7},{7,6},{8,9},{9,8},{10,11... | collective-permute-start | bytes 387080 | tf_op jit(solution)/shard_map/ppermute | solution.py:20
  46.6 17.7 %collective-permute-start.17 = (bf16[8,2,56,768]{3,2,1,0:T(8,128)(2,1)}, bf16[8,2,56,768]{3,2,1,0:T(8,128)(2,1)S(1)}, u32[]{:S(2)}, u32[]{:S(2)}) collective-permute-start(bf16[8,2,56,768]{3,2,1,0:T(8,128)(2,1)} %bitcast.12.refs_9_), channel_id=1, source_target_pairs={{0,16},{1,49},{2,18},{3,51},{4,20},{5,53},{6,22},{7,55},{8,24},{9,... | collective-permute-start | bytes 4128776 | tf_op jit(solution)/shard_map/ppermute | solution.py:31
  46.8 42.7 %copy-start.3 = (bf16[4,2,56,384]{3,2,1,0:T(8,128)(2,1)}, bf16[4,2,56,384]{3,2,1,0:T(8,128)(2,1)S(1)}, u32[]{:S(2)}) copy-start(bf16[4,2,56,384]{3,2,1,0:T(8,128)(2,1)S(1)} %pad_maximum_fusion.refs_0_) | copy-start | bytes 1032196
  46.8 8.6 %collective-permute-start.4 = (bf16[4,2,56,384]{3,2,1,0:T(8,128)(2,1)S(1)}, bf16[4,2,56,384]{3,2,1,0:T(8,128)(2,1)S(1)}, u32[]{:S(2)}, u32[]{:S(2)}) collective-permute-start(bf16[4,2,56,384]{3,2,1,0:T(8,128)(2,1)S(1)} %pad_maximum_fusion.refs_0_), channel_id=1, source_target_pairs={{0,2},{1,15},{2,4},{3,1},{4,6},{5,3},{6,8},{7,5},{8,10},{9,7},{10,... | collective-permute-start | bytes 1032200 | tf_op jit(solution)/shard_map/ppermute | solution.py:31
  55.4 8.9 %copy-start.8 = (bf16[4,2,56,384]{3,2,1,0:T(8,128)(2,1)}, bf16[4,2,56,384]{3,2,1,0:T(8,128)(2,1)S(1)}, u32[]{:S(2)}) copy-start(bf16[4,2,56,384]{3,2,1,0:T(8,128)(2,1)S(1)} %collective-permute-done.4.refs_1_) | copy-start | bytes 1032196
  55.4 6.4 %collective-permute-start.5 = (bf16[4,2,56,384]{3,2,1,0:T(8,128)(2,1)S(1)}, bf16[4,2,56,384]{3,2,1,0:T(8,128)(2,1)S(1)}, u32[]{:S(2)}, u32[]{:S(2)}) collective-permute-start(bf16[4,2,56,384]{3,2,1,0:T(8,128)(2,1)S(1)} %collective-permute-done.4.refs_1_), channel_id=1, source_target_pairs={{0,2},{1,15},{2,4},{3,1},{4,6},{5,3},{6,8},{7,5},{8,10},{9,7},{10,... | collective-permute-start | bytes 1032200 | tf_op jit(solution)/shard_map/ppermute | solution.py:31
  61.8 33.9 %copy-start.4 = (bf16[4,2,56,384]{3,2,1,0:T(8,128)(2,1)}, bf16[4,2,56,384]{3,2,1,0:T(8,128)(2,1)S(1)}, u32[]{:S(2)}) copy-start(bf16[4,2,56,384]{3,2,1,0:T(8,128)(2,1)S(1)} %collective-permute-done.5.refs_2_) | copy-start | bytes 1032196
  64.3 25.2 %copy-start.2 = (bf16[8,2,56,768]{3,2,1,0:T(8,128)(2,1)}, bf16[8,2,56,768]{3,2,1,0:T(8,128)(2,1)S(1)}, u32[]{:S(2)}) copy-start(bf16[8,2,56,768]{3,2,1,0:T(8,128)(2,1)S(1)} %collective-permute-done.17.refs_10_) | copy-start | bytes 4128772
  64.5 35.2 %copy-start.6 = (f32[4,72]{1,0:T(4,128)S(1)}, f32[4,72]{1,0:T(4,128)}, u32[]{:S(2)}) copy-start(f32[4,72]{1,0:T(4,128)} %param.17) | copy-start | bytes 3460
  64.5 23.4 %collective-permute-start.18 = (bf16[4,2,56,768]{3,2,1,0:T(8,128)(2,1)S(1)}, bf16[4,2,56,768]{3,2,1,0:T(8,128)(2,1)S(1)}, u32[]{:S(2)}, u32[]{:S(2)}) collective-permute-start(bf16[4,2,56,768]{3,2,1,0:T(8,128)(2,1)S(1)} %fusion), channel_id=1, source_target_pairs={{0,16},{1,49},{2,18},{3,51},{4,20},{5,53},{6,22},{7,55},{8,24},{9,... | collective-permute-start | bytes 2064392 | tf_op jit(solution)/shard_map/ppermute | solution.py:31
  65.8 13.8 %collective-permute-start.6 = (bf16[4,2,56,384]{3,2,1,0:T(8,128)(2,1)S(1)}, bf16[4,2,56,384]{3,2,1,0:T(8,128)(2,1)}, u32[]{:S(2)}, u32[]{:S(2)}) collective-permute-start(bf16[4,2,56,384]{3,2,1,0:T(8,128)(2,1)S(1)} %collective-permute-done.5.refs_2_), channel_id=1, source_target_pairs={{0,2},{1,15},{2,4},{3,1},{4,6},{5,3},{6,8},{7,5},{8,10},{9,7},{10,... | collective-permute-start | bytes 1032200 | tf_op jit(solution)/shard_map/ppermute | solution.py:31
  67.0 34.1 %collective-permute-start.19 = (bf16[8,2,56,768]{3,2,1,0:T(8,128)(2,1)S(1)}, bf16[8,2,56,768]{3,2,1,0:T(8,128)(2,1)}, u32[]{:S(2)}, u32[]{:S(2)}) collective-permute-start(bf16[8,2,56,768]{3,2,1,0:T(8,128)(2,1)S(1)} %collective-permute-done.17.refs_10_), channel_id=1, source_target_pairs={{0,1},{1,0},{2,3},{3,2},{4,5},{5,4},{6,7},{7,6},{8,9},{9,8},{10,11... | collective-permute-start | bytes 4128776 | tf_op jit(solution)/shard_map/ppermute | solution.py:20
  68.5 27.1 %copy-start.9 = (bf16[4,2,56,384]{3,2,1,0:T(8,128)(2,1)S(1)}, bf16[4,2,56,384]{3,2,1,0:T(8,128)(2,1)}, u32[]{:S(2)}) copy-start(bf16[4,2,56,384]{3,2,1,0:T(8,128)(2,1)} %copy-done.8) | copy-start | bytes 1032196
  80.5 5.4 %collective-permute-start.7 = (bf16[2,2,56,384]{3,2,1,0:T(8,128)(2,1)S(1)}, bf16[2,2,56,384]{3,2,1,0:T(8,128)(2,1)}, u32[]{:S(2)}, u32[]{:S(2)}) collective-permute-start(bf16[2,2,56,384]{3,2,1,0:T(8,128)(2,1)S(1)} %constant_dynamic-slice_fusion.1), channel_id=1, source_target_pairs={{0,2},{1,15},{2,4},{3,1},{4,6},{5,3},{6,8},{7,5},{8,10},{9,7},{10,... | collective-permute-start | bytes 516104 | tf_op jit(solution)/shard_map/ppermute | solution.py:31
  87.9 13.3 %copy-start.1 = (bf16[4,2,56,768]{3,2,1,0:T(8,128)(2,1)}, bf16[4,2,56,768]{3,2,1,0:T(8,128)(2,1)S(1)}, u32[]{:S(2)}) copy-start(bf16[4,2,56,768]{3,2,1,0:T(8,128)(2,1)S(1)} %collective-permute-done.18.refs_11_) | copy-start | bytes 2064388
  89.5 11.6 %collective-permute-start.20 = (bf16[4,2,56,768]{3,2,1,0:T(8,128)(2,1)S(1)}, bf16[4,2,56,768]{3,2,1,0:T(8,128)(2,1)}, u32[]{:S(2)}, u32[]{:S(2)}) collective-permute-start(bf16[4,2,56,768]{3,2,1,0:T(8,128)(2,1)S(1)} %fusion.1), channel_id=1, source_target_pairs={{0,1},{1,0},{2,3},{3,2},{4,5},{5,4},{6,7},{7,6},{8,9},{9,8},{10,11... | collective-permute-start | bytes 2064392 | tf_op jit(solution)/shard_map/ppermute | solution.py:20
  95.6 3.7 %collective-permute-start.8 = (bf16[4,2,56,384]{3,2,1,0:T(8,128)(2,1)S(1)}, bf16[4,2,56,384]{3,2,1,0:T(8,128)(2,1)S(1)}, u32[]{:S(2)}, u32[]{:S(2)}) collective-permute-start(bf16[4,2,56,384]{3,2,1,0:T(8,128)(2,1)S(1)} %copy-done.9), channel_id=1, source_target_pairs={{0,1},{1,0},{2,3},{3,2},{4,5},{5,4},{6,7},{7,6},{8,9},{9,8},{10,11... | collective-permute-start | bytes 1032200 | tf_op jit(solution)/shard_map/ppermute | solution.py:20
  95.7 4.7 %collective-permute-start.9 = (bf16[4,2,56,384]{3,2,1,0:T(8,128)(2,1)S(1)}, bf16[4,2,56,384]{3,2,1,0:T(8,128)(2,1)}, u32[]{:S(2)}, u32[]{:S(2)}) collective-permute-start(bf16[4,2,56,384]{3,2,1,0:T(8,128)(2,1)S(1)} %collective-permute-done.5.refs_2_), channel_id=1, source_target_pairs={{0,1},{1,0},{2,3},{3,2},{4,5},{5,4},{6,7},{7,6},{8,9},{9,8},{10,11... | collective-permute-start | bytes 1032200 | tf_op jit(solution)/shard_map/ppermute | solution.py:20
  96.1 5.0 %collective-permute-start.10 = (bf16[4,2,56,384]{3,2,1,0:T(8,128)(2,1)}, bf16[4,2,56,384]{3,2,1,0:T(8,128)(2,1)}, u32[]{:S(2)}, u32[]{:S(2)}) collective-permute-start(bf16[4,2,56,384]{3,2,1,0:T(8,128)(2,1)} %collective-permute-done.6.refs_3_), channel_id=1, source_target_pairs={{0,1},{1,0},{2,3},{3,2},{4,5},{5,4},{6,7},{7,6},{8,9},{9,8},{10,11... | collective-permute-start | bytes 1032200 | tf_op jit(solution)/shard_map/ppermute | solution.py:20
  99.3 1.8 copy-start.10
  99.3 1.8 collective-permute-start.11
  128.0 6.7 %copy-start.5 = (f32[1,6,1152]{2,0,1:T(1,128)S(1)}, f32[1,6,1152]{2,0,1:T(1,128)}, u32[]{:S(2)}) copy-start(f32[1,6,1152]{2,0,1:T(1,128)} %param.11) | copy-start | bytes 82948
  128.0 7.7 %copy-start.7 = (s32[32]{0:T(128)S(1)}, s32[32]{0:T(128)}, u32[]{:S(2)}) copy-start(s32[32]{0:T(128)} %block_clip.1) | copy-start | bytes 388
  128.0 7.8 %copy-start.11 = (s32[8]{0:T(128)S(1)}, s32[8]{0:T(128)}, u32[]{:S(2)}) copy-start(s32[8]{0:T(128)} %clip_tokens.1) | copy-start | bytes 100
  128.0 33.8 %all-to-all-start = ((bf16[32,144,128]{2,1,0:T(8,128)(2,1)}), bf16[32,144,128]{2,1,0:T(8,128)(2,1)S(1)}, u32[]{:S(2)}, u32[]{:S(2)}) async-start(bf16[32,144,128]{2,1,0:T(8,128)(2,1)} %mixing.1), calls=%async_computation | async-start | bytes 2359296 | tf_op jit(solution)/shard_map/all_to_all | solution.py:338
  161.8 1.0 copy-start
  185.4 5.8 %collective-permute-start.21 = (f32[8,512]{1,0:T(8,128)S(1)}, f32[8,512]{1,0:T(8,128)S(1)}, u32[]{:S(2)}, u32[]{:S(2)}) collective-permute-start(f32[8,512]{1,0:T(8,128)S(1)} %constant_dynamic-slice_fusion), channel_id=1, source_target_pairs={{0,1},{1,0},{2,3},{3,2},{4,5},{5,4},{6,7},{7,6},{8,9},{9,8},{10,11... | collective-permute-start | bytes 49160 | tf_op jit(solution)/shard_map/ppermute | solution.py:372
Sparse Core Ops, SparseCore 0:
  10.1 106.4 all-gather.2

commit v6 on v5

--- a/solution.py
+++ b/solution.py
@@ -12,7 +12,7 @@
 F32 = jnp.float32
 LANES = 128
 TEMPORAL_ROWS = 256
-X_RING, Z_RING, SPLIT = 4, 8, 384
+X_RING, Z_RING, SPLIT = 4, 8, 512
 X_SLOTS = (0, -1, 1, 2)
 Z_SLOTS = (0, -1, -2, -3, 1, 2, 3, 4)
 
@@ -45,7 +45,6 @@
     near = [plane_step(second, False, far) for far in (1, 2, 3)]
     near.append(plane_step(own_half(second), False, 4))
     mine = jnp.concatenate([plane_step(first, True), plane_step(own_half(first), True, 2)])
-    started = jnp.concatenate([mine[:1], mine[2:]], axis=2)
     theirs = swap_cores(mine)
     low, high = in_core_order(core, mine[:2], theirs[:2])
     opposite = jnp.concatenate(in_core_order(core, mine[2:], theirs[2:]))
@@ -53,18 +52,16 @@
     rows = [row]
     for _ in range(3):
         rows.append(plane_step(rows[-1], False))
-    mine = jnp.concatenate(near) + started * jnp.zeros((), BF16)
+    mine = jnp.concatenate(near)
     theirs = swap_cores(mine)
     low, high = in_core_order(core, mine[:6], theirs[:6])
     opposite = jnp.concatenate(in_core_order(core, mine[6:], theirs[6:]))
     ring = jnp.concatenate([second, low, high, opposite]).reshape((Z_RING,) + second.shape)
     across = plane_step(ring, True)
-    second_step = jnp.concatenate([rows[2]] * 2, axis=3) * jnp.zeros((), BF16)
-    beyond = plane_step(lax.dynamic_slice_in_dim(across, 4 * core, 4, 0) + second_step, True)
+    beyond = plane_step(lax.dynamic_slice_in_dim(across, 4 * core, 4, 0), True)
     rows.append(plane_step(lax.dynamic_slice_in_dim(rows[3], 2 * core, 2, 0), False))
-    last_step = jnp.concatenate([jnp.concatenate([rows[4]] * 2, axis=3)] * 2) * jnp.zeros((), BF16)
     rows += [swap_cores(part) for part in rows[1:]]
-    return rows, [ring, across, beyond, swap_cores(across), swap_cores(beyond + last_step)]
+    return rows, [ring, across, beyond, swap_cores(across), swap_cores(beyond)]
 
 
 def pick(table, index):
@@ -303,6 +300,7 @@
     gathered = lax.all_gather(later_rows, ("seq", "cfg"), axis=0, tiled=False)
     shards = gathered.shape[0]
     row_parts, ring_parts = spread_in_plane(first_rows, branch_index)
+    small = pltpu.CompilerParams(vmem_limit_bytes=40 * 2**20)
     params = pltpu.CompilerParams(vmem_limit_bytes=58 * 2**20)
     vmem = pl.BlockSpec(memory_space=pltpu.VMEM)
     smem = pl.BlockSpec(memory_space=pltpu.SMEM)
@@ -317,7 +315,7 @@
         scratch_shapes=[pltpu.VMEM((shards,) + first_rows.shape, BF16)]
         + projection_scratch(rows, width)
         + [pltpu.SemaphoreType.DMA],
-        compiler_params=params,
+        compiler_params=small,
         cost_estimate=cost,
         name="spatial",
     )(clip_tokens, block_clip, tokens[0], levels, gains, *row_parts, *ring_parts)

time: 200 us -> 196 us (0.980)
  starting transfers between devices: 50.1 us -> 59.5 us
  waiting for transfers between devices: 60.9 us -> 51.8 us
  other arithmetic: 11.1 us -> 5.75 us
  local copies, waits for them, and re-layouts: 5.63 us -> 8.32 us
  Pallas kernels: 58.1 us -> 55.8 us
    ppermute x12, starting transfers between devices: 21.3 us -> 28.6 us  [plane_step(): return lax.ppermute(array, ('seq', 'cfg'), pairs)]
    ppermute x12, waiting for transfers between devices: 38.3 us -> 32 us  [plane_step(): return lax.ppermute(array, ('seq', 'cfg'), pairs)]
    ppermute x9, starting transfers between devices: 17.3 us -> 21 us  [swap_cores(): return lax.ppermute(array, 'cfg', [(0, 1), (1, 0)])]
    unnamed x4, other arithmetic: 3.22 us -> 0.35 us
    ppermute x9, waiting for transfers between devices: 6.32 us -> 3.54 us  [swap_cores(): return lax.ppermute(array, 'cfg', [(0, 1), (1, 0)])]
    unnamed x26, local copies, waits for them, and re-layouts: 2.87 us -> 5.6 us
    pallas_call x1, Pallas kernels: 19.3 us -> 16.9 us  [body(): pl.pallas_call(functools.partial(spatial_kernel, head_size), out_shape=ja...]
  transfers between devices with their start and end apart: 24 -> 24, of which waited for: 14 -> 13; matrix products, arithmetic and copies ran while one was open for 6% -> 3% of each run, Pallas kernels for 14% -> 14%
where the time goes in v6:
time: 196 us; the launch traced here: 195 us
  starting transfers between devices  59.5 us (30%)
  Pallas kernels  55.8 us (28%)
  waiting for transfers between devices  51.8 us (26%)
  between operations  13.7 us (7%)
  local copies, waits for them, and re-layouts  8.32 us (4%)
  other arithmetic  5.75 us (3%)
    ppermute x12, waiting for transfers between devices, plane_step(): return lax.ppermute(array, ('seq', 'cfg'), pairs)  32 us
    ppermute x12, starting transfers between devices, plane_step(): return lax.ppermute(array, ('seq', 'cfg'), pairs)  28.6 us
    pallas_call x1, Pallas kernels, body(): pl.pallas_call(functools.partial(temporal_kernel, head_size), out_shape=j...  21.9 us
    ppermute x9, starting transfers between devices, swap_cores(): return lax.ppermute(array, 'cfg', [(0, 1), (1, 0)])  21 us
    pallas_call x1, Pallas kernels, body(): pl.pallas_call(functools.partial(spatial_kernel, head_size), out_shape=ja...  16.9 us
    all_to_all x1, waiting for transfers between devices, body(): lax.all_to_all(residual, 'seq', split_axis=0, concat_axis=0, tiled=True)  15.5 us
    pallas_call x1, Pallas kernels, body(): pl.pallas_call(functools.partial(prepare_kernel, head_size), out_shape=[j...  9.52 us
    pallas_call x1, Pallas kernels, body(): pl.pallas_call(functools.partial(mixing_kernel, head_size), out_shape=jax...  7.43 us
  transfers between devices with their start and end apart: 24, of which 13 were waited for; matrix products, arithmetic and copies ran while one was open for 3% of the time, Pallas kernels for 14%

profile of v6, /device:TPU:1, one launch (start us, length us, event | category | flops | bytes accessed | tf_op | source)
XLA Modules:
  0.0 194.8 jit_solution(16428365218860040740)
XLA Ops:
  6.5 1.7 fusion.4
  8.2 0.0 all-gather.3.cloned.1.call-update
  8.3 0.9 pad.8
  9.2 3.3 %collective-permute-start = (bf16[56,1152]{1,0:T(8,128)(2,1)S(1)}, bf16[56,1152]{1,0:T(8,128)(2,1)S(1)}, u32[]{:S(2)}, u32[]{:S(2)}) collective-permute-start(bf16[56,1152]{1,0:T(8,128)(2,1)S(1)} %pad.8), channel_id=1, source_target_pairs={{0,1},{1,0},{2,3},{3,2},{4,5},{5,4},{6,7},{7,6},{8,9},{9,8},{10,11... | collective-permute-start | bytes 387080 | tf_op jit(solution)/shard_map/ppermute | solution.py:20
  12.5 1.0 collective-permute-done
  13.5 1.0 select_bitcast_fusion
  14.5 3.9 %collective-permute-start.12 = (bf16[2,56,640]{2,1,0:T(8,128)(2,1)S(1)}, bf16[2,56,640]{2,1,0:T(8,128)(2,1)S(1)}, u32[]{:S(2)}, u32[]{:S(2)}) collective-permute-start(bf16[2,56,640]{2,1,0:T(8,128)(2,1)S(1)} %get-tuple-element.10), channel_id=1, source_target_pairs={{0,2},{1,15},{2,4},{3,1},{4,6},{5,3},{6,8},{7,5},{8,10},{9,7},{10,... | collective-permute-start | bytes 430088 | tf_op jit(solution)/shard_map/ppermute | solution.py:31
  18.4 1.2 collective-permute-start.13
  19.6 0.4 collective-permute-start.14
  20.0 2.6 %collective-permute-start.1 = (bf16[2,56,512]{2,1,0:T(8,128)(2,1)S(1)}, bf16[2,56,512]{2,1,0:T(8,128)(2,1)S(1)}, u32[]{:S(2)}, u32[]{:S(2)}) collective-permute-start(bf16[2,56,512]{2,1,0:T(8,128)(2,1)S(1)} %pad_maximum_fusion.4), channel_id=1, source_target_pairs={{0,16},{1,49},{2,18},{3,51},{4,20},{5,53},{6,22},{7,55},{8,24},{9,... | collective-permute-start | bytes 344072 | tf_op jit(solution)/shard_map/ppermute | solution.py:31
  22.7 0.6 collective-permute-start.2
  23.3 4.3 %collective-permute-done.2 = bf16[1,56,512]{2,1,0:T(8,128)(2,1)S(1)} collective-permute-done((bf16[1,56,512]{2,1,0:T(8,128)(2,1)S(1)}, bf16[1,56,512]{2,1,0:T(8,128)(2,1)S(1)}, u32[]{:S(2)}, u32[]{:S(2)}) %collective-permute-start.2) | collective-permute-done | bytes 57376 | tf_op jit(solution)/shard_map/ppermute | solution.py:31
  27.6 4.5 %collective-permute-start.15 = (bf16[1,56,640]{2,1,0:T(8,128)(2,1)S(1)}, bf16[1,56,640]{2,1,0:T(8,128)(2,1)S(1)}, u32[]{:S(2)}, u32[]{:S(2)}) collective-permute-start(bf16[1,56,640]{2,1,0:T(8,128)(2,1)S(1)} %fusion.5), channel_id=1, source_target_pairs={{0,8},{1,9},{2,10},{3,11},{4,12},{5,13},{6,14},{7,15},{8,0},{9,1},... | collective-permute-start | bytes 215048 | tf_op jit(solution)/shard_map/ppermute | solution.py:31
  32.1 0.1 collective-permute-start.3
  32.2 4.2 %collective-permute-done.15 = bf16[1,56,640]{2,1,0:T(8,128)(2,1)S(1)} collective-permute-done((bf16[1,56,640]{2,1,0:T(8,128)(2,1)S(1)}, bf16[1,56,640]{2,1,0:T(8,128)(2,1)S(1)}, u32[]{:S(2)}, u32[]{:S(2)}) %collective-permute-start.15) | collective-permute-done | bytes 71712 | tf_op jit(solution)/shard_map/ppermute | solution.py:31
  36.4 0.1 pad_maximum_fusion
  36.5 2.5 %collective-permute-start.16 = (bf16[7,56,640]{2,1,0:T(8,128)(2,1)S(1)}, bf16[7,56,640]{2,1,0:T(8,128)(2,1)S(1)}, u32[]{:S(2)}, u32[]{:S(2)}) collective-permute-start(bf16[7,56,640]{2,1,0:T(8,128)(2,1)S(1)} %pad_maximum_fusion), channel_id=1, source_target_pairs={{0,1},{1,0},{2,3},{3,2},{4,5},{5,4},{6,7},{7,6},{8,9},{9,8},{10,11... | collective-permute-start | bytes 1505288 | tf_op jit(solution)/shard_map/ppermute | solution.py:20
  39.1 1.4 collective-permute-done.16
  40.5 0.1 select_dynamic-update-slice_fusion.1
  40.6 0.1 select_dynamic-update-slice_fusion
  40.8 1.3 collective-permute-start.17
  42.2 0.0 copy-start.1
  42.2 0.1 pad_maximum_fusion.1.refs_0_
  42.3 2.0 %collective-permute-start.4 = (bf16[4,2,56,512]{3,2,1,0:T(8,128)(2,1)S(1)}, bf16[4,2,56,512]{3,2,1,0:T(8,128)(2,1)S(1)}, u32[]{:S(2)}, u32[]{:S(2)}) collective-permute-start(bf16[4,2,56,512]{3,2,1,0:T(8,128)(2,1)S(1)} %pad_maximum_fusion.1.refs_0_), channel_id=1, source_target_pairs={{0,2},{1,15},{2,4},{3,1},{4,6},{5,3},{6,8},{7,5},{8,10},{9,7},{10,... | collective-permute-start | bytes 1376264 | tf_op jit(solution)/shard_map/ppermute | solution.py:31
  44.3 8.4 %collective-permute-done.4.refs_1_ = bf16[4,2,56,512]{3,2,1,0:T(8,128)(2,1)S(1)} collective-permute-done((bf16[4,2,56,512]{3,2,1,0:T(8,128)(2,1)S(1)}, bf16[4,2,56,512]{3,2,1,0:T(8,128)(2,1)S(1)}, u32[]{:S(2)}, u32[]{:S(2)}) %collective-permute-start.4) | collective-permute-done | bytes 458784 | tf_op jit(solution)/shard_map/ppermute | solution.py:31
  52.8 3.1 %collective-permute-start.5 = (bf16[4,2,56,512]{3,2,1,0:T(8,128)(2,1)S(1)}, bf16[4,2,56,512]{3,2,1,0:T(8,128)(2,1)}, u32[]{:S(2)}, u32[]{:S(2)}) collective-permute-start(bf16[4,2,56,512]{3,2,1,0:T(8,128)(2,1)S(1)} %collective-permute-done.4.refs_1_), channel_id=1, source_target_pairs={{0,2},{1,15},{2,4},{3,1},{4,6},{5,3},{6,8},{7,5},{8,10},{9,7},{10,... | collective-permute-start | bytes 1376264 | tf_op jit(solution)/shard_map/ppermute | solution.py:31
  55.8 0.2 collective-permute-done.17.refs_10_
  56.0 0.9 constant_dynamic-slice_fusion.1
  56.9 2.3 %collective-permute-start.18 = (bf16[4,2,56,640]{3,2,1,0:T(8,128)(2,1)}, bf16[4,2,56,640]{3,2,1,0:T(8,128)(2,1)}, u32[]{:S(2)}, u32[]{:S(2)}) collective-permute-start(bf16[4,2,56,640]{3,2,1,0:T(8,128)(2,1)} %constant_dynamic-slice_fusion.1), channel_id=1, source_target_pairs={{0,16},{1,49},{2,18},{3,51},{4,20},{5,53},{6,22},{7,55},{8,24},{9,... | collective-permute-start | bytes 1720328 | tf_op jit(solution)/shard_map/ppermute | solution.py:31
  59.2 0.4 collective-permute-start.19
  59.6 1.6 collective-permute-done.5.refs_2_
  61.3 3.2 %collective-permute-start.6 = (bf16[4,2,56,512]{3,2,1,0:T(8,128)(2,1)}, bf16[4,2,56,512]{3,2,1,0:T(8,128)(2,1)S(1)}, u32[]{:S(2)}, u32[]{:S(2)}) collective-permute-start(bf16[4,2,56,512]{3,2,1,0:T(8,128)(2,1)} %collective-permute-done.5.refs_2_), channel_id=1, source_target_pairs={{0,2},{1,15},{2,4},{3,1},{4,6},{5,3},{6,8},{7,5},{8,10},{9,7},{10,... | collective-permute-start | bytes 1376264 | tf_op jit(solution)/shard_map/ppermute | solution.py:31
  64.5 0.2 collective-permute-start.8
  64.7 0.3 collective-permute-start.9
  65.0 3.0 %collective-permute-done.18.refs_11_ = bf16[4,2,56,640]{3,2,1,0:T(8,128)(2,1)} collective-permute-done((bf16[4,2,56,640]{3,2,1,0:T(8,128)(2,1)}, bf16[4,2,56,640]{3,2,1,0:T(8,128)(2,1)}, u32[]{:S(2)}, u32[]{:S(2)}) %collective-permute-start.18) | collective-permute-done | bytes 573472 | tf_op jit(solution)/shard_map/ppermute | solution.py:31
  68.0 5.6 %collective-permute-start.20 = (bf16[4,2,56,640]{3,2,1,0:T(8,128)(2,1)}, bf16[4,2,56,640]{3,2,1,0:T(8,128)(2,1)}, u32[]{:S(2)}, u32[]{:S(2)}) collective-permute-start(bf16[4,2,56,640]{3,2,1,0:T(8,128)(2,1)} %collective-permute-done.18.refs_11_), channel_id=1, source_target_pairs={{0,1},{1,0},{2,3},{3,2},{4,5},{5,4},{6,7},{7,6},{8,9},{9,8},{10,11... | collective-permute-start | bytes 1720328 | tf_op jit(solution)/shard_map/ppermute | solution.py:20
  73.6 4.6 %collective-permute-done.6.refs_3_ = bf16[4,2,56,512]{3,2,1,0:T(8,128)(2,1)S(1)} collective-permute-done((bf16[4,2,56,512]{3,2,1,0:T(8,128)(2,1)}, bf16[4,2,56,512]{3,2,1,0:T(8,128)(2,1)S(1)}, u32[]{:S(2)}, u32[]{:S(2)}) %collective-permute-start.6) | collective-permute-done | bytes 458784 | tf_op jit(solution)/shard_map/ppermute | solution.py:31
  78.2 3.5 %collective-permute-start.7 = (bf16[2,2,56,512]{3,2,1,0:T(8,128)(2,1)S(1)}, bf16[2,2,56,512]{3,2,1,0:T(8,128)(2,1)S(1)}, u32[]{:S(2)}, u32[]{:S(2)}) collective-permute-start(bf16[2,2,56,512]{3,2,1,0:T(8,128)(2,1)S(1)} %constant_dynamic-slice_fusion.2), channel_id=1, source_target_pairs={{0,2},{1,15},{2,4},{3,1},{4,6},{5,3},{6,8},{7,5},{8,10},{9,7},{10,... | collective-permute-start | bytes 688136 | tf_op jit(solution)/shard_map/ppermute | solution.py:31
  81.8 2.1 %collective-permute-start.10 = (bf16[4,2,56,512]{3,2,1,0:T(8,128)(2,1)S(1)}, bf16[4,2,56,512]{3,2,1,0:T(8,128)(2,1)}, u32[]{:S(2)}, u32[]{:S(2)}) collective-permute-start(bf16[4,2,56,512]{3,2,1,0:T(8,128)(2,1)S(1)} %collective-permute-done.6.refs_3_), channel_id=1, source_target_pairs={{0,1},{1,0},{2,3},{3,2},{4,5},{5,4},{6,7},{7,6},{8,9},{9,8},{10,11... | collective-permute-start | bytes 1376264 | tf_op jit(solution)/shard_map/ppermute | solution.py:20
  83.9 5.6 %collective-permute-done.7.refs_4_ = bf16[2,2,56,512]{3,2,1,0:T(8,128)(2,1)S(1)} collective-permute-done((bf16[2,2,56,512]{3,2,1,0:T(8,128)(2,1)S(1)}, bf16[2,2,56,512]{3,2,1,0:T(8,128)(2,1)S(1)}, u32[]{:S(2)}, u32[]{:S(2)}) %collective-permute-start.7) | collective-permute-done | bytes 229408 | tf_op jit(solution)/shard_map/ppermute | solution.py:31
  89.5 6.4 %collective-permute-start.11 = (bf16[2,2,56,512]{3,2,1,0:T(8,128)(2,1)S(1)}, bf16[2,2,56,512]{3,2,1,0:T(8,128)(2,1)}, u32[]{:S(2)}, u32[]{:S(2)}) collective-permute-start(bf16[2,2,56,512]{3,2,1,0:T(8,128)(2,1)S(1)} %collective-permute-done.7.refs_4_), channel_id=1, source_target_pairs={{0,1},{1,0},{2,3},{3,2},{4,5},{5,4},{6,7},{7,6},{8,9},{9,8},{10,11... | collective-permute-start | bytes 688136 | tf_op jit(solution)/shard_map/ppermute | solution.py:20
  95.9 0.1 copy.14
  96.0 1.1 collective-permute-done.11.refs_8_
  97.2 1.3 copy-done.4
  98.5 1.0 copy-done.6
  99.5 16.9 %spatial.1.attended = bf16[1152,512]{1,0:T(8,128)(2,1)S(1)} custom-call(s32[8]{0:T(128)S(1)} %copy-done.7, s32[32]{0:T(128)S(1)} %copy-done.3, bf16[512,1152]{1,0:T(8,128)(2,1)S(1)} %bitcast.34, f32[6,1,1152]{2,1,0:T(1,128)S(1)} %bitcast.30, f32[72,4]{1,0:T(8,128)S(1)} %bitcast.27, bf16[4,2,56,512]{3,2,1,0:T(8,128)(2,1)S(1)} %pad_maximum_fusion.1.refs_0_, ...), custom_call_target="tpu_custom_call" | custom-call | flops 20000000000 | bytes 20000000 | tf_op jit(solution)/shard_map/spatial/pallas_call | solution.py:310
  116.5 1.0 copy-done.8
  117.5 7.4 %mixing.1 = bf16[32,144,128]{2,1,0:T(8,128)(2,1)} custom-call(bf16[512,1152]{1,0:T(8,128)(2,1)} %bitcast.33, f32[6,1,1152]{2,1,0:T(1,128)} %bitcast.29, bf16[1152,512]{1,0:T(8,128)(2,1)} %copy-done.8, bf16[64,96,1152]{2,1,0:T(8,128)(2,1)} %bitcast.35), custom_call_target="tpu_custom_call" | custom-call | flops 20000000000 | bytes 20000000 | tf_op jit(solution)/shard_map/mixing/pallas_call | solution.py:322
  124.9 5.0 %all-to-all-start = ((bf16[32,144,128]{2,1,0:T(8,128)(2,1)}), bf16[32,144,128]{2,1,0:T(8,128)(2,1)S(1)}, u32[]{:S(2)}, u32[]{:S(2)}) async-start(bf16[32,144,128]{2,1,0:T(8,128)(2,1)} %mixing.1), calls=%async_computation | async-start | bytes 2359296 | tf_op jit(solution)/shard_map/all_to_all | solution.py:336
  129.9 1.1 copy.15
  131.0 0.1 eq.29
  131.1 0.1 select_reduce_fusion
  131.2 0.9 and_convert_fusion.allowed
  132.0 9.5 %prepare.1 = (bf16[3456,1152]{1,0:T(8,128)(2,1)}, bf16[1152,1152]{1,0:T(8,128)(2,1)}) custom-call(bf16[64,96,1152]{2,1,0:T(8,128)(2,1)} %bitcast.36), custom_call_target="tpu_custom_call" | custom-call | bytes 30000000 | tf_op jit(solution)/shard_map/prepare/pallas_call | solution.py:337
  141.6 15.5 %all-to-all-done.received = bf16[32,144,128]{2,1,0:T(8,128)(2,1)S(1)} async-done(((bf16[32,144,128]{2,1,0:T(8,128)(2,1)}), bf16[32,144,128]{2,1,0:T(8,128)(2,1)S(1)}, u32[]{:S(2)}, u32[]{:S(2)}) %all-to-all-start) | async-done | bytes 1179680 | tf_op jit(solution)/shard_map/all_to_all | solution.py:336
  157.0 1.0 copy-done.9
  158.1 21.9 %temporal.1 = f32[16,512]{1,0:T(8,128)} custom-call(bf16[32,144,128]{2,1,0:T(8,128)(2,1)} %copy-done.9, f32[1152,6]{1,0:T(8,128)} %bitcast.37, f32[72,4]{1,0:T(8,128)} %bitcast.28, f32[256,256]{1,0:T(8,128)} %and_convert_fusion.allowed, bf16[16,1152]{1,0:T(8,128)(2,1)} %bitcast.43, bf16[3456,1152]{1,0:T(8,128)(2,1)} %get-tuple-element.7.held_columns, ...), custom_call_target="tpu_custom_call" | custom-call | flops 20000000000 | bytes 20000000 | tf_op jit(solution)/shard_map/temporal/pallas_call | solution.py:350
  180.0 0.7 constant_dynamic-slice_fusion
  180.7 4.9 %collective-permute-start.21 = (f32[8,512]{1,0:T(8,128)S(1)}, f32[8,512]{1,0:T(8,128)S(1)}, u32[]{:S(2)}, u32[]{:S(2)}) collective-permute-start(f32[8,512]{1,0:T(8,128)S(1)} %constant_dynamic-slice_fusion), channel_id=1, source_target_pairs={{0,1},{1,0},{2,3},{3,2},{4,5},{5,4},{6,7},{7,6},{8,9},{9,8},{10,11... | collective-permute-start | bytes 49160 | tf_op jit(solution)/shard_map/ppermute | solution.py:370
  185.6 0.1 broadcast_compare_fusion
  185.7 0.8 collective-permute-done.21
  186.5 0.7 multiply_add_fusion
  187.2 0.1 reshape.70
  187.3 0.7 fusion.6
  (47 shorter events, 0.4 us)
Async XLA Ops:
  6.5 111.0 %all-gather.3.cloned.1.call-start = ((), (), s32[]{:S(2)}) async-start(), calls=%async_computation.1 | async-start | bytes 14376960 | tf_op jit(solution)/shard_map/all_gather | solution.py:300
  9.2 4.3 %collective-permute-start = (bf16[56,1152]{1,0:T(8,128)(2,1)S(1)}, bf16[56,1152]{1,0:T(8,128)(2,1)S(1)}, u32[]{:S(2)}, u32[]{:S(2)}) collective-permute-start(bf16[56,1152]{1,0:T(8,128)(2,1)S(1)} %pad.8), channel_id=1, source_target_pairs={{0,1},{1,0},{2,3},{3,2},{4,5},{5,4},{6,7},{7,6},{8,9},{9,8},{10,11... | collective-permute-start | bytes 387080 | tf_op jit(solution)/shard_map/ppermute | solution.py:20
  14.5 21.9 %collective-permute-start.12 = (bf16[2,56,640]{2,1,0:T(8,128)(2,1)S(1)}, bf16[2,56,640]{2,1,0:T(8,128)(2,1)S(1)}, u32[]{:S(2)}, u32[]{:S(2)}) collective-permute-start(bf16[2,56,640]{2,1,0:T(8,128)(2,1)S(1)} %get-tuple-element.10), channel_id=1, source_target_pairs={{0,2},{1,15},{2,4},{3,1},{4,6},{5,3},{6,8},{7,5},{8,10},{9,7},{10,... | collective-permute-start | bytes 430088 | tf_op jit(solution)/shard_map/ppermute | solution.py:31
  18.4 18.0 %collective-permute-start.13 = (bf16[2,56,640]{2,1,0:T(8,128)(2,1)S(1)}, bf16[2,56,640]{2,1,0:T(8,128)(2,1)S(1)}, u32[]{:S(2)}, u32[]{:S(2)}) collective-permute-start(bf16[2,56,640]{2,1,0:T(8,128)(2,1)S(1)} %get-tuple-element.10), channel_id=1, source_target_pairs={{0,4},{1,13},{2,6},{3,15},{4,8},{5,1},{6,10},{7,3},{8,12},{9,5},{1... | collective-permute-start | bytes 430088 | tf_op jit(solution)/shard_map/ppermute | solution.py:31
  19.6 16.8 %collective-permute-start.14 = (bf16[2,56,640]{2,1,0:T(8,128)(2,1)S(1)}, bf16[2,56,640]{2,1,0:T(8,128)(2,1)S(1)}, u32[]{:S(2)}, u32[]{:S(2)}) collective-permute-start(bf16[2,56,640]{2,1,0:T(8,128)(2,1)S(1)} %get-tuple-element.10), channel_id=1, source_target_pairs={{0,6},{1,11},{2,8},{3,13},{4,10},{5,15},{6,12},{7,1},{8,14},{9,3},... | collective-permute-start | bytes 430088 | tf_op jit(solution)/shard_map/ppermute | solution.py:31
  20.0 12.0 %collective-permute-start.1 = (bf16[2,56,512]{2,1,0:T(8,128)(2,1)S(1)}, bf16[2,56,512]{2,1,0:T(8,128)(2,1)S(1)}, u32[]{:S(2)}, u32[]{:S(2)}) collective-permute-start(bf16[2,56,512]{2,1,0:T(8,128)(2,1)S(1)} %pad_maximum_fusion.4), channel_id=1, source_target_pairs={{0,16},{1,49},{2,18},{3,51},{4,20},{5,53},{6,22},{7,55},{8,24},{9,... | collective-permute-start | bytes 344072 | tf_op jit(solution)/shard_map/ppermute | solution.py:31
  22.7 4.9 %collective-permute-start.2 = (bf16[1,56,512]{2,1,0:T(8,128)(2,1)S(1)}, bf16[1,56,512]{2,1,0:T(8,128)(2,1)S(1)}, u32[]{:S(2)}, u32[]{:S(2)}) collective-permute-start(bf16[1,56,512]{2,1,0:T(8,128)(2,1)S(1)} %fusion.7), channel_id=1, source_target_pairs={{0,32},{1,33},{2,34},{3,35},{4,36},{5,37},{6,38},{7,39},{8,40},{9,... | collective-permute-start | bytes 172040 | tf_op jit(solution)/shard_map/ppermute | solution.py:31
  27.6 8.8 %collective-permute-start.15 = (bf16[1,56,640]{2,1,0:T(8,128)(2,1)S(1)}, bf16[1,56,640]{2,1,0:T(8,128)(2,1)S(1)}, u32[]{:S(2)}, u32[]{:S(2)}) collective-permute-start(bf16[1,56,640]{2,1,0:T(8,128)(2,1)S(1)} %fusion.5), channel_id=1, source_target_pairs={{0,8},{1,9},{2,10},{3,11},{4,12},{5,13},{6,14},{7,15},{8,0},{9,1},... | collective-permute-start | bytes 215048 | tf_op jit(solution)/shard_map/ppermute | solution.py:31
  32.1 7.0 %collective-permute-start.3 = (bf16[3,56,512]{2,1,0:T(8,128)(2,1)S(1)}, bf16[3,56,512]{2,1,0:T(8,128)(2,1)S(1)}, u32[]{:S(2)}, u32[]{:S(2)}) collective-permute-start(bf16[3,56,512]{2,1,0:T(8,128)(2,1)S(1)} %pad_maximum_fusion.2), channel_id=1, source_target_pairs={{0,1},{1,0},{2,3},{3,2},{4,5},{5,4},{6,7},{7,6},{8,9},{9,8},{10,11... | collective-permute-start | bytes 516104 | tf_op jit(solution)/shard_map/ppermute | solution.py:20
  36.5 4.0 %collective-permute-start.16 = (bf16[7,56,640]{2,1,0:T(8,128)(2,1)S(1)}, bf16[7,56,640]{2,1,0:T(8,128)(2,1)S(1)}, u32[]{:S(2)}, u32[]{:S(2)}) collective-permute-start(bf16[7,56,640]{2,1,0:T(8,128)(2,1)S(1)} %pad_maximum_fusion), channel_id=1, source_target_pairs={{0,1},{1,0},{2,3},{3,2},{4,5},{5,4},{6,7},{7,6},{8,9},{9,8},{10,11... | collective-permute-start | bytes 1505288 | tf_op jit(solution)/shard_map/ppermute | solution.py:20
  40.8 15.2 %collective-permute-start.17 = (bf16[8,2,56,640]{3,2,1,0:T(8,128)(2,1)S(1)}, bf16[8,2,56,640]{3,2,1,0:T(8,128)(2,1)S(1)}, u32[]{:S(2)}, u32[]{:S(2)}) collective-permute-start(bf16[8,2,56,640]{3,2,1,0:T(8,128)(2,1)S(1)} %bitcast.31), channel_id=1, source_target_pairs={{0,16},{1,49},{2,18},{3,51},{4,20},{5,53},{6,22},{7,55},{8,24},{9,... | collective-permute-start | bytes 3440648 | tf_op jit(solution)/shard_map/ppermute | solution.py:31
  42.2 53.8 %copy-start.10 = (f32[4,72]{1,0:T(4,128)S(1)}, f32[4,72]{1,0:T(4,128)}, u32[]{:S(2)}) copy-start(f32[4,72]{1,0:T(4,128)} %param.17) | copy-start | bytes 3460
  42.2 55.0 %copy-start.1 = (f32[1,6,1152]{2,0,1:T(1,128)S(1)}, f32[1,6,1152]{2,0,1:T(1,128)}, u32[]{:S(2)}) copy-start(f32[1,6,1152]{2,0,1:T(1,128)} %param.11) | copy-start | bytes 82948
  42.2 55.0 %copy-start.3 = (s32[32]{0:T(128)S(1)}, s32[32]{0:T(128)}, u32[]{:S(2)}) copy-start(s32[32]{0:T(128)} %block_clip.1) | copy-start | bytes 388
  42.2 55.0 %copy-start.7 = (s32[8]{0:T(128)S(1)}, s32[8]{0:T(128)}, u32[]{:S(2)}) copy-start(s32[8]{0:T(128)} %clip_tokens.1) | copy-start | bytes 100
  42.3 10.5 %collective-permute-start.4 = (bf16[4,2,56,512]{3,2,1,0:T(8,128)(2,1)S(1)}, bf16[4,2,56,512]{3,2,1,0:T(8,128)(2,1)S(1)}, u32[]{:S(2)}, u32[]{:S(2)}) collective-permute-start(bf16[4,2,56,512]{3,2,1,0:T(8,128)(2,1)S(1)} %pad_maximum_fusion.1.refs_0_), channel_id=1, source_target_pairs={{0,2},{1,15},{2,4},{3,1},{4,6},{5,3},{6,8},{7,5},{8,10},{9,7},{10,... | collective-permute-start | bytes 1376264 | tf_op jit(solution)/shard_map/ppermute | solution.py:31
  52.8 6.9 %copy-start.5 = (bf16[4,2,56,512]{3,2,1,0:T(8,128)(2,1)}, bf16[4,2,56,512]{3,2,1,0:T(8,128)(2,1)S(1)}, u32[]{:S(2)}) copy-start(bf16[4,2,56,512]{3,2,1,0:T(8,128)(2,1)S(1)} %collective-permute-done.4.refs_1_) | copy-start | bytes 1376260
  52.8 8.5 %collective-permute-start.5 = (bf16[4,2,56,512]{3,2,1,0:T(8,128)(2,1)S(1)}, bf16[4,2,56,512]{3,2,1,0:T(8,128)(2,1)}, u32[]{:S(2)}, u32[]{:S(2)}) collective-permute-start(bf16[4,2,56,512]{3,2,1,0:T(8,128)(2,1)S(1)} %collective-permute-done.4.refs_1_), channel_id=1, source_target_pairs={{0,2},{1,15},{2,4},{3,1},{4,6},{5,3},{6,8},{7,5},{8,10},{9,7},{10,... | collective-permute-start | bytes 1376264 | tf_op jit(solution)/shard_map/ppermute | solution.py:31
  56.9 11.1 %collective-permute-start.18 = (bf16[4,2,56,640]{3,2,1,0:T(8,128)(2,1)}, bf16[4,2,56,640]{3,2,1,0:T(8,128)(2,1)}, u32[]{:S(2)}, u32[]{:S(2)}) collective-permute-start(bf16[4,2,56,640]{3,2,1,0:T(8,128)(2,1)} %constant_dynamic-slice_fusion.1), channel_id=1, source_target_pairs={{0,16},{1,49},{2,18},{3,51},{4,20},{5,53},{6,22},{7,55},{8,24},{9,... | collective-permute-start | bytes 1720328 | tf_op jit(solution)/shard_map/ppermute | solution.py:31
  59.2 38.0 %collective-permute-start.19 = (bf16[8,2,56,640]{3,2,1,0:T(8,128)(2,1)S(1)}, bf16[8,2,56,640]{3,2,1,0:T(8,128)(2,1)}, u32[]{:S(2)}, u32[]{:S(2)}) collective-permute-start(bf16[8,2,56,640]{3,2,1,0:T(8,128)(2,1)S(1)} %collective-permute-done.17.refs_10_), channel_id=1, source_target_pairs={{0,1},{1,0},{2,3},{3,2},{4,5},{5,4},{6,7},{7,6},{8,9},{9,8},{10,11... | collective-permute-start | bytes 3440648 | tf_op jit(solution)/shard_map/ppermute | solution.py:20
  61.3 17.0 %collective-permute-start.6 = (bf16[4,2,56,512]{3,2,1,0:T(8,128)(2,1)}, bf16[4,2,56,512]{3,2,1,0:T(8,128)(2,1)S(1)}, u32[]{:S(2)}, u32[]{:S(2)}) collective-permute-start(bf16[4,2,56,512]{3,2,1,0:T(8,128)(2,1)} %collective-permute-done.5.refs_2_), channel_id=1, source_target_pairs={{0,2},{1,15},{2,4},{3,1},{4,6},{5,3},{6,8},{7,5},{8,10},{9,7},{10,... | collective-permute-start | bytes 1376264 | tf_op jit(solution)/shard_map/ppermute | solution.py:31
  64.5 17.3 %collective-permute-start.8 = (bf16[4,2,56,512]{3,2,1,0:T(8,128)(2,1)}, bf16[4,2,56,512]{3,2,1,0:T(8,128)(2,1)}, u32[]{:S(2)}, u32[]{:S(2)}) collective-permute-start(bf16[4,2,56,512]{3,2,1,0:T(8,128)(2,1)} %copy-done.5), channel_id=1, source_target_pairs={{0,1},{1,0},{2,3},{3,2},{4,5},{5,4},{6,7},{7,6},{8,9},{9,8},{10,11... | collective-permute-start | bytes 1376264 | tf_op jit(solution)/shard_map/ppermute | solution.py:20
  64.7 31.3 %collective-permute-start.9 = (bf16[4,2,56,512]{3,2,1,0:T(8,128)(2,1)}, bf16[4,2,56,512]{3,2,1,0:T(8,128)(2,1)}, u32[]{:S(2)}, u32[]{:S(2)}) collective-permute-start(bf16[4,2,56,512]{3,2,1,0:T(8,128)(2,1)} %collective-permute-done.5.refs_2_), channel_id=1, source_target_pairs={{0,1},{1,0},{2,3},{3,2},{4,5},{5,4},{6,7},{7,6},{8,9},{9,8},{10,11... | collective-permute-start | bytes 1376264 | tf_op jit(solution)/shard_map/ppermute | solution.py:20
  68.0 29.2 %collective-permute-start.20 = (bf16[4,2,56,640]{3,2,1,0:T(8,128)(2,1)}, bf16[4,2,56,640]{3,2,1,0:T(8,128)(2,1)}, u32[]{:S(2)}, u32[]{:S(2)}) collective-permute-start(bf16[4,2,56,640]{3,2,1,0:T(8,128)(2,1)} %collective-permute-done.18.refs_11_), channel_id=1, source_target_pairs={{0,1},{1,0},{2,3},{3,2},{4,5},{5,4},{6,7},{7,6},{8,9},{9,8},{10,11... | collective-permute-start | bytes 1720328 | tf_op jit(solution)/shard_map/ppermute | solution.py:20
  78.2 11.3 %collective-permute-start.7 = (bf16[2,2,56,512]{3,2,1,0:T(8,128)(2,1)S(1)}, bf16[2,2,56,512]{3,2,1,0:T(8,128)(2,1)S(1)}, u32[]{:S(2)}, u32[]{:S(2)}) collective-permute-start(bf16[2,2,56,512]{3,2,1,0:T(8,128)(2,1)S(1)} %constant_dynamic-slice_fusion.2), channel_id=1, source_target_pairs={{0,2},{1,15},{2,4},{3,1},{4,6},{5,3},{6,8},{7,5},{8,10},{9,7},{10,... | collective-permute-start | bytes 688136 | tf_op jit(solution)/shard_map/ppermute | solution.py:31
  81.8 15.4 %collective-permute-start.10 = (bf16[4,2,56,512]{3,2,1,0:T(8,128)(2,1)S(1)}, bf16[4,2,56,512]{3,2,1,0:T(8,128)(2,1)}, u32[]{:S(2)}, u32[]{:S(2)}) collective-permute-start(bf16[4,2,56,512]{3,2,1,0:T(8,128)(2,1)S(1)} %collective-permute-done.6.refs_3_), channel_id=1, source_target_pairs={{0,1},{1,0},{2,3},{3,2},{4,5},{5,4},{6,7},{7,6},{8,9},{9,8},{10,11... | collective-permute-start | bytes 1376264 | tf_op jit(solution)/shard_map/ppermute | solution.py:20
  89.5 7.6 %collective-permute-start.11 = (bf16[2,2,56,512]{3,2,1,0:T(8,128)(2,1)S(1)}, bf16[2,2,56,512]{3,2,1,0:T(8,128)(2,1)}, u32[]{:S(2)}, u32[]{:S(2)}) collective-permute-start(bf16[2,2,56,512]{3,2,1,0:T(8,128)(2,1)S(1)} %collective-permute-done.7.refs_4_), channel_id=1, source_target_pairs={{0,1},{1,0},{2,3},{3,2},{4,5},{5,4},{6,7},{7,6},{8,9},{9,8},{10,11... | collective-permute-start | bytes 688136 | tf_op jit(solution)/shard_map/ppermute | solution.py:20
  96.0 20.4 %copy-start = (f32[4,72]{0,1:T(8,128)}, f32[4,72]{0,1:T(8,128)S(1)}, u32[]{:S(2)}) copy-start(f32[4,72]{0,1:T(8,128)S(1)} %copy.14) | copy-start | bytes 3460
  97.2 1.3 copy-start.4
  98.5 1.0 copy-start.6
  116.5 1.0 copy-start.8
  124.9 5.0 %copy-start.2 = (f32[1,6,1152]{2,0,1:T(1,128)S(1)}, f32[1,6,1152]{2,0,1:T(1,128)}, u32[]{:S(2)}) copy-start(f32[1,6,1152]{2,0,1:T(1,128)} %param.11) | copy-start | bytes 82948
  124.9 32.1 %all-to-all-start = ((bf16[32,144,128]{2,1,0:T(8,128)(2,1)}), bf16[32,144,128]{2,1,0:T(8,128)(2,1)S(1)}, u32[]{:S(2)}, u32[]{:S(2)}) async-start(bf16[32,144,128]{2,1,0:T(8,128)(2,1)} %mixing.1), calls=%async_computation | async-start | bytes 2359296 | tf_op jit(solution)/shard_map/all_to_all | solution.py:336
  157.0 1.0 copy-start.9
  180.7 5.8 %collective-permute-start.21 = (f32[8,512]{1,0:T(8,128)S(1)}, f32[8,512]{1,0:T(8,128)S(1)}, u32[]{:S(2)}, u32[]{:S(2)}) collective-permute-start(f32[8,512]{1,0:T(8,128)S(1)} %constant_dynamic-slice_fusion), channel_id=1, source_target_pairs={{0,1},{1,0},{2,3},{3,2},{4,5},{5,4},{6,7},{7,6},{8,9},{9,8},{10,11... | collective-permute-start | bytes 49160 | tf_op jit(solution)/shard_map/ppermute | solution.py:370
Sparse Core Ops, SparseCore 0:
  10.1 101.7 all-gather.2

commit v7 on v6

--- a/solution.py
+++ b/solution.py
@@ -59,7 +59,7 @@
     ring = jnp.concatenate([second, low, high, opposite]).reshape((Z_RING,) + second.shape)
     across = plane_step(ring, True)
     beyond = plane_step(lax.dynamic_slice_in_dim(across, 4 * core, 4, 0), True)
-    rows.append(plane_step(lax.dynamic_slice_in_dim(rows[3], 2 * core, 2, 0), False))
+    rows.append(plane_step(lax.dynamic_slice_in_dim(rows[0], 2 * core, 2, 0), False, 4))
     rows += [swap_cores(part) for part in rows[1:]]
     return rows, [ring, across, beyond, swap_cores(across), swap_cores(beyond)]
 

time: 196 us -> 196 us (level)
  starting transfers between devices: 59.5 us -> 50.2 us
  waiting for transfers between devices: 51.8 us -> 59.8 us
  local copies, waits for them, and re-layouts: 8.32 us -> 10.6 us
    ppermute x9, starting transfers between devices: 21 us -> 10.8 us  [swap_cores(): return lax.ppermute(array, 'cfg', [(0, 1), (1, 0)])]
    ppermute x12, waiting for transfers between devices: 32 us -> 40.5 us  [plane_step(): return lax.ppermute(array, ('seq', 'cfg'), pairs)]
    unnamed x26 -> x30, local copies, waits for them, and re-layouts: 5.6 us -> 7.85 us
  transfers between devices with their start and end apart: 24 -> 24, of which waited for: 13 -> 9; matrix products, arithmetic and copies ran while one was open for 3% -> 3% of each run, Pallas kernels for 14% -> 14%
where the time goes in v7:
time: 196 us
  waiting for transfers between devices  59.8 us (31%)
  Pallas kernels  55.8 us (28%)
  starting transfers between devices  50.2 us (26%)
  between operations  13.7 us (7%)
  local copies, waits for them, and re-layouts  10.6 us (5%)
  other arithmetic  5.76 us (3%)
    ppermute x12, waiting for transfers between devices, plane_step(): return lax.ppermute(array, ('seq', 'cfg'), pairs)  40.5 us
    ppermute x12, starting transfers between devices, plane_step(): return lax.ppermute(array, ('seq', 'cfg'), pairs)  28.5 us
    pallas_call x1, Pallas kernels, body(): pl.pallas_call(functools.partial(temporal_kernel, head_size), out_shape=j...  21.9 us
    pallas_call x1, Pallas kernels, body(): pl.pallas_call(functools.partial(spatial_kernel, head_size), out_shape=ja...  16.9 us
    all_to_all x1, waiting for transfers between devices, body(): lax.all_to_all(residual, 'seq', split_axis=0, concat_axis=0, tiled=True)  15.5 us
    ppermute x9, starting transfers between devices, swap_cores(): return lax.ppermute(array, 'cfg', [(0, 1), (1, 0)])  10.8 us
    pallas_call x1, Pallas kernels, body(): pl.pallas_call(functools.partial(prepare_kernel, head_size), out_shape=[j...  9.53 us
    unnamed x30, local copies, waits for them, and re-layouts  7.85 us
  transfers between devices with their start and end apart: 24, of which 9 were waited for; matrix products, arithmetic and copies ran while one was open for 3% of the time, Pallas kernels for 14%

profile of v7, /device:TPU:1, one launch (start us, length us, event | category | flops | bytes accessed | tf_op | source)
XLA Modules:
  0.0 195.8 jit_solution(80737610844652586)
XLA Ops:
  6.5 1.7 fusion.4
  8.2 0.0 all-gather.3.cloned.1.call-update
  8.3 0.9 pad.8
  9.2 3.3 %collective-permute-start = (bf16[56,1152]{1,0:T(8,128)(2,1)S(1)}, bf16[56,1152]{1,0:T(8,128)(2,1)S(1)}, u32[]{:S(2)}, u32[]{:S(2)}) collective-permute-start(bf16[56,1152]{1,0:T(8,128)(2,1)S(1)} %pad.8), channel_id=1, source_target_pairs={{0,1},{1,0},{2,3},{3,2},{4,5},{5,4},{6,7},{7,6},{8,9},{9,8},{10,11... | collective-permute-start | bytes 387080 | tf_op jit(solution)/shard_map/ppermute | solution.py:20
  12.5 1.0 collective-permute-done
  13.5 1.0 select_bitcast_fusion
  14.5 3.9 %collective-permute-start.12 = (bf16[2,56,640]{2,1,0:T(8,128)(2,1)S(1)}, bf16[2,56,640]{2,1,0:T(8,128)(2,1)S(1)}, u32[]{:S(2)}, u32[]{:S(2)}) collective-permute-start(bf16[2,56,640]{2,1,0:T(8,128)(2,1)S(1)} %get-tuple-element.10), channel_id=1, source_target_pairs={{0,2},{1,15},{2,4},{3,1},{4,6},{5,3},{6,8},{7,5},{8,10},{9,7},{10,... | collective-permute-start | bytes 430088 | tf_op jit(solution)/shard_map/ppermute | solution.py:31
  18.4 1.2 collective-permute-start.13
  19.6 0.4 collective-permute-start.14
  20.1 4.6 %collective-permute-start.15 = (bf16[1,56,640]{2,1,0:T(8,128)(2,1)S(1)}, bf16[1,56,640]{2,1,0:T(8,128)(2,1)S(1)}, u32[]{:S(2)}, u32[]{:S(2)}) collective-permute-start(bf16[1,56,640]{2,1,0:T(8,128)(2,1)S(1)} %fusion.5), channel_id=1, source_target_pairs={{0,8},{1,9},{2,10},{3,11},{4,12},{5,13},{6,14},{7,15},{8,0},{9,1},... | collective-permute-start | bytes 215048 | tf_op jit(solution)/shard_map/ppermute | solution.py:31
  24.7 2.7 %collective-permute-start.2 = (bf16[1,56,512]{2,1,0:T(8,128)(2,1)S(1)}, bf16[1,56,512]{2,1,0:T(8,128)(2,1)S(1)}, u32[]{:S(2)}, u32[]{:S(2)}) collective-permute-start(bf16[1,56,512]{2,1,0:T(8,128)(2,1)S(1)} %fusion.7), channel_id=1, source_target_pairs={{0,32},{1,33},{2,34},{3,35},{4,36},{5,37},{6,38},{7,39},{8,40},{9,... | collective-permute-start | bytes 172040 | tf_op jit(solution)/shard_map/ppermute | solution.py:31
  27.4 3.9 %collective-permute-done.15 = bf16[1,56,640]{2,1,0:T(8,128)(2,1)S(1)} collective-permute-done((bf16[1,56,640]{2,1,0:T(8,128)(2,1)S(1)}, bf16[1,56,640]{2,1,0:T(8,128)(2,1)S(1)}, u32[]{:S(2)}, u32[]{:S(2)}) %collective-permute-start.15) | collective-permute-done | bytes 71712 | tf_op jit(solution)/shard_map/ppermute | solution.py:31
  31.4 2.5 %collective-permute-start.1 = (bf16[2,56,512]{2,1,0:T(8,128)(2,1)S(1)}, bf16[2,56,512]{2,1,0:T(8,128)(2,1)S(1)}, u32[]{:S(2)}, u32[]{:S(2)}) collective-permute-start(bf16[2,56,512]{2,1,0:T(8,128)(2,1)S(1)} %pad_maximum_fusion.4), channel_id=1, source_target_pairs={{0,16},{1,49},{2,18},{3,51},{4,20},{5,53},{6,22},{7,55},{8,24},{9,... | collective-permute-start | bytes 344072 | tf_op jit(solution)/shard_map/ppermute | solution.py:31
  33.9 0.1 pad_maximum_fusion
  34.0 1.4 collective-permute-start.16
  35.4 0.9 collective-permute-done.1
  36.4 3.7 %collective-permute-start.3 = (bf16[3,56,512]{2,1,0:T(8,128)(2,1)S(1)}, bf16[3,56,512]{2,1,0:T(8,128)(2,1)S(1)}, u32[]{:S(2)}, u32[]{:S(2)}) collective-permute-start(bf16[3,56,512]{2,1,0:T(8,128)(2,1)S(1)} %pad_maximum_fusion.2), channel_id=1, source_target_pairs={{0,1},{1,0},{2,3},{3,2},{4,5},{5,4},{6,7},{7,6},{8,9},{9,8},{10,11... | collective-permute-start | bytes 516104 | tf_op jit(solution)/shard_map/ppermute | solution.py:20
  40.1 0.1 select_dynamic-update-slice_fusion.1
  40.3 0.1 select_dynamic-update-slice_fusion
  40.5 1.2 collective-permute-start.17
  41.7 0.0 copy-start.12
  41.7 0.0 copy-start.1
  41.8 0.1 pad_maximum_fusion.1.refs_0_
  41.8 1.0 collective-permute-start.4
  42.8 10.4 %collective-permute-done.4.refs_1_ = bf16[4,2,56,512]{3,2,1,0:T(8,128)(2,1)} collective-permute-done((bf16[4,2,56,512]{3,2,1,0:T(8,128)(2,1)S(1)}, bf16[4,2,56,512]{3,2,1,0:T(8,128)(2,1)}, u32[]{:S(2)}, u32[]{:S(2)}) %collective-permute-start.4) | collective-permute-done | bytes 458784 | tf_op jit(solution)/shard_map/ppermute | solution.py:31
  53.2 2.9 %collective-permute-start.5 = (bf16[4,2,56,512]{3,2,1,0:T(8,128)(2,1)}, bf16[4,2,56,512]{3,2,1,0:T(8,128)(2,1)}, u32[]{:S(2)}, u32[]{:S(2)}) collective-permute-start(bf16[4,2,56,512]{3,2,1,0:T(8,128)(2,1)} %collective-permute-done.4.refs_1_), channel_id=1, source_target_pairs={{0,2},{1,15},{2,4},{3,1},{4,6},{5,3},{6,8},{7,5},{8,10},{9,7},{10,... | collective-permute-start | bytes 1376264 | tf_op jit(solution)/shard_map/ppermute | solution.py:31
  56.1 0.9 constant_dynamic-slice_fusion.1
  57.0 1.7 collective-permute-start.18
  58.7 0.1 collective-permute-start.19
  58.8 3.1 %collective-permute-start.7 = (bf16[2,2,56,512]{3,2,1,0:T(8,128)(2,1)S(1)}, bf16[2,2,56,512]{3,2,1,0:T(8,128)(2,1)S(1)}, u32[]{:S(2)}, u32[]{:S(2)}) collective-permute-start(bf16[2,2,56,512]{3,2,1,0:T(8,128)(2,1)S(1)} %constant_dynamic-slice_fusion.2), channel_id=1, source_target_pairs={{0,8},{1,9},{2,10},{3,11},{4,12},{5,13},{6,14},{7,15},{8,0},{9,1},... | collective-permute-start | bytes 688136 | tf_op jit(solution)/shard_map/ppermute | solution.py:31
  62.0 3.2 %collective-permute-start.6 = (bf16[4,2,56,512]{3,2,1,0:T(8,128)(2,1)}, bf16[4,2,56,512]{3,2,1,0:T(8,128)(2,1)}, u32[]{:S(2)}, u32[]{:S(2)}) collective-permute-start(bf16[4,2,56,512]{3,2,1,0:T(8,128)(2,1)} %collective-permute-done.5.refs_2_), channel_id=1, source_target_pairs={{0,2},{1,15},{2,4},{3,1},{4,6},{5,3},{6,8},{7,5},{8,10},{9,7},{10,... | collective-permute-start | bytes 1376264 | tf_op jit(solution)/shard_map/ppermute | solution.py:31
  65.2 4.5 %collective-permute-done.7.refs_4_ = bf16[2,2,56,512]{3,2,1,0:T(8,128)(2,1)S(1)} collective-permute-done((bf16[2,2,56,512]{3,2,1,0:T(8,128)(2,1)S(1)}, bf16[2,2,56,512]{3,2,1,0:T(8,128)(2,1)S(1)}, u32[]{:S(2)}, u32[]{:S(2)}) %collective-permute-start.7) | collective-permute-done | bytes 229408 | tf_op jit(solution)/shard_map/ppermute | solution.py:31
  69.6 1.4 collective-permute-start.11
  71.1 0.7 copy-done.5
  71.7 0.4 collective-permute-start.20
  72.1 0.1 collective-permute-start.8
  72.3 0.7 copy-done.7
  72.9 0.4 collective-permute-start.9
  73.3 20.8 %collective-permute-done.6.refs_3_ = bf16[4,2,56,512]{3,2,1,0:T(8,128)(2,1)} collective-permute-done((bf16[4,2,56,512]{3,2,1,0:T(8,128)(2,1)}, bf16[4,2,56,512]{3,2,1,0:T(8,128)(2,1)}, u32[]{:S(2)}, u32[]{:S(2)}) %collective-permute-start.6) | collective-permute-done | bytes 458784 | tf_op jit(solution)/shard_map/ppermute | solution.py:31
  94.2 0.1 copy.14
  94.3 2.0 %collective-permute-done.10.refs_7_ = bf16[4,2,56,512]{3,2,1,0:T(8,128)(2,1)} collective-permute-done((bf16[4,2,56,512]{3,2,1,0:T(8,128)(2,1)}, bf16[4,2,56,512]{3,2,1,0:T(8,128)(2,1)}, u32[]{:S(2)}, u32[]{:S(2)}) %collective-permute-start.10) | collective-permute-done | bytes 458784 | tf_op jit(solution)/shard_map/ppermute | solution.py:20
  96.4 1.3 copy-done.4
  97.6 0.9 copy-done.6
  98.6 0.9 copy-done.8
  99.5 16.9 %spatial.1.attended = bf16[1152,512]{1,0:T(8,128)(2,1)S(1)} custom-call(s32[8]{0:T(128)S(1)} %copy-done.9, s32[32]{0:T(128)S(1)} %copy-done.3, bf16[512,1152]{1,0:T(8,128)(2,1)S(1)} %bitcast.34, f32[6,1,1152]{2,1,0:T(1,128)S(1)} %bitcast.30, f32[72,4]{1,0:T(8,128)S(1)} %bitcast.27, bf16[4,2,56,512]{3,2,1,0:T(8,128)(2,1)S(1)} %pad_maximum_fusion.1.refs_0_, ...), custom_call_target="tpu_custom_call" | custom-call | flops 20000000000 | bytes 20000000 | tf_op jit(solution)/shard_map/spatial/pallas_call | solution.py:310
  116.5 1.0 copy-done.10
  117.5 7.5 %mixing.1 = bf16[32,144,128]{2,1,0:T(8,128)(2,1)} custom-call(bf16[512,1152]{1,0:T(8,128)(2,1)} %bitcast.33, f32[6,1,1152]{2,1,0:T(1,128)} %bitcast.29, bf16[1152,512]{1,0:T(8,128)(2,1)} %copy-done.10, bf16[64,96,1152]{2,1,0:T(8,128)(2,1)} %bitcast.35), custom_call_target="tpu_custom_call" | custom-call | flops 20000000000 | bytes 20000000 | tf_op jit(solution)/shard_map/mixing/pallas_call | solution.py:322
  125.0 0.0 copy-start.2
  125.0 5.9 %all-to-all-start = ((bf16[32,144,128]{2,1,0:T(8,128)(2,1)}), bf16[32,144,128]{2,1,0:T(8,128)(2,1)S(1)}, u32[]{:S(2)}, u32[]{:S(2)}) async-start(bf16[32,144,128]{2,1,0:T(8,128)(2,1)} %mixing.1), calls=%async_computation | async-start | bytes 2359296 | tf_op jit(solution)/shard_map/all_to_all | solution.py:336
  131.0 1.1 copy.15
  132.1 0.1 eq.29
  132.1 0.1 select_reduce_fusion
  132.2 0.9 and_convert_fusion.allowed
  133.1 9.5 %prepare.1 = (bf16[3456,1152]{1,0:T(8,128)(2,1)}, bf16[1152,1152]{1,0:T(8,128)(2,1)}) custom-call(bf16[64,96,1152]{2,1,0:T(8,128)(2,1)} %bitcast.36), custom_call_target="tpu_custom_call" | custom-call | bytes 30000000 | tf_op jit(solution)/shard_map/prepare/pallas_call | solution.py:337
  142.6 15.5 %all-to-all-done.received = bf16[32,144,128]{2,1,0:T(8,128)(2,1)S(1)} async-done(((bf16[32,144,128]{2,1,0:T(8,128)(2,1)}), bf16[32,144,128]{2,1,0:T(8,128)(2,1)S(1)}, u32[]{:S(2)}, u32[]{:S(2)}) %all-to-all-start) | async-done | bytes 1179680 | tf_op jit(solution)/shard_map/all_to_all | solution.py:336
  158.1 1.0 copy-done.11
  159.1 21.9 %temporal.1 = f32[16,512]{1,0:T(8,128)} custom-call(bf16[32,144,128]{2,1,0:T(8,128)(2,1)} %copy-done.11, f32[1152,6]{1,0:T(8,128)} %bitcast.37, f32[72,4]{1,0:T(8,128)} %bitcast.28, f32[256,256]{1,0:T(8,128)} %and_convert_fusion.allowed, bf16[16,1152]{1,0:T(8,128)(2,1)} %bitcast.43, bf16[3456,1152]{1,0:T(8,128)(2,1)} %get-tuple-element.7.held_columns, ...), custom_call_target="tpu_custom_call" | custom-call | flops 20000000000 | bytes 20000000 | tf_op jit(solution)/shard_map/temporal/pallas_call | solution.py:350
  181.0 0.7 constant_dynamic-slice_fusion
  181.7 4.9 %collective-permute-start.21 = (f32[8,512]{1,0:T(8,128)S(1)}, f32[8,512]{1,0:T(8,128)S(1)}, u32[]{:S(2)}, u32[]{:S(2)}) collective-permute-start(f32[8,512]{1,0:T(8,128)S(1)} %constant_dynamic-slice_fusion), channel_id=1, source_target_pairs={{0,1},{1,0},{2,3},{3,2},{4,5},{5,4},{6,7},{7,6},{8,9},{9,8},{10,11... | collective-permute-start | bytes 49160 | tf_op jit(solution)/shard_map/ppermute | solution.py:370
  186.7 0.1 broadcast_compare_fusion
  186.8 0.8 collective-permute-done.21
  187.5 0.7 multiply_add_fusion
  188.2 0.1 reshape.70
  188.3 0.7 fusion.6
  (51 shorter events, 0.4 us)
Async XLA Ops:
  6.5 111.0 %all-gather.3.cloned.1.call-start = ((), (), s32[]{:S(2)}) async-start(), calls=%async_computation.1 | async-start | bytes 14376960 | tf_op jit(solution)/shard_map/all_gather | solution.py:300
  9.2 4.3 %collective-permute-start = (bf16[56,1152]{1,0:T(8,128)(2,1)S(1)}, bf16[56,1152]{1,0:T(8,128)(2,1)S(1)}, u32[]{:S(2)}, u32[]{:S(2)}) collective-permute-start(bf16[56,1152]{1,0:T(8,128)(2,1)S(1)} %pad.8), channel_id=1, source_target_pairs={{0,1},{1,0},{2,3},{3,2},{4,5},{5,4},{6,7},{7,6},{8,9},{9,8},{10,11... | collective-permute-start | bytes 387080 | tf_op jit(solution)/shard_map/ppermute | solution.py:20
  14.5 19.4 %collective-permute-start.12 = (bf16[2,56,640]{2,1,0:T(8,128)(2,1)S(1)}, bf16[2,56,640]{2,1,0:T(8,128)(2,1)S(1)}, u32[]{:S(2)}, u32[]{:S(2)}) collective-permute-start(bf16[2,56,640]{2,1,0:T(8,128)(2,1)S(1)} %get-tuple-element.10), channel_id=1, source_target_pairs={{0,2},{1,15},{2,4},{3,1},{4,6},{5,3},{6,8},{7,5},{8,10},{9,7},{10,... | collective-permute-start | bytes 430088 | tf_op jit(solution)/shard_map/ppermute | solution.py:31
  18.4 15.5 %collective-permute-start.13 = (bf16[2,56,640]{2,1,0:T(8,128)(2,1)S(1)}, bf16[2,56,640]{2,1,0:T(8,128)(2,1)S(1)}, u32[]{:S(2)}, u32[]{:S(2)}) collective-permute-start(bf16[2,56,640]{2,1,0:T(8,128)(2,1)S(1)} %get-tuple-element.10), channel_id=1, source_target_pairs={{0,4},{1,13},{2,6},{3,15},{4,8},{5,1},{6,10},{7,3},{8,12},{9,5},{1... | collective-permute-start | bytes 430088 | tf_op jit(solution)/shard_map/ppermute | solution.py:31
  19.6 14.3 %collective-permute-start.14 = (bf16[2,56,640]{2,1,0:T(8,128)(2,1)S(1)}, bf16[2,56,640]{2,1,0:T(8,128)(2,1)S(1)}, u32[]{:S(2)}, u32[]{:S(2)}) collective-permute-start(bf16[2,56,640]{2,1,0:T(8,128)(2,1)S(1)} %get-tuple-element.10), channel_id=1, source_target_pairs={{0,6},{1,11},{2,8},{3,13},{4,10},{5,15},{6,12},{7,1},{8,14},{9,3},... | collective-permute-start | bytes 430088 | tf_op jit(solution)/shard_map/ppermute | solution.py:31
  20.1 11.2 %collective-permute-start.15 = (bf16[1,56,640]{2,1,0:T(8,128)(2,1)S(1)}, bf16[1,56,640]{2,1,0:T(8,128)(2,1)S(1)}, u32[]{:S(2)}, u32[]{:S(2)}) collective-permute-start(bf16[1,56,640]{2,1,0:T(8,128)(2,1)S(1)} %fusion.5), channel_id=1, source_target_pairs={{0,8},{1,9},{2,10},{3,11},{4,12},{5,13},{6,14},{7,15},{8,0},{9,1},... | collective-permute-start | bytes 215048 | tf_op jit(solution)/shard_map/ppermute | solution.py:31
  24.7 10.7 %collective-permute-start.2 = (bf16[1,56,512]{2,1,0:T(8,128)(2,1)S(1)}, bf16[1,56,512]{2,1,0:T(8,128)(2,1)S(1)}, u32[]{:S(2)}, u32[]{:S(2)}) collective-permute-start(bf16[1,56,512]{2,1,0:T(8,128)(2,1)S(1)} %fusion.7), channel_id=1, source_target_pairs={{0,32},{1,33},{2,34},{3,35},{4,36},{5,37},{6,38},{7,39},{8,40},{9,... | collective-permute-start | bytes 172040 | tf_op jit(solution)/shard_map/ppermute | solution.py:31
  31.4 5.0 %collective-permute-start.1 = (bf16[2,56,512]{2,1,0:T(8,128)(2,1)S(1)}, bf16[2,56,512]{2,1,0:T(8,128)(2,1)S(1)}, u32[]{:S(2)}, u32[]{:S(2)}) collective-permute-start(bf16[2,56,512]{2,1,0:T(8,128)(2,1)S(1)} %pad_maximum_fusion.4), channel_id=1, source_target_pairs={{0,16},{1,49},{2,18},{3,51},{4,20},{5,53},{6,22},{7,55},{8,24},{9,... | collective-permute-start | bytes 344072 | tf_op jit(solution)/shard_map/ppermute | solution.py:31
  34.0 6.1 %collective-permute-start.16 = (bf16[7,56,640]{2,1,0:T(8,128)(2,1)S(1)}, bf16[7,56,640]{2,1,0:T(8,128)(2,1)S(1)}, u32[]{:S(2)}, u32[]{:S(2)}) collective-permute-start(bf16[7,56,640]{2,1,0:T(8,128)(2,1)S(1)} %pad_maximum_fusion), channel_id=1, source_target_pairs={{0,1},{1,0},{2,3},{3,2},{4,5},{5,4},{6,7},{7,6},{8,9},{9,8},{10,11... | collective-permute-start | bytes 1505288 | tf_op jit(solution)/shard_map/ppermute | solution.py:20
  36.4 5.3 %collective-permute-start.3 = (bf16[3,56,512]{2,1,0:T(8,128)(2,1)S(1)}, bf16[3,56,512]{2,1,0:T(8,128)(2,1)S(1)}, u32[]{:S(2)}, u32[]{:S(2)}) collective-permute-start(bf16[3,56,512]{2,1,0:T(8,128)(2,1)S(1)} %pad_maximum_fusion.2), channel_id=1, source_target_pairs={{0,1},{1,0},{2,3},{3,2},{4,5},{5,4},{6,7},{7,6},{8,9},{9,8},{10,11... | collective-permute-start | bytes 516104 | tf_op jit(solution)/shard_map/ppermute | solution.py:20
  40.5 15.6 %collective-permute-start.17 = (bf16[8,2,56,640]{3,2,1,0:T(8,128)(2,1)S(1)}, bf16[8,2,56,640]{3,2,1,0:T(8,128)(2,1)S(1)}, u32[]{:S(2)}, u32[]{:S(2)}) collective-permute-start(bf16[8,2,56,640]{3,2,1,0:T(8,128)(2,1)S(1)} %bitcast.31), channel_id=1, source_target_pairs={{0,16},{1,49},{2,18},{3,51},{4,20},{5,53},{6,22},{7,55},{8,24},{9,... | collective-permute-start | bytes 3440648 | tf_op jit(solution)/shard_map/ppermute | solution.py:31
  41.7 52.5 %copy-start.12 = (f32[4,72]{1,0:T(4,128)S(1)}, f32[4,72]{1,0:T(4,128)}, u32[]{:S(2)}) copy-start(f32[4,72]{1,0:T(4,128)} %param.17) | copy-start | bytes 3460
  41.7 54.6 %copy-start.1 = (f32[1,6,1152]{2,0,1:T(1,128)S(1)}, f32[1,6,1152]{2,0,1:T(1,128)}, u32[]{:S(2)}) copy-start(f32[1,6,1152]{2,0,1:T(1,128)} %param.11) | copy-start | bytes 82948
  41.7 54.6 %copy-start.3 = (s32[32]{0:T(128)S(1)}, s32[32]{0:T(128)}, u32[]{:S(2)}) copy-start(s32[32]{0:T(128)} %block_clip.1) | copy-start | bytes 388
  41.7 54.6 %copy-start.9 = (s32[8]{0:T(128)S(1)}, s32[8]{0:T(128)}, u32[]{:S(2)}) copy-start(s32[8]{0:T(128)} %clip_tokens.1) | copy-start | bytes 100
  41.8 11.4 %collective-permute-start.4 = (bf16[4,2,56,512]{3,2,1,0:T(8,128)(2,1)S(1)}, bf16[4,2,56,512]{3,2,1,0:T(8,128)(2,1)}, u32[]{:S(2)}, u32[]{:S(2)}) collective-permute-start(bf16[4,2,56,512]{3,2,1,0:T(8,128)(2,1)S(1)} %pad_maximum_fusion.1.refs_0_), channel_id=1, source_target_pairs={{0,2},{1,15},{2,4},{3,1},{4,6},{5,3},{6,8},{7,5},{8,10},{9,7},{10,... | collective-permute-start | bytes 1376264 | tf_op jit(solution)/shard_map/ppermute | solution.py:31
  53.2 8.8 %collective-permute-start.5 = (bf16[4,2,56,512]{3,2,1,0:T(8,128)(2,1)}, bf16[4,2,56,512]{3,2,1,0:T(8,128)(2,1)}, u32[]{:S(2)}, u32[]{:S(2)}) collective-permute-start(bf16[4,2,56,512]{3,2,1,0:T(8,128)(2,1)} %collective-permute-done.4.refs_1_), channel_id=1, source_target_pairs={{0,2},{1,15},{2,4},{3,1},{4,6},{5,3},{6,8},{7,5},{8,10},{9,7},{10,... | collective-permute-start | bytes 1376264 | tf_op jit(solution)/shard_map/ppermute | solution.py:31
  57.0 14.7 %collective-permute-start.18 = (bf16[4,2,56,640]{3,2,1,0:T(8,128)(2,1)}, bf16[4,2,56,640]{3,2,1,0:T(8,128)(2,1)S(1)}, u32[]{:S(2)}, u32[]{:S(2)}) collective-permute-start(bf16[4,2,56,640]{3,2,1,0:T(8,128)(2,1)} %constant_dynamic-slice_fusion.1), channel_id=1, source_target_pairs={{0,16},{1,49},{2,18},{3,51},{4,20},{5,53},{6,22},{7,55},{8,24},{9,... | collective-permute-start | bytes 1720328 | tf_op jit(solution)/shard_map/ppermute | solution.py:31
  58.7 37.6 %collective-permute-start.19 = (bf16[8,2,56,640]{3,2,1,0:T(8,128)(2,1)S(1)}, bf16[8,2,56,640]{3,2,1,0:T(8,128)(2,1)}, u32[]{:S(2)}, u32[]{:S(2)}) collective-permute-start(bf16[8,2,56,640]{3,2,1,0:T(8,128)(2,1)S(1)} %collective-permute-done.17.refs_10_), channel_id=1, source_target_pairs={{0,1},{1,0},{2,3},{3,2},{4,5},{5,4},{6,7},{7,6},{8,9},{9,8},{10,11... | collective-permute-start | bytes 3440648 | tf_op jit(solution)/shard_map/ppermute | solution.py:20
  58.8 10.8 %collective-permute-start.7 = (bf16[2,2,56,512]{3,2,1,0:T(8,128)(2,1)S(1)}, bf16[2,2,56,512]{3,2,1,0:T(8,128)(2,1)S(1)}, u32[]{:S(2)}, u32[]{:S(2)}) collective-permute-start(bf16[2,2,56,512]{3,2,1,0:T(8,128)(2,1)S(1)} %constant_dynamic-slice_fusion.2), channel_id=1, source_target_pairs={{0,8},{1,9},{2,10},{3,11},{4,12},{5,13},{6,14},{7,15},{8,0},{9,1},... | collective-permute-start | bytes 688136 | tf_op jit(solution)/shard_map/ppermute | solution.py:31
  62.0 32.2 %collective-permute-start.6 = (bf16[4,2,56,512]{3,2,1,0:T(8,128)(2,1)}, bf16[4,2,56,512]{3,2,1,0:T(8,128)(2,1)}, u32[]{:S(2)}, u32[]{:S(2)}) collective-permute-start(bf16[4,2,56,512]{3,2,1,0:T(8,128)(2,1)} %collective-permute-done.5.refs_2_), channel_id=1, source_target_pairs={{0,2},{1,15},{2,4},{3,1},{4,6},{5,3},{6,8},{7,5},{8,10},{9,7},{10,... | collective-permute-start | bytes 1376264 | tf_op jit(solution)/shard_map/ppermute | solution.py:31
  69.6 2.6 %collective-permute-start.11 = (bf16[2,2,56,512]{3,2,1,0:T(8,128)(2,1)S(1)}, bf16[2,2,56,512]{3,2,1,0:T(8,128)(2,1)S(1)}, u32[]{:S(2)}, u32[]{:S(2)}) collective-permute-start(bf16[2,2,56,512]{3,2,1,0:T(8,128)(2,1)S(1)} %collective-permute-done.7.refs_4_), channel_id=1, source_target_pairs={{0,1},{1,0},{2,3},{3,2},{4,5},{5,4},{6,7},{7,6},{8,9},{9,8},{10,11... | collective-permute-start | bytes 688136 | tf_op jit(solution)/shard_map/ppermute | solution.py:20
  71.1 0.7 copy-start.5
  71.7 24.6 %collective-permute-start.20 = (bf16[4,2,56,640]{3,2,1,0:T(8,128)(2,1)S(1)}, bf16[4,2,56,640]{3,2,1,0:T(8,128)(2,1)}, u32[]{:S(2)}, u32[]{:S(2)}) collective-permute-start(bf16[4,2,56,640]{3,2,1,0:T(8,128)(2,1)S(1)} %collective-permute-done.18.refs_11_), channel_id=1, source_target_pairs={{0,1},{1,0},{2,3},{3,2},{4,5},{5,4},{6,7},{7,6},{8,9},{9,8},{10,11... | collective-permute-start | bytes 1720328 | tf_op jit(solution)/shard_map/ppermute | solution.py:20
  72.1 22.1 %collective-permute-start.8 = (bf16[4,2,56,512]{3,2,1,0:T(8,128)(2,1)}, bf16[4,2,56,512]{3,2,1,0:T(8,128)(2,1)}, u32[]{:S(2)}, u32[]{:S(2)}) collective-permute-start(bf16[4,2,56,512]{3,2,1,0:T(8,128)(2,1)} %collective-permute-done.4.refs_1_), channel_id=1, source_target_pairs={{0,1},{1,0},{2,3},{3,2},{4,5},{5,4},{6,7},{7,6},{8,9},{9,8},{10,11... | collective-permute-start | bytes 1376264 | tf_op jit(solution)/shard_map/ppermute | solution.py:20
  72.3 0.7 copy-start.7
  72.9 21.3 %collective-permute-start.9 = (bf16[4,2,56,512]{3,2,1,0:T(8,128)(2,1)}, bf16[4,2,56,512]{3,2,1,0:T(8,128)(2,1)}, u32[]{:S(2)}, u32[]{:S(2)}) collective-permute-start(bf16[4,2,56,512]{3,2,1,0:T(8,128)(2,1)} %collective-permute-done.5.refs_2_), channel_id=1, source_target_pairs={{0,1},{1,0},{2,3},{3,2},{4,5},{5,4},{6,7},{7,6},{8,9},{9,8},{10,11... | collective-permute-start | bytes 1376264 | tf_op jit(solution)/shard_map/ppermute | solution.py:20
  94.2 2.2 %collective-permute-start.10 = (bf16[4,2,56,512]{3,2,1,0:T(8,128)(2,1)}, bf16[4,2,56,512]{3,2,1,0:T(8,128)(2,1)}, u32[]{:S(2)}, u32[]{:S(2)}) collective-permute-start(bf16[4,2,56,512]{3,2,1,0:T(8,128)(2,1)} %collective-permute-done.6.refs_3_), channel_id=1, source_target_pairs={{0,1},{1,0},{2,3},{3,2},{4,5},{5,4},{6,7},{7,6},{8,9},{9,8},{10,11... | collective-permute-start | bytes 1376264 | tf_op jit(solution)/shard_map/ppermute | solution.py:20
  94.3 22.2 %copy-start = (f32[4,72]{0,1:T(8,128)}, f32[4,72]{0,1:T(8,128)S(1)}, u32[]{:S(2)}) copy-start(f32[4,72]{0,1:T(8,128)S(1)} %copy.14) | copy-start | bytes 3460
  96.3 1.3 copy-start.4
  97.6 0.9 copy-start.6
  98.6 0.9 copy-start.8
  116.5 1.0 copy-start.10
  125.0 6.0 %copy-start.2 = (f32[1,6,1152]{2,0,1:T(1,128)S(1)}, f32[1,6,1152]{2,0,1:T(1,128)}, u32[]{:S(2)}) copy-start(f32[1,6,1152]{2,0,1:T(1,128)} %param.11) | copy-start | bytes 82948
  125.0 33.1 %all-to-all-start = ((bf16[32,144,128]{2,1,0:T(8,128)(2,1)}), bf16[32,144,128]{2,1,0:T(8,128)(2,1)S(1)}, u32[]{:S(2)}, u32[]{:S(2)}) async-start(bf16[32,144,128]{2,1,0:T(8,128)(2,1)} %mixing.1), calls=%async_computation | async-start | bytes 2359296 | tf_op jit(solution)/shard_map/all_to_all | solution.py:336
  158.1 1.0 copy-start.11
  181.7 5.8 %collective-permute-start.21 = (f32[8,512]{1,0:T(8,128)S(1)}, f32[8,512]{1,0:T(8,128)S(1)}, u32[]{:S(2)}, u32[]{:S(2)}) collective-permute-start(f32[8,512]{1,0:T(8,128)S(1)} %constant_dynamic-slice_fusion), channel_id=1, source_target_pairs={{0,1},{1,0},{2,3},{3,2},{4,5},{5,4},{6,7},{7,6},{8,9},{9,8},{10,11... | collective-permute-start | bytes 49160 | tf_op jit(solution)/shard_map/ppermute | solution.py:370
Sparse Core Ops, SparseCore 0:
  10.1 105.6 all-gather.2

commit v8 on v6

--- a/solution.py
+++ b/solution.py
@@ -108,10 +108,12 @@
     return centred * lax.rsqrt(variance + 1e-06)
 
 
-def lay_out(landing, target, first, count):
+def lay_out(landing, target, first, count, arriving=None):
     size = 8 * count
 
     def group(g, carry):
+        if arriving is not None:
+            arriving(g).wait()
         rows = [landing[8 * g + i][first : first + count] for i in range(8)]
         target[pl.ds(pl.multiple_of(g * size, 16), size), :] = jnp.concatenate(rows, axis=0)
         return carry
@@ -194,12 +196,16 @@
     attend(projected, attended, gains, 0, inside, None, head_size)
 
 
-def mixing_kernel(head_size, tokens, levels, attended, gathered, residual, landing, out_rows, sem):
+def mixing_kernel(head_size, tokens, levels, attended, gathered, residual, landing, out_rows, sems):
     first, kept = landing.shape[1] * 2, landing.shape[1]
-    arriving = pltpu.make_async_copy(gathered.at[:, pl.ds(first, kept), :], landing, sem)
-    arriving.start()
-    arriving.wait()
-    lay_out(landing, out_rows, head_size - first, head_size // 4)
+
+    def arriving(g):
+        shards = pl.ds(8 * g, 8)
+        return pltpu.make_async_copy(gathered.at[shards, pl.ds(first, kept), :], landing.at[shards], sems.at[g])
+
+    for g in range(landing.shape[0] // 8):
+        arriving(g).start()
+    lay_out(landing, out_rows, head_size - first, head_size // 4, arriving)
     for start in range(0, tokens.shape[0], 256):
         chunk = slice(start, start + 256)
         projection = dot_over(attended[:, chunk], out_rows[...], 0, 1)
@@ -327,7 +333,7 @@
         scratch_shapes=[
             pltpu.VMEM((shards, 32, width), BF16),
             pltpu.VMEM((width, width), BF16),
-            pltpu.SemaphoreType.DMA,
+            pltpu.SemaphoreType.DMA((shards // 8,)),
         ],
         compiler_params=params,
         cost_estimate=cost,

time: 196 us -> 195 us (level)
  no operation moved by 1% of the time
where the time goes in v8:
time: 195 us; the launch traced here: 194 us
  starting transfers between devices  59.5 us (31%)
  Pallas kernels  55.4 us (28%)
  waiting for transfers between devices  51.8 us (27%)
  between operations  13.7 us (7%)
  local copies, waits for them, and re-layouts  8.32 us (4%)
  other arithmetic  5.75 us (3%)
    ppermute x12, waiting for transfers between devices, plane_step(): return lax.ppermute(array, ('seq', 'cfg'), pairs)  32 us
    ppermute x12, starting transfers between devices, plane_step(): return lax.ppermute(array, ('seq', 'cfg'), pairs)  28.6 us
    pallas_call x1, Pallas kernels, body(): pl.pallas_call(functools.partial(temporal_kernel, head_size), out_shape=j...  21.9 us
    ppermute x9, starting transfers between devices, swap_cores(): return lax.ppermute(array, 'cfg', [(0, 1), (1, 0)])  21 us
    pallas_call x1, Pallas kernels, body(): pl.pallas_call(functools.partial(spatial_kernel, head_size), out_shape=ja...  16.9 us
    all_to_all x1, waiting for transfers between devices, body(): lax.all_to_all(residual, 'seq', split_axis=0, concat_axis=0, tiled=True)  15.5 us
    pallas_call x1, Pallas kernels, body(): pl.pallas_call(functools.partial(prepare_kernel, head_size), out_shape=[j...  9.52 us
    pallas_call x1, Pallas kernels, body(): pl.pallas_call(functools.partial(mixing_kernel, head_size), out_shape=jax...  7.08 us
  transfers between devices with their start and end apart: 24, of which 13 were waited for; matrix products, arithmetic and copies ran while one was open for 3% of the time, Pallas kernels for 14%

profile of v8, /device:TPU:1, one launch (start us, length us, event | category | flops | bytes accessed | tf_op | source)
XLA Modules:
  0.0 194.4 jit_solution(12447531871793638392)
XLA Ops:
  6.5 1.7 fusion.4
  8.2 0.0 all-gather.3.cloned.1.call-update
  8.3 0.9 pad.8
  9.2 3.3 %collective-permute-start = (bf16[56,1152]{1,0:T(8,128)(2,1)S(1)}, bf16[56,1152]{1,0:T(8,128)(2,1)S(1)}, u32[]{:S(2)}, u32[]{:S(2)}) collective-permute-start(bf16[56,1152]{1,0:T(8,128)(2,1)S(1)} %pad.8), channel_id=1, source_target_pairs={{0,1},{1,0},{2,3},{3,2},{4,5},{5,4},{6,7},{7,6},{8,9},{9,8},{10,11... | collective-permute-start | bytes 387080 | tf_op jit(solution)/shard_map/ppermute | solution.py:20
  12.5 1.0 collective-permute-done
  13.5 1.0 select_bitcast_fusion
  14.5 3.9 %collective-permute-start.12 = (bf16[2,56,640]{2,1,0:T(8,128)(2,1)S(1)}, bf16[2,56,640]{2,1,0:T(8,128)(2,1)S(1)}, u32[]{:S(2)}, u32[]{:S(2)}) collective-permute-start(bf16[2,56,640]{2,1,0:T(8,128)(2,1)S(1)} %get-tuple-element.10), channel_id=1, source_target_pairs={{0,2},{1,15},{2,4},{3,1},{4,6},{5,3},{6,8},{7,5},{8,10},{9,7},{10,... | collective-permute-start | bytes 430088 | tf_op jit(solution)/shard_map/ppermute | solution.py:31
  18.4 1.2 collective-permute-start.13
  19.6 0.4 collective-permute-start.14
  20.0 2.6 %collective-permute-start.1 = (bf16[2,56,512]{2,1,0:T(8,128)(2,1)S(1)}, bf16[2,56,512]{2,1,0:T(8,128)(2,1)S(1)}, u32[]{:S(2)}, u32[]{:S(2)}) collective-permute-start(bf16[2,56,512]{2,1,0:T(8,128)(2,1)S(1)} %pad_maximum_fusion.4), channel_id=1, source_target_pairs={{0,16},{1,49},{2,18},{3,51},{4,20},{5,53},{6,22},{7,55},{8,24},{9,... | collective-permute-start | bytes 344072 | tf_op jit(solution)/shard_map/ppermute | solution.py:31
  22.7 0.6 collective-permute-start.2
  23.3 4.3 %collective-permute-done.2 = bf16[1,56,512]{2,1,0:T(8,128)(2,1)S(1)} collective-permute-done((bf16[1,56,512]{2,1,0:T(8,128)(2,1)S(1)}, bf16[1,56,512]{2,1,0:T(8,128)(2,1)S(1)}, u32[]{:S(2)}, u32[]{:S(2)}) %collective-permute-start.2) | collective-permute-done | bytes 57376 | tf_op jit(solution)/shard_map/ppermute | solution.py:31
  27.6 4.5 %collective-permute-start.15 = (bf16[1,56,640]{2,1,0:T(8,128)(2,1)S(1)}, bf16[1,56,640]{2,1,0:T(8,128)(2,1)S(1)}, u32[]{:S(2)}, u32[]{:S(2)}) collective-permute-start(bf16[1,56,640]{2,1,0:T(8,128)(2,1)S(1)} %fusion.5), channel_id=1, source_target_pairs={{0,8},{1,9},{2,10},{3,11},{4,12},{5,13},{6,14},{7,15},{8,0},{9,1},... | collective-permute-start | bytes 215048 | tf_op jit(solution)/shard_map/ppermute | solution.py:31
  32.1 0.1 collective-permute-start.3
  32.2 4.2 %collective-permute-done.15 = bf16[1,56,640]{2,1,0:T(8,128)(2,1)S(1)} collective-permute-done((bf16[1,56,640]{2,1,0:T(8,128)(2,1)S(1)}, bf16[1,56,640]{2,1,0:T(8,128)(2,1)S(1)}, u32[]{:S(2)}, u32[]{:S(2)}) %collective-permute-start.15) | collective-permute-done | bytes 71712 | tf_op jit(solution)/shard_map/ppermute | solution.py:31
  36.4 0.1 pad_maximum_fusion
  36.5 2.5 %collective-permute-start.16 = (bf16[7,56,640]{2,1,0:T(8,128)(2,1)S(1)}, bf16[7,56,640]{2,1,0:T(8,128)(2,1)S(1)}, u32[]{:S(2)}, u32[]{:S(2)}) collective-permute-start(bf16[7,56,640]{2,1,0:T(8,128)(2,1)S(1)} %pad_maximum_fusion), channel_id=1, source_target_pairs={{0,1},{1,0},{2,3},{3,2},{4,5},{5,4},{6,7},{7,6},{8,9},{9,8},{10,11... | collective-permute-start | bytes 1505288 | tf_op jit(solution)/shard_map/ppermute | solution.py:20
  39.1 1.4 collective-permute-done.16
  40.5 0.1 select_dynamic-update-slice_fusion.1
  40.6 0.1 select_dynamic-update-slice_fusion
  40.8 1.3 collective-permute-start.17
  42.2 0.0 copy-start.1
  42.2 0.1 pad_maximum_fusion.1.refs_0_
  42.3 2.0 %collective-permute-start.4 = (bf16[4,2,56,512]{3,2,1,0:T(8,128)(2,1)S(1)}, bf16[4,2,56,512]{3,2,1,0:T(8,128)(2,1)S(1)}, u32[]{:S(2)}, u32[]{:S(2)}) collective-permute-start(bf16[4,2,56,512]{3,2,1,0:T(8,128)(2,1)S(1)} %pad_maximum_fusion.1.refs_0_), channel_id=1, source_target_pairs={{0,2},{1,15},{2,4},{3,1},{4,6},{5,3},{6,8},{7,5},{8,10},{9,7},{10,... | collective-permute-start | bytes 1376264 | tf_op jit(solution)/shard_map/ppermute | solution.py:31
  44.3 8.4 %collective-permute-done.4.refs_1_ = bf16[4,2,56,512]{3,2,1,0:T(8,128)(2,1)S(1)} collective-permute-done((bf16[4,2,56,512]{3,2,1,0:T(8,128)(2,1)S(1)}, bf16[4,2,56,512]{3,2,1,0:T(8,128)(2,1)S(1)}, u32[]{:S(2)}, u32[]{:S(2)}) %collective-permute-start.4) | collective-permute-done | bytes 458784 | tf_op jit(solution)/shard_map/ppermute | solution.py:31
  52.8 3.1 %collective-permute-start.5 = (bf16[4,2,56,512]{3,2,1,0:T(8,128)(2,1)S(1)}, bf16[4,2,56,512]{3,2,1,0:T(8,128)(2,1)}, u32[]{:S(2)}, u32[]{:S(2)}) collective-permute-start(bf16[4,2,56,512]{3,2,1,0:T(8,128)(2,1)S(1)} %collective-permute-done.4.refs_1_), channel_id=1, source_target_pairs={{0,2},{1,15},{2,4},{3,1},{4,6},{5,3},{6,8},{7,5},{8,10},{9,7},{10,... | collective-permute-start | bytes 1376264 | tf_op jit(solution)/shard_map/ppermute | solution.py:31
  55.8 0.2 collective-permute-done.17.refs_10_
  56.0 0.9 constant_dynamic-slice_fusion.1
  56.9 2.3 %collective-permute-start.18 = (bf16[4,2,56,640]{3,2,1,0:T(8,128)(2,1)}, bf16[4,2,56,640]{3,2,1,0:T(8,128)(2,1)}, u32[]{:S(2)}, u32[]{:S(2)}) collective-permute-start(bf16[4,2,56,640]{3,2,1,0:T(8,128)(2,1)} %constant_dynamic-slice_fusion.1), channel_id=1, source_target_pairs={{0,16},{1,49},{2,18},{3,51},{4,20},{5,53},{6,22},{7,55},{8,24},{9,... | collective-permute-start | bytes 1720328 | tf_op jit(solution)/shard_map/ppermute | solution.py:31
  59.2 0.4 collective-permute-start.19
  59.6 1.6 collective-permute-done.5.refs_2_
  61.3 3.2 %collective-permute-start.6 = (bf16[4,2,56,512]{3,2,1,0:T(8,128)(2,1)}, bf16[4,2,56,512]{3,2,1,0:T(8,128)(2,1)S(1)}, u32[]{:S(2)}, u32[]{:S(2)}) collective-permute-start(bf16[4,2,56,512]{3,2,1,0:T(8,128)(2,1)} %collective-permute-done.5.refs_2_), channel_id=1, source_target_pairs={{0,2},{1,15},{2,4},{3,1},{4,6},{5,3},{6,8},{7,5},{8,10},{9,7},{10,... | collective-permute-start | bytes 1376264 | tf_op jit(solution)/shard_map/ppermute | solution.py:31
  64.5 0.2 collective-permute-start.8
  64.7 0.3 collective-permute-start.9
  65.0 3.0 %collective-permute-done.18.refs_11_ = bf16[4,2,56,640]{3,2,1,0:T(8,128)(2,1)} collective-permute-done((bf16[4,2,56,640]{3,2,1,0:T(8,128)(2,1)}, bf16[4,2,56,640]{3,2,1,0:T(8,128)(2,1)}, u32[]{:S(2)}, u32[]{:S(2)}) %collective-permute-start.18) | collective-permute-done | bytes 573472 | tf_op jit(solution)/shard_map/ppermute | solution.py:31
  68.0 5.6 %collective-permute-start.20 = (bf16[4,2,56,640]{3,2,1,0:T(8,128)(2,1)}, bf16[4,2,56,640]{3,2,1,0:T(8,128)(2,1)}, u32[]{:S(2)}, u32[]{:S(2)}) collective-permute-start(bf16[4,2,56,640]{3,2,1,0:T(8,128)(2,1)} %collective-permute-done.18.refs_11_), channel_id=1, source_target_pairs={{0,1},{1,0},{2,3},{3,2},{4,5},{5,4},{6,7},{7,6},{8,9},{9,8},{10,11... | collective-permute-start | bytes 1720328 | tf_op jit(solution)/shard_map/ppermute | solution.py:20
  73.6 4.6 %collective-permute-done.6.refs_3_ = bf16[4,2,56,512]{3,2,1,0:T(8,128)(2,1)S(1)} collective-permute-done((bf16[4,2,56,512]{3,2,1,0:T(8,128)(2,1)}, bf16[4,2,56,512]{3,2,1,0:T(8,128)(2,1)S(1)}, u32[]{:S(2)}, u32[]{:S(2)}) %collective-permute-start.6) | collective-permute-done | bytes 458784 | tf_op jit(solution)/shard_map/ppermute | solution.py:31
  78.2 3.5 %collective-permute-start.7 = (bf16[2,2,56,512]{3,2,1,0:T(8,128)(2,1)S(1)}, bf16[2,2,56,512]{3,2,1,0:T(8,128)(2,1)S(1)}, u32[]{:S(2)}, u32[]{:S(2)}) collective-permute-start(bf16[2,2,56,512]{3,2,1,0:T(8,128)(2,1)S(1)} %constant_dynamic-slice_fusion.2), channel_id=1, source_target_pairs={{0,2},{1,15},{2,4},{3,1},{4,6},{5,3},{6,8},{7,5},{8,10},{9,7},{10,... | collective-permute-start | bytes 688136 | tf_op jit(solution)/shard_map/ppermute | solution.py:31
  81.8 2.1 %collective-permute-start.10 = (bf16[4,2,56,512]{3,2,1,0:T(8,128)(2,1)S(1)}, bf16[4,2,56,512]{3,2,1,0:T(8,128)(2,1)}, u32[]{:S(2)}, u32[]{:S(2)}) collective-permute-start(bf16[4,2,56,512]{3,2,1,0:T(8,128)(2,1)S(1)} %collective-permute-done.6.refs_3_), channel_id=1, source_target_pairs={{0,1},{1,0},{2,3},{3,2},{4,5},{5,4},{6,7},{7,6},{8,9},{9,8},{10,11... | collective-permute-start | bytes 1376264 | tf_op jit(solution)/shard_map/ppermute | solution.py:20
  83.9 5.6 %collective-permute-done.7.refs_4_ = bf16[2,2,56,512]{3,2,1,0:T(8,128)(2,1)S(1)} collective-permute-done((bf16[2,2,56,512]{3,2,1,0:T(8,128)(2,1)S(1)}, bf16[2,2,56,512]{3,2,1,0:T(8,128)(2,1)S(1)}, u32[]{:S(2)}, u32[]{:S(2)}) %collective-permute-start.7) | collective-permute-done | bytes 229408 | tf_op jit(solution)/shard_map/ppermute | solution.py:31
  89.5 6.4 %collective-permute-start.11 = (bf16[2,2,56,512]{3,2,1,0:T(8,128)(2,1)S(1)}, bf16[2,2,56,512]{3,2,1,0:T(8,128)(2,1)}, u32[]{:S(2)}, u32[]{:S(2)}) collective-permute-start(bf16[2,2,56,512]{3,2,1,0:T(8,128)(2,1)S(1)} %collective-permute-done.7.refs_4_), channel_id=1, source_target_pairs={{0,1},{1,0},{2,3},{3,2},{4,5},{5,4},{6,7},{7,6},{8,9},{9,8},{10,11... | collective-permute-start | bytes 688136 | tf_op jit(solution)/shard_map/ppermute | solution.py:20
  95.9 0.1 copy.14
  96.0 1.1 collective-permute-done.11.refs_8_
  97.2 1.3 copy-done.4
  98.5 1.0 copy-done.6
  99.5 16.9 %spatial.1.attended = bf16[1152,512]{1,0:T(8,128)(2,1)S(1)} custom-call(s32[8]{0:T(128)S(1)} %copy-done.7, s32[32]{0:T(128)S(1)} %copy-done.3, bf16[512,1152]{1,0:T(8,128)(2,1)S(1)} %bitcast.34, f32[6,1,1152]{2,1,0:T(1,128)S(1)} %bitcast.30, f32[72,4]{1,0:T(8,128)S(1)} %bitcast.27, bf16[4,2,56,512]{3,2,1,0:T(8,128)(2,1)S(1)} %pad_maximum_fusion.1.refs_0_, ...), custom_call_target="tpu_custom_call" | custom-call | flops 20000000000 | bytes 20000000 | tf_op jit(solution)/shard_map/spatial/pallas_call | solution.py:316
  116.5 1.0 copy-done.8
  117.5 7.1 %mixing.1 = bf16[32,144,128]{2,1,0:T(8,128)(2,1)} custom-call(bf16[512,1152]{1,0:T(8,128)(2,1)} %bitcast.33, f32[6,1,1152]{2,1,0:T(1,128)} %bitcast.29, bf16[1152,512]{1,0:T(8,128)(2,1)} %copy-done.8, bf16[64,96,1152]{2,1,0:T(8,128)(2,1)} %bitcast.35), custom_call_target="tpu_custom_call" | custom-call | flops 20000000000 | bytes 20000000 | tf_op jit(solution)/shard_map/mixing/pallas_call | solution.py:328
  124.6 5.0 %all-to-all-start = ((bf16[32,144,128]{2,1,0:T(8,128)(2,1)}), bf16[32,144,128]{2,1,0:T(8,128)(2,1)S(1)}, u32[]{:S(2)}, u32[]{:S(2)}) async-start(bf16[32,144,128]{2,1,0:T(8,128)(2,1)} %mixing.1), calls=%async_computation | async-start | bytes 2359296 | tf_op jit(solution)/shard_map/all_to_all | solution.py:342
  129.6 1.1 copy.15
  130.6 0.1 eq.29
  130.7 0.1 select_reduce_fusion
  130.8 0.9 and_convert_fusion.allowed
  131.7 9.5 %prepare.1 = (bf16[3456,1152]{1,0:T(8,128)(2,1)}, bf16[1152,1152]{1,0:T(8,128)(2,1)}) custom-call(bf16[64,96,1152]{2,1,0:T(8,128)(2,1)} %bitcast.36), custom_call_target="tpu_custom_call" | custom-call | bytes 30000000 | tf_op jit(solution)/shard_map/prepare/pallas_call | solution.py:343
  141.2 15.5 %all-to-all-done.received = bf16[32,144,128]{2,1,0:T(8,128)(2,1)S(1)} async-done(((bf16[32,144,128]{2,1,0:T(8,128)(2,1)}), bf16[32,144,128]{2,1,0:T(8,128)(2,1)S(1)}, u32[]{:S(2)}, u32[]{:S(2)}) %all-to-all-start) | async-done | bytes 1179680 | tf_op jit(solution)/shard_map/all_to_all | solution.py:342
  156.7 1.0 copy-done.9
  157.7 21.9 %temporal.1 = f32[16,512]{1,0:T(8,128)} custom-call(bf16[32,144,128]{2,1,0:T(8,128)(2,1)} %copy-done.9, f32[1152,6]{1,0:T(8,128)} %bitcast.37, f32[72,4]{1,0:T(8,128)} %bitcast.28, f32[256,256]{1,0:T(8,128)} %and_convert_fusion.allowed, bf16[16,1152]{1,0:T(8,128)(2,1)} %bitcast.43, bf16[3456,1152]{1,0:T(8,128)(2,1)} %get-tuple-element.7.held_columns, ...), custom_call_target="tpu_custom_call" | custom-call | flops 20000000000 | bytes 20000000 | tf_op jit(solution)/shard_map/temporal/pallas_call | solution.py:356
  179.6 0.7 constant_dynamic-slice_fusion
  180.3 4.9 %collective-permute-start.21 = (f32[8,512]{1,0:T(8,128)S(1)}, f32[8,512]{1,0:T(8,128)S(1)}, u32[]{:S(2)}, u32[]{:S(2)}) collective-permute-start(f32[8,512]{1,0:T(8,128)S(1)} %constant_dynamic-slice_fusion), channel_id=1, source_target_pairs={{0,1},{1,0},{2,3},{3,2},{4,5},{5,4},{6,7},{7,6},{8,9},{9,8},{10,11... | collective-permute-start | bytes 49160 | tf_op jit(solution)/shard_map/ppermute | solution.py:376
  185.3 0.1 broadcast_compare_fusion
  185.3 0.8 collective-permute-done.21
  186.1 0.7 multiply_add_fusion
  186.8 0.1 reshape.70
  186.9 0.7 fusion.6
  (47 shorter events, 0.4 us)
Async XLA Ops:
  6.5 111.0 %all-gather.3.cloned.1.call-start = ((), (), s32[]{:S(2)}) async-start(), calls=%async_computation.1 | async-start | bytes 14376960 | tf_op jit(solution)/shard_map/all_gather | solution.py:306
  9.2 4.3 %collective-permute-start = (bf16[56,1152]{1,0:T(8,128)(2,1)S(1)}, bf16[56,1152]{1,0:T(8,128)(2,1)S(1)}, u32[]{:S(2)}, u32[]{:S(2)}) collective-permute-start(bf16[56,1152]{1,0:T(8,128)(2,1)S(1)} %pad.8), channel_id=1, source_target_pairs={{0,1},{1,0},{2,3},{3,2},{4,5},{5,4},{6,7},{7,6},{8,9},{9,8},{10,11... | collective-permute-start | bytes 387080 | tf_op jit(solution)/shard_map/ppermute | solution.py:20
  14.5 21.9 %collective-permute-start.12 = (bf16[2,56,640]{2,1,0:T(8,128)(2,1)S(1)}, bf16[2,56,640]{2,1,0:T(8,128)(2,1)S(1)}, u32[]{:S(2)}, u32[]{:S(2)}) collective-permute-start(bf16[2,56,640]{2,1,0:T(8,128)(2,1)S(1)} %get-tuple-element.10), channel_id=1, source_target_pairs={{0,2},{1,15},{2,4},{3,1},{4,6},{5,3},{6,8},{7,5},{8,10},{9,7},{10,... | collective-permute-start | bytes 430088 | tf_op jit(solution)/shard_map/ppermute | solution.py:31
  18.4 18.0 %collective-permute-start.13 = (bf16[2,56,640]{2,1,0:T(8,128)(2,1)S(1)}, bf16[2,56,640]{2,1,0:T(8,128)(2,1)S(1)}, u32[]{:S(2)}, u32[]{:S(2)}) collective-permute-start(bf16[2,56,640]{2,1,0:T(8,128)(2,1)S(1)} %get-tuple-element.10), channel_id=1, source_target_pairs={{0,4},{1,13},{2,6},{3,15},{4,8},{5,1},{6,10},{7,3},{8,12},{9,5},{1... | collective-permute-start | bytes 430088 | tf_op jit(solution)/shard_map/ppermute | solution.py:31
  19.6 16.8 %collective-permute-start.14 = (bf16[2,56,640]{2,1,0:T(8,128)(2,1)S(1)}, bf16[2,56,640]{2,1,0:T(8,128)(2,1)S(1)}, u32[]{:S(2)}, u32[]{:S(2)}) collective-permute-start(bf16[2,56,640]{2,1,0:T(8,128)(2,1)S(1)} %get-tuple-element.10), channel_id=1, source_target_pairs={{0,6},{1,11},{2,8},{3,13},{4,10},{5,15},{6,12},{7,1},{8,14},{9,3},... | collective-permute-start | bytes 430088 | tf_op jit(solution)/shard_map/ppermute | solution.py:31
  20.0 12.0 %collective-permute-start.1 = (bf16[2,56,512]{2,1,0:T(8,128)(2,1)S(1)}, bf16[2,56,512]{2,1,0:T(8,128)(2,1)S(1)}, u32[]{:S(2)}, u32[]{:S(2)}) collective-permute-start(bf16[2,56,512]{2,1,0:T(8,128)(2,1)S(1)} %pad_maximum_fusion.4), channel_id=1, source_target_pairs={{0,16},{1,49},{2,18},{3,51},{4,20},{5,53},{6,22},{7,55},{8,24},{9,... | collective-permute-start | bytes 344072 | tf_op jit(solution)/shard_map/ppermute | solution.py:31
  22.7 4.9 %collective-permute-start.2 = (bf16[1,56,512]{2,1,0:T(8,128)(2,1)S(1)}, bf16[1,56,512]{2,1,0:T(8,128)(2,1)S(1)}, u32[]{:S(2)}, u32[]{:S(2)}) collective-permute-start(bf16[1,56,512]{2,1,0:T(8,128)(2,1)S(1)} %fusion.7), channel_id=1, source_target_pairs={{0,32},{1,33},{2,34},{3,35},{4,36},{5,37},{6,38},{7,39},{8,40},{9,... | collective-permute-start | bytes 172040 | tf_op jit(solution)/shard_map/ppermute | solution.py:31
  27.6 8.8 %collective-permute-start.15 = (bf16[1,56,640]{2,1,0:T(8,128)(2,1)S(1)}, bf16[1,56,640]{2,1,0:T(8,128)(2,1)S(1)}, u32[]{:S(2)}, u32[]{:S(2)}) collective-permute-start(bf16[1,56,640]{2,1,0:T(8,128)(2,1)S(1)} %fusion.5), channel_id=1, source_target_pairs={{0,8},{1,9},{2,10},{3,11},{4,12},{5,13},{6,14},{7,15},{8,0},{9,1},... | collective-permute-start | bytes 215048 | tf_op jit(solution)/shard_map/ppermute | solution.py:31
  32.1 7.0 %collective-permute-start.3 = (bf16[3,56,512]{2,1,0:T(8,128)(2,1)S(1)}, bf16[3,56,512]{2,1,0:T(8,128)(2,1)S(1)}, u32[]{:S(2)}, u32[]{:S(2)}) collective-permute-start(bf16[3,56,512]{2,1,0:T(8,128)(2,1)S(1)} %pad_maximum_fusion.2), channel_id=1, source_target_pairs={{0,1},{1,0},{2,3},{3,2},{4,5},{5,4},{6,7},{7,6},{8,9},{9,8},{10,11... | collective-permute-start | bytes 516104 | tf_op jit(solution)/shard_map/ppermute | solution.py:20
  36.5 4.0 %collective-permute-start.16 = (bf16[7,56,640]{2,1,0:T(8,128)(2,1)S(1)}, bf16[7,56,640]{2,1,0:T(8,128)(2,1)S(1)}, u32[]{:S(2)}, u32[]{:S(2)}) collective-permute-start(bf16[7,56,640]{2,1,0:T(8,128)(2,1)S(1)} %pad_maximum_fusion), channel_id=1, source_target_pairs={{0,1},{1,0},{2,3},{3,2},{4,5},{5,4},{6,7},{7,6},{8,9},{9,8},{10,11... | collective-permute-start | bytes 1505288 | tf_op jit(solution)/shard_map/ppermute | solution.py:20
  40.8 15.2 %collective-permute-start.17 = (bf16[8,2,56,640]{3,2,1,0:T(8,128)(2,1)S(1)}, bf16[8,2,56,640]{3,2,1,0:T(8,128)(2,1)S(1)}, u32[]{:S(2)}, u32[]{:S(2)}) collective-permute-start(bf16[8,2,56,640]{3,2,1,0:T(8,128)(2,1)S(1)} %bitcast.31), channel_id=1, source_target_pairs={{0,16},{1,49},{2,18},{3,51},{4,20},{5,53},{6,22},{7,55},{8,24},{9,... | collective-permute-start | bytes 3440648 | tf_op jit(solution)/shard_map/ppermute | solution.py:31
  42.2 53.8 %copy-start.10 = (f32[4,72]{1,0:T(4,128)S(1)}, f32[4,72]{1,0:T(4,128)}, u32[]{:S(2)}) copy-start(f32[4,72]{1,0:T(4,128)} %param.17) | copy-start | bytes 3460
  42.2 55.0 %copy-start.1 = (f32[1,6,1152]{2,0,1:T(1,128)S(1)}, f32[1,6,1152]{2,0,1:T(1,128)}, u32[]{:S(2)}) copy-start(f32[1,6,1152]{2,0,1:T(1,128)} %param.11) | copy-start | bytes 82948
  42.2 55.0 %copy-start.3 = (s32[32]{0:T(128)S(1)}, s32[32]{0:T(128)}, u32[]{:S(2)}) copy-start(s32[32]{0:T(128)} %block_clip.1) | copy-start | bytes 388
  42.2 55.0 %copy-start.7 = (s32[8]{0:T(128)S(1)}, s32[8]{0:T(128)}, u32[]{:S(2)}) copy-start(s32[8]{0:T(128)} %clip_tokens.1) | copy-start | bytes 100
  42.3 10.5 %collective-permute-start.4 = (bf16[4,2,56,512]{3,2,1,0:T(8,128)(2,1)S(1)}, bf16[4,2,56,512]{3,2,1,0:T(8,128)(2,1)S(1)}, u32[]{:S(2)}, u32[]{:S(2)}) collective-permute-start(bf16[4,2,56,512]{3,2,1,0:T(8,128)(2,1)S(1)} %pad_maximum_fusion.1.refs_0_), channel_id=1, source_target_pairs={{0,2},{1,15},{2,4},{3,1},{4,6},{5,3},{6,8},{7,5},{8,10},{9,7},{10,... | collective-permute-start | bytes 1376264 | tf_op jit(solution)/shard_map/ppermute | solution.py:31
  52.8 6.9 %copy-start.5 = (bf16[4,2,56,512]{3,2,1,0:T(8,128)(2,1)}, bf16[4,2,56,512]{3,2,1,0:T(8,128)(2,1)S(1)}, u32[]{:S(2)}) copy-start(bf16[4,2,56,512]{3,2,1,0:T(8,128)(2,1)S(1)} %collective-permute-done.4.refs_1_) | copy-start | bytes 1376260
  52.8 8.5 %collective-permute-start.5 = (bf16[4,2,56,512]{3,2,1,0:T(8,128)(2,1)S(1)}, bf16[4,2,56,512]{3,2,1,0:T(8,128)(2,1)}, u32[]{:S(2)}, u32[]{:S(2)}) collective-permute-start(bf16[4,2,56,512]{3,2,1,0:T(8,128)(2,1)S(1)} %collective-permute-done.4.refs_1_), channel_id=1, source_target_pairs={{0,2},{1,15},{2,4},{3,1},{4,6},{5,3},{6,8},{7,5},{8,10},{9,7},{10,... | collective-permute-start | bytes 1376264 | tf_op jit(solution)/shard_map/ppermute | solution.py:31
  56.9 11.1 %collective-permute-start.18 = (bf16[4,2,56,640]{3,2,1,0:T(8,128)(2,1)}, bf16[4,2,56,640]{3,2,1,0:T(8,128)(2,1)}, u32[]{:S(2)}, u32[]{:S(2)}) collective-permute-start(bf16[4,2,56,640]{3,2,1,0:T(8,128)(2,1)} %constant_dynamic-slice_fusion.1), channel_id=1, source_target_pairs={{0,16},{1,49},{2,18},{3,51},{4,20},{5,53},{6,22},{7,55},{8,24},{9,... | collective-permute-start | bytes 1720328 | tf_op jit(solution)/shard_map/ppermute | solution.py:31
  59.2 38.0 %collective-permute-start.19 = (bf16[8,2,56,640]{3,2,1,0:T(8,128)(2,1)S(1)}, bf16[8,2,56,640]{3,2,1,0:T(8,128)(2,1)}, u32[]{:S(2)}, u32[]{:S(2)}) collective-permute-start(bf16[8,2,56,640]{3,2,1,0:T(8,128)(2,1)S(1)} %collective-permute-done.17.refs_10_), channel_id=1, source_target_pairs={{0,1},{1,0},{2,3},{3,2},{4,5},{5,4},{6,7},{7,6},{8,9},{9,8},{10,11... | collective-permute-start | bytes 3440648 | tf_op jit(solution)/shard_map/ppermute | solution.py:20
  61.3 17.0 %collective-permute-start.6 = (bf16[4,2,56,512]{3,2,1,0:T(8,128)(2,1)}, bf16[4,2,56,512]{3,2,1,0:T(8,128)(2,1)S(1)}, u32[]{:S(2)}, u32[]{:S(2)}) collective-permute-start(bf16[4,2,56,512]{3,2,1,0:T(8,128)(2,1)} %collective-permute-done.5.refs_2_), channel_id=1, source_target_pairs={{0,2},{1,15},{2,4},{3,1},{4,6},{5,3},{6,8},{7,5},{8,10},{9,7},{10,... | collective-permute-start | bytes 1376264 | tf_op jit(solution)/shard_map/ppermute | solution.py:31
  64.5 17.3 %collective-permute-start.8 = (bf16[4,2,56,512]{3,2,1,0:T(8,128)(2,1)}, bf16[4,2,56,512]{3,2,1,0:T(8,128)(2,1)}, u32[]{:S(2)}, u32[]{:S(2)}) collective-permute-start(bf16[4,2,56,512]{3,2,1,0:T(8,128)(2,1)} %copy-done.5), channel_id=1, source_target_pairs={{0,1},{1,0},{2,3},{3,2},{4,5},{5,4},{6,7},{7,6},{8,9},{9,8},{10,11... | collective-permute-start | bytes 1376264 | tf_op jit(solution)/shard_map/ppermute | solution.py:20
  64.7 31.3 %collective-permute-start.9 = (bf16[4,2,56,512]{3,2,1,0:T(8,128)(2,1)}, bf16[4,2,56,512]{3,2,1,0:T(8,128)(2,1)}, u32[]{:S(2)}, u32[]{:S(2)}) collective-permute-start(bf16[4,2,56,512]{3,2,1,0:T(8,128)(2,1)} %collective-permute-done.5.refs_2_), channel_id=1, source_target_pairs={{0,1},{1,0},{2,3},{3,2},{4,5},{5,4},{6,7},{7,6},{8,9},{9,8},{10,11... | collective-permute-start | bytes 1376264 | tf_op jit(solution)/shard_map/ppermute | solution.py:20
  68.0 29.2 %collective-permute-start.20 = (bf16[4,2,56,640]{3,2,1,0:T(8,128)(2,1)}, bf16[4,2,56,640]{3,2,1,0:T(8,128)(2,1)}, u32[]{:S(2)}, u32[]{:S(2)}) collective-permute-start(bf16[4,2,56,640]{3,2,1,0:T(8,128)(2,1)} %collective-permute-done.18.refs_11_), channel_id=1, source_target_pairs={{0,1},{1,0},{2,3},{3,2},{4,5},{5,4},{6,7},{7,6},{8,9},{9,8},{10,11... | collective-permute-start | bytes 1720328 | tf_op jit(solution)/shard_map/ppermute | solution.py:20
  78.2 11.3 %collective-permute-start.7 = (bf16[2,2,56,512]{3,2,1,0:T(8,128)(2,1)S(1)}, bf16[2,2,56,512]{3,2,1,0:T(8,128)(2,1)S(1)}, u32[]{:S(2)}, u32[]{:S(2)}) collective-permute-start(bf16[2,2,56,512]{3,2,1,0:T(8,128)(2,1)S(1)} %constant_dynamic-slice_fusion.2), channel_id=1, source_target_pairs={{0,2},{1,15},{2,4},{3,1},{4,6},{5,3},{6,8},{7,5},{8,10},{9,7},{10,... | collective-permute-start | bytes 688136 | tf_op jit(solution)/shard_map/ppermute | solution.py:31
  81.8 15.4 %collective-permute-start.10 = (bf16[4,2,56,512]{3,2,1,0:T(8,128)(2,1)S(1)}, bf16[4,2,56,512]{3,2,1,0:T(8,128)(2,1)}, u32[]{:S(2)}, u32[]{:S(2)}) collective-permute-start(bf16[4,2,56,512]{3,2,1,0:T(8,128)(2,1)S(1)} %collective-permute-done.6.refs_3_), channel_id=1, source_target_pairs={{0,1},{1,0},{2,3},{3,2},{4,5},{5,4},{6,7},{7,6},{8,9},{9,8},{10,11... | collective-permute-start | bytes 1376264 | tf_op jit(solution)/shard_map/ppermute | solution.py:20
  89.5 7.6 %collective-permute-start.11 = (bf16[2,2,56,512]{3,2,1,0:T(8,128)(2,1)S(1)}, bf16[2,2,56,512]{3,2,1,0:T(8,128)(2,1)}, u32[]{:S(2)}, u32[]{:S(2)}) collective-permute-start(bf16[2,2,56,512]{3,2,1,0:T(8,128)(2,1)S(1)} %collective-permute-done.7.refs_4_), channel_id=1, source_target_pairs={{0,1},{1,0},{2,3},{3,2},{4,5},{5,4},{6,7},{7,6},{8,9},{9,8},{10,11... | collective-permute-start | bytes 688136 | tf_op jit(solution)/shard_map/ppermute | solution.py:20
  96.0 20.4 %copy-start = (f32[4,72]{0,1:T(8,128)}, f32[4,72]{0,1:T(8,128)S(1)}, u32[]{:S(2)}) copy-start(f32[4,72]{0,1:T(8,128)S(1)} %copy.14) | copy-start | bytes 3460
  97.2 1.3 copy-start.4
  98.5 1.0 copy-start.6
  116.5 1.0 copy-start.8
  124.6 5.0 %copy-start.2 = (f32[1,6,1152]{2,0,1:T(1,128)S(1)}, f32[1,6,1152]{2,0,1:T(1,128)}, u32[]{:S(2)}) copy-start(f32[1,6,1152]{2,0,1:T(1,128)} %param.11) | copy-start | bytes 82948
  124.6 32.1 %all-to-all-start = ((bf16[32,144,128]{2,1,0:T(8,128)(2,1)}), bf16[32,144,128]{2,1,0:T(8,128)(2,1)S(1)}, u32[]{:S(2)}, u32[]{:S(2)}) async-start(bf16[32,144,128]{2,1,0:T(8,128)(2,1)} %mixing.1), calls=%async_computation | async-start | bytes 2359296 | tf_op jit(solution)/shard_map/all_to_all | solution.py:342
  156.7 1.0 copy-start.9
  180.3 5.8 %collective-permute-start.21 = (f32[8,512]{1,0:T(8,128)S(1)}, f32[8,512]{1,0:T(8,128)S(1)}, u32[]{:S(2)}, u32[]{:S(2)}) collective-permute-start(f32[8,512]{1,0:T(8,128)S(1)} %constant_dynamic-slice_fusion), channel_id=1, source_target_pairs={{0,1},{1,0},{2,3},{3,2},{4,5},{5,4},{6,7},{7,6},{8,9},{9,8},{10,11... | collective-permute-start | bytes 49160 | tf_op jit(solution)/shard_map/ppermute | solution.py:376
Sparse Core Ops, SparseCore 0:
  10.1 101.7 all-gather.2
